TPU v7x, 256 devices: a whole 4x4x8 slice. The times are simulated.
256 devices in a mesh: row: 16 (over y, x_hi, core), col: 16 (over z, x_lo).
Axes of the slice: x: 4 (x_hi: 2, x_lo: 2; x = x_hi * 2 + x_lo), y: 4, z: 8, core: 2. Of those that a mesh axis runs over, the one named last changes fastest.
Arguments:
- amplitudes: bfloat16 [192, 192, 12288], P('row', None, 'col'), may hold values from -6 to 6
- integral_plus: bfloat16 [12288, 2048], P('col'), may hold values from -0.078125 to 0.078125
- integral_minus: bfloat16 [12288, 2048], P('col'), may hold values from -0.078125 to 0.078125
- cd_irrep: int32 [96], P('col'), may hold values from 0 to 3
- ab_irrep: int32 [16], replicated, may hold values from 0 to 3
Outputs:
- residual: bfloat16 [2048, 36864], P('col', 'row')
All inputs are finite; a program needn't handle non-finite values.
Results may differ from a plain program's by a relative error of at most 0.022.
Values may be sent and summed in bfloat16 or wider, within the bound.
No kernel may reach another device: no remote copies, remote signals or barrier semaphores. Data moves between devices by JAX's collectives and lax.ppermute only.
A program may use at most 128 MiB of HBM per device.

v0:
```python
import jax
import jax.numpy as jnp
from jax import lax
from jax.sharding import PartitionSpec as P


def on_device(amplitudes, integral_plus, integral_minus, cd_irrep, ab_irrep):
    own_rows = amplitudes.shape[0] * amplitudes.shape[1]
    width = amplitudes.shape[2]
    slab = integral_plus.shape[1]
    kt_local = cd_irrep.shape[0]
    tile = width // kt_local
    slab_tiles = slab // tile
    received = lax.all_to_all(amplitudes, "row", split_axis=1, concat_axis=0, tiled=True)
    wide = amplitudes.astype(jnp.float32)
    swapped = jnp.swapaxes(received, 0, 1).astype(jnp.float32)
    amp_plus = (wide + swapped).astype(jnp.bfloat16).reshape(own_rows, width)
    amp_minus = (wide - swapped).astype(jnp.bfloat16).reshape(own_rows, width)
    tile_mask = (cd_irrep[:, None] == ab_irrep[None, :]).astype(jnp.bfloat16)

    def masked(block):
        shaped = block.reshape(kt_local, tile, slab_tiles, tile) * tile_mask[:, None, :, None]
        return shaped.reshape(width, slab)

    plus_kept = masked(integral_plus)
    minus_kept = masked(integral_minus)
    term = lax.dot_general(
        plus_kept, amp_plus, (((0,), (1,)), ((), ())), preferred_element_type=jnp.float32
    )
    term = term + lax.dot_general(
        minus_kept, amp_minus, (((0,), (1,)), ((), ())), preferred_element_type=jnp.float32
    )
    return lax.psum_scatter(
        (0.5 * term).astype(jnp.bfloat16), "col", scatter_dimension=0, tiled=True
    )


def solution(mesh):
    return jax.shard_map(
        on_device,
        mesh=mesh,
        in_specs=(P("row", None, "col"), P("col", None), P("col", None), P("col"), P()),
        out_specs=P("col", "row"),
        check_vma=False,
    )
```

profile of v0, /device:TPU:2, one launch (start us, length us, event | category | flops | bytes accessed | tf_op | source)
XLA Modules:
  0.0 359.7 jit_solution(2218710668557249488)
XLA Ops:
  6.5 6.2 %copy.11 = bf16[12,192,768]{2,0,1:T(8,128)(2,1)} copy(bf16[12,192,768]{2,1,0:T(8,128)(2,1)} %param.5) | data formatting | bytes 7077888 | tf_op args[0]
  12.8 0.0 copy-start.3
  12.8 0.0 copy-start.4
  12.8 6.3 %all-to-all-start = ((bf16[12,192,768]{2,0,1:T(8,128)(2,1)}), bf16[12,192,768]{2,0,1:T(8,128)(2,1)}, u32[]{:S(2)}, u32[]{:S(2)}) async-start(bf16[12,192,768]{2,0,1:T(8,128)(2,1)} %copy.11), calls=%async_computation | async-start | bytes 9437184 | tf_op jit(solution)/shard_map/all_to_all | solution.py:14
  19.1 0.2 reduce-scatter.2.cloned.1.call-start
  19.3 0.0 copy-done.3
  19.3 0.0 copy-done.4
  19.4 0.1 compare_convert_fusion
  19.4 57.2 %all-to-all-done = bf16[12,192,768]{2,0,1:T(8,128)(2,1)} async-done(((bf16[12,192,768]{2,0,1:T(8,128)(2,1)}), bf16[12,192,768]{2,0,1:T(8,128)(2,1)}, u32[]{:S(2)}, u32[]{:S(2)}) %all-to-all-start) | async-done | bytes 3538976 | tf_op jit(solution)/shard_map/all_to_all | solution.py:14
  76.6 6.3 %copy_convert_fusion = f32[12,192,768]{2,1,0:T(8,128)} fusion(bf16[12,192,768]{2,0,1:T(8,128)(2,1)} %all-to-all-done), kind=kLoop, calls=%fused_computation.5 | loop fusion | flops 1769472 | bytes 10616832 | tf_op jit(solution)/shard_map/convert_element_type | solution.py:16
  82.9 8.9 %reshape.46 = f32[12,16,12,768]{3,2,1,0:T(8,128)} reshape(f32[12,192,768]{2,1,0:T(8,128)} %copy_convert_fusion) | data formatting | bytes 14155776 | tf_op jit(solution)/shard_map/convert_element_type | solution.py:16
  91.8 11.6 %copy.13 = f32[16,12,12,768]{3,1,0,2:T(8,128)} copy(f32[16,12,12,768]{3,2,0,1:T(8,128)} %bitcast.17) | data formatting | bytes 14155776 | tf_op jit(solution)/shard_map/convert_element_type | solution.py:16
  103.4 0.0 copy-start
  103.4 9.4 %reshape.45 = f32[192,12,768]{2,0,1:T(8,128)} reshape(f32[16,12,12,768]{3,1,0,2:T(8,128)} %copy.13) | data formatting | bytes 14155776 | tf_op jit(solution)/shard_map/convert_element_type | solution.py:16
  112.7 0.0 copy-done
  112.7 0.0 copy-start.5
  112.7 6.5 %fusion.1 = (bf16[12,192,768]{2,1,0:T(8,128)(2,1)}, bf16[12,192,768]{2,1,0:T(8,128)(2,1)S(1)}) fusion(bf16[12,192,768]{2,1,0:T(8,128)(2,1)S(1)} %copy-done, f32[192,12,768]{2,0,1:T(8,128)} %reshape.45), kind=kLoop, calls=%fused_computation.4 | loop fusion | flops 8847360 | bytes 17694720 | tf_op jit(solution)/shard_map/convert_element_type | solution.py:18
  119.3 0.5 mul.24
  119.7 0.0 copy-start.2
  119.8 0.0 copy-done.5
  119.8 0.0 copy-start.1
  119.8 12.9 %fusion.2 = f32[2048,2304]{1,0:T(8,128)} fusion(bf16[2304,768]{1,0:T(8,128)(2,1)S(1)} %bitcast.19, bf16[768,2048]{1,0:T(8,128)(2,1)S(1)} %copy-done.5, bf16[96,8,16,128]{3,2,1,0:T(8,128)(2,1)S(1)} %bitcast.20), kind=kOutput, calls=%fused_computation.8 | convolution fusion | flops 7249330176 | bytes 28704768 | tf_op jit(solution)/shard_map/dot_general | solution.py:27
  132.7 0.0 copy-done.2
  132.7 0.0 copy-done.1
  132.7 17.4 %multiply_convert_fusion = bf16[2048,2304]{1,0:T(8,128)(2,1)} fusion(f32[2048,2304]{1,0:T(8,128)} %fusion.2, bf16[2304,768]{1,0:T(8,128)(2,1)S(1)} %bitcast.18, bf16[768,2048]{1,0:T(8,128)(2,1)} %param.7, bf16[96,8,16,128]{3,2,1,0:T(8,128)(2,1)} %bitcast.21), kind=kOutput, calls=%fused_computation | convolution fusion | flops 7263485952 | bytes 38141952 | tf_op jit(solution)/shard_map/dot_general | solution.py:30
  150.1 0.0 reduce-scatter.2.cloned.1.call-update
  150.1 202.7 %reduce-scatter.2.cloned.1.call-done = bf16[128,2304]{1,0:T(8,128)(2,1)} async-done(((bf16[2048,2304]{1,0:T(8,128)(2,1)}), bf16[128,2304]{1,0:T(8,128)(2,1)}) %reduce-scatter.2.cloned.1.call-update) | async-done | bytes 589840 | tf_op jit(solution)/shard_map/reduce_scatter | solution.py:33
Async XLA Ops:
  12.8 6.6 %copy-start.3 = (s32[16]{0:T(128)S(1)}, s32[16]{0:T(128)}, u32[]{:S(2)}) copy-start(s32[16]{0:T(128)} %param.9) | copy-start | bytes 196
  12.8 6.6 %copy-start.4 = (s32[6]{0:T(128)S(1)}, s32[6]{0:T(128)}, u32[]{:S(2)}) copy-start(s32[6]{0:T(128)} %param.8) | copy-start | bytes 76
  12.8 63.8 %all-to-all-start = ((bf16[12,192,768]{2,0,1:T(8,128)(2,1)}), bf16[12,192,768]{2,0,1:T(8,128)(2,1)}, u32[]{:S(2)}, u32[]{:S(2)}) async-start(bf16[12,192,768]{2,0,1:T(8,128)(2,1)} %copy.11), calls=%async_computation | async-start | bytes 9437184 | tf_op jit(solution)/shard_map/all_to_all | solution.py:14
  19.1 333.7 %reduce-scatter.2.cloned.1.call-start = ((), (), s32[]{:S(2)}) async-start(), calls=%async_computation.2 | async-start | bytes 10027008 | tf_op jit(solution)/shard_map/reduce_scatter | solution.py:33
  103.4 9.4 %copy-start = (bf16[12,192,768]{2,1,0:T(8,128)(2,1)S(1)}, bf16[12,192,768]{2,1,0:T(8,128)(2,1)}, u32[]{:S(2)}) copy-start(bf16[12,192,768]{2,1,0:T(8,128)(2,1)} %param.5) | copy-start | bytes 10616836
  112.7 7.0 %copy-start.5 = (bf16[768,2048]{1,0:T(8,128)(2,1)S(1)}, bf16[768,2048]{1,0:T(8,128)(2,1)}, u32[]{:S(2)}) copy-start(bf16[768,2048]{1,0:T(8,128)(2,1)} %param.6) | copy-start | bytes 9437188
  119.7 12.9 %copy-start.2 = (bf16[6,128,16,128]{3,2,1,0:T(8,128)(2,1)}, bf16[6,128,16,128]{3,2,1,0:T(8,128)(2,1)S(1)}, u32[]{:S(2)}) copy-start(bf16[6,128,16,128]{3,2,1,0:T(8,128)(2,1)S(1)} %mul.24) | copy-start | bytes 9437188
  119.8 12.9 %copy-start.1 = (bf16[12,192,768]{2,1,0:T(8,128)(2,1)S(1)}, bf16[12,192,768]{2,1,0:T(8,128)(2,1)}, u32[]{:S(2)}) copy-start(bf16[12,192,768]{2,1,0:T(8,128)(2,1)} %get-tuple-element.5) | copy-start | bytes 10616836
Sparse Core Ops, SparseCore 0:
  150.2 202.5 reduce-scatter.1
where the time goes:
time: 362 us; the launch traced here: 360 us
  waiting for transfers between devices  260 us (72%)
  local copies, waits for them, and re-layouts  36.6 us (10%)
  matrix products  30.3 us (8%)
  between operations  13.5 us (4%)
  other arithmetic  12.9 us (4%)
  starting transfers between devices  6.53 us (2%)
    reduce_scatter x1, waiting for transfers between devices, on_device(): lax.psum_scatter((0.5 * term).astype(jnp.bfloat16), 'col', scatter_dimens...  203 us
    all_to_all x1, waiting for transfers between devices, on_device(): lax.all_to_all(amplitudes, 'row', split_axis=1, concat_axis=0, tiled=True)  57.2 us
    convert_element_type x3, local copies, waits for them, and re-layouts, on_device(): swapped = jnp.swapaxes(received, 0, 1).astype(jnp.float32)  29.8 us
    dot_general x1, matrix products, on_device(): lax.dot_general(minus_kept, amp_minus, (((0,), (1,)), ((), ())), preferre...  17.4 us
    dot_general x1, matrix products, on_device(): lax.dot_general(plus_kept, amp_plus, (((0,), (1,)), ((), ())), preferred_...  12.9 us
  transfers between devices with their start and end apart: 2, of which 2 were waited for; matrix products, arithmetic and copies ran while one was open for 0% of the time, Pallas kernels for 0%

commit v1 on v0

v1 whole, which is shorter than its diff:
```python
import functools

import jax
import jax.numpy as jnp
import numpy as np
from jax import lax
from jax.experimental import pallas as pl
from jax.experimental.pallas import tpu as pltpu
from jax.sharding import Mesh
from jax.sharding import PartitionSpec as P

TILE = 128
GROUP = 4
N_X = 2
VMEM = 48 * 2**20


def params():
    return pltpu.CompilerParams(vmem_limit_bytes=VMEM)


def send_order(rows):
    out = []
    for chunk in range(rows // GROUP):
        for r in range(GROUP):
            for jl in range(GROUP):
                for i in range(rows):
                    out.append((i * GROUP + r) * rows + chunk * GROUP + jl)
    return np.eye(GROUP * rows * rows, dtype=np.float32)[np.array(out)]


def receive_order(rows):
    out = [
        (s * GROUP + i) * rows + jl
        for i in range(GROUP)
        for s in range(GROUP)
        for jl in range(rows)
    ]
    return np.eye(GROUP * GROUP * rows, dtype=np.float32)[np.array(out)]


def pack_kernel(order_ref, amp_ref, *out_refs):
    rows, wide, width = amp_ref.shape
    block = amp_ref[...].reshape(rows * wide, width)
    per = out_refs[0].shape[0]
    for c, out_ref in enumerate(out_refs):
        out_ref[...] = jnp.dot(
            order_ref[c * per : (c + 1) * per, :], block, preferred_element_type=jnp.float32
        ).astype(out_ref.dtype)


def pack(amplitudes, order, count):
    rows, occ, width = amplitudes.shape
    steps = occ // (GROUP * rows)
    per = GROUP * GROUP * rows
    return pl.pallas_call(
        pack_kernel,
        grid=(steps,),
        in_specs=[
            pl.BlockSpec((count * per, order.shape[1]), lambda q: (0, 0)),
            pl.BlockSpec((rows, GROUP * rows, width), lambda q: (0, q, 0)),
        ],
        out_specs=[pl.BlockSpec((per, width), lambda q: (q, 0))] * count,
        out_shape=[jax.ShapeDtypeStruct((steps * per, width), jnp.bfloat16)] * count,
        compiler_params=params(),
        cost_estimate=pl.CostEstimate(
            flops=2 * count * steps * per * order.shape[1] * width,
            bytes_accessed=2 * (rows * occ * width + count * steps * per * width),
            transcendentals=0,
        ),
    )(order, amplitudes)


def mask_kernel(cd_ref, ab_ref, me_ref, plus_ref, minus_ref, out_ref):
    z = pl.program_id(0)
    me = me_ref[0]
    kt = cd_ref.shape[0]
    for half, ref in enumerate((plus_ref, minus_ref)):
        for w in range(N_X):
            lanes = pl.ds(pl.multiple_of((w ^ me) * TILE, TILE), TILE)
            for p in range(kt):
                rows = pl.ds((half * kt + p) * TILE, TILE)
                kept = cd_ref[p] == ab_ref[z * N_X + w]

                @pl.when(kept)
                def _():
                    out_ref[rows, lanes] = ref[p * TILE : (p + 1) * TILE, w * TILE : (w + 1) * TILE]

                @pl.when(jnp.logical_not(kept))
                def _():
                    out_ref[rows, lanes] = jnp.zeros((TILE, TILE), out_ref.dtype)


def mask(cd_irrep, ab_irrep, me, plus, minus):
    width, slab = plus.shape
    pair = N_X * TILE
    smem = pl.BlockSpec(memory_space=pltpu.SMEM)
    return pl.pallas_call(
        mask_kernel,
        grid=(slab // pair,),
        in_specs=[
            smem,
            smem,
            smem,
            pl.BlockSpec((width, pair), lambda z: (0, z)),
            pl.BlockSpec((width, pair), lambda z: (0, z)),
        ],
        out_specs=pl.BlockSpec((2 * width, pair), lambda z: (0, z)),
        out_shape=jax.ShapeDtypeStruct((2 * width, slab), jnp.bfloat16),
        compiler_params=params(),
        cost_estimate=pl.CostEstimate(
            flops=0, bytes_accessed=8 * width * slab, transcendentals=0
        ),
    )(cd_irrep, ab_irrep, me, plus, minus)


def ladder_kernel(order_ref, own_ref, received_ref, weight_ref, *refs):
    out_refs, both = refs[:-1], refs[-1]
    group, occ, width = own_ref.shape
    span = order_ref.shape[0]
    piece = span // group

    @pl.when(pl.program_id(0) == 0)
    def _():
        for q in range(occ // piece):
            other = jnp.dot(
                order_ref[...],
                received_ref[q * span : (q + 1) * span, :],
                preferred_element_type=jnp.float32,
            )
            for i in range(group):
                cols = slice(q * piece, (q + 1) * piece)
                own = own_ref[i, cols, :].astype(jnp.float32)
                swap = other[i * piece : (i + 1) * piece]
                rows = slice(i * occ + q * piece, i * occ + (q + 1) * piece)
                both[rows, :width] = (own + swap).astype(jnp.bfloat16)
                both[rows, width:] = (own - swap).astype(jnp.bfloat16)

    for i in range(group):
        rows = slice(i * occ, (i + 1) * occ)
        term = 0.5 * jnp.dot(both[rows, :], weight_ref[...], preferred_element_type=jnp.float32)
        for w in range(N_X):
            half = term[:, w * TILE : (w + 1) * TILE].astype(jnp.bfloat16)
            if len(out_refs) == 1:
                out_refs[0][0, w, rows, :] = half
            else:
                out_refs[w][0, rows, :] = half


def ladder(order, amplitudes, received, weights, chunk, apart):
    _, occ, width = amplitudes.shape
    rows = GROUP * occ
    pair = N_X * TILE
    steps = weights.shape[1] // pair
    if apart:
        out = [jax.ShapeDtypeStruct((steps, rows, TILE), jnp.bfloat16)] * N_X
        out_specs = [pl.BlockSpec((1, rows, TILE), lambda z: (z, 0, 0))] * N_X
    else:
        out = jax.ShapeDtypeStruct((steps, N_X, rows, TILE), jnp.bfloat16)
        out_specs = pl.BlockSpec((1, N_X, rows, TILE), lambda z: (z, 0, 0, 0))
    return pl.pallas_call(
        ladder_kernel,
        grid=(steps,),
        in_specs=[
            pl.BlockSpec(order.shape, lambda z: (0, 0)),
            pl.BlockSpec((GROUP, occ, width), lambda z: (chunk, 0, 0)),
            pl.BlockSpec((rows, width), lambda z: (0, 0)),
            pl.BlockSpec((2 * width, pair), lambda z: (0, z)),
        ],
        out_specs=out_specs,
        out_shape=out,
        scratch_shapes=[pltpu.VMEM((rows, 2 * width), jnp.bfloat16)],
        compiler_params=params(),
        cost_estimate=pl.CostEstimate(
            flops=4 * rows * width * steps * pair,
            bytes_accessed=4 * rows * width + 4 * width * steps * pair + 2 * rows * steps * pair,
            transcendentals=0,
        ),
    )(order, amplitudes, received, weights)


def finish_kernel(a0, a1, b0, c0, c1, out_ref):
    rows = b0.shape[0]
    first = a0[...].astype(jnp.float32) + a1[...].astype(jnp.float32)
    last = c0[...].astype(jnp.float32) + c1[...].astype(jnp.float32)
    for k, part in enumerate((first, b0[...].astype(jnp.float32), last)):
        out_ref[:, k * rows : (k + 1) * rows] = part.T.astype(out_ref.dtype)


def on_device(order_out, order_in, amplitudes, integral_plus, integral_minus, cd_irrep, ab_irrep):
    me = lax.axis_index("xl").reshape(1).astype(jnp.int32)
    swap = functools.partial(lax.ppermute, axis_name="xl", perm=[(0, 1), (1, 0)])
    per = order_in.shape[0]

    def exchange(packed):
        return lax.all_to_all(packed, "row", split_axis=0, concat_axis=0, tiled=True)

    def scatter(part):
        return lax.psum_scatter(part, "z", scatter_dimension=0, tiled=True)

    (packed0,) = pack(amplitudes, order_out[:per], 1)
    received0 = exchange(packed0)
    packed1, packed2 = pack(amplitudes, order_out[per:], 2)
    weights = mask(cd_irrep, ab_irrep, me, integral_plus, integral_minus)
    received0, packed1, packed2, weights = lax.optimization_barrier(
        (received0, packed1, packed2, weights)
    )
    received1 = exchange(packed1)
    sum0 = scatter(ladder(order_in, amplitudes, received0, weights, 0, False))
    received1, packed2 = lax.optimization_barrier((received1, packed2))
    received2 = exchange(packed2)
    near1, far1 = ladder(order_in, amplitudes, received1, weights, 1, True)
    other1 = swap(far1)
    sum2 = scatter(ladder(order_in, amplitudes, received2, weights, 2, False))
    sum1 = scatter(
        (near1.astype(jnp.float32) + other1.astype(jnp.float32)).astype(jnp.bfloat16)
    )
    last0 = swap(sum0[0, 1])
    last2 = swap(sum2[0, 1])
    rows = sum1.shape[1]
    return pl.pallas_call(
        finish_kernel,
        out_shape=jax.ShapeDtypeStruct((TILE, 3 * rows), jnp.bfloat16),
        compiler_params=params(),
    )(sum0[0, 0], last0, sum1[0], sum2[0, 0], last2)


def solution(mesh):
    rows, cols = mesh.shape["row"], mesh.shape["col"]
    fine = Mesh(mesh.devices.reshape(rows, cols // N_X, N_X), ("row", "z", "xl"))

    def program(amplitudes, integral_plus, integral_minus, cd_irrep, ab_irrep):
        own = amplitudes.shape[0] // rows
        order_out = jnp.asarray(send_order(own), jnp.bfloat16)
        order_in = jnp.asarray(receive_order(own), jnp.bfloat16)
        col = ("z", "xl")
        return jax.shard_map(
            on_device,
            mesh=fine,
            in_specs=(P(), P(), P("row", None, col), P(col, None), P(col, None), P(col), P()),
            out_specs=P(col, "row"),
            check_vma=False,
        )(order_out, order_in, amplitudes, integral_plus, integral_minus, cd_irrep, ab_irrep)

    return program
```

time: 362 us -> 203 us (0.56)
  waiting for transfers between devices: 260 us -> 78.4 us
  Pallas kernels: 0 us -> 48.1 us
  blocking collectives: 0 us -> 44.3 us
  local copies, waits for them, and re-layouts: 36.6 us -> 6 us
  matrix products: 30.3 us -> 0 us
  other arithmetic: 12.9 us -> 1.58 us
  starting transfers between devices: 6.53 us -> 10.2 us
    reduce_scatter x1 -> x3, waiting for transfers between devices: 203 us -> 36.9 us  [scatter(): return lax.psum_scatter(part, 'z', scatter_dimension=0, tiled=True)]
    all_to_all x1, waiting for transfers between devices: 57.2 us -> 6.72 us  [exchange(): lax.all_to_all(packed, 'row', split_axis=0, concat_axis=0, tiled=True)]
    pallas_call x0 -> x7, Pallas kernels: none -> 48.1 us  [the longest x3 31.5 us: ladder(): pl.pallas_call(ladder_kernel, grid=(steps,), in_specs=[pl.BlockSpec(order...]
    all_to_all x0 -> x2, blocking collectives: none -> 44.3 us  [exchange(): lax.all_to_all(packed, 'row', split_axis=0, concat_axis=0, tiled=True)]
    ppermute x0 -> x3, waiting for transfers between devices: none -> 34.7 us  [the longest x1 34.6 us: on_device(): other1 = swap(far1)]
    dot_general x2 -> x0, matrix products: 30.3 us -> none  [the longest x1 17.4 us: on_device(): lax.dot_general(minus_kept, amp_minus, (((0,), (1,)), ((), ())), preferre...]
    convert_element_type x3 -> x0, local copies, waits for them, and re-layouts: 29.8 us -> none  [on_device(): swapped = jnp.swapaxes(received, 0, 1).astype(jnp.float32)]
    convert_element_type x3 -> x1, other arithmetic: 12.9 us -> 1.58 us  [on_device(): (near1.astype(jnp.float32) + other1.astype(jnp.float32)).astype(jnp.bfloa...]
  transfers between devices with their start and end apart: 2 -> 7, of which waited for: 2 -> 3; matrix products, arithmetic and copies ran while one was open for 0% -> 2% of each run, Pallas kernels for 0% -> 16%
where the time goes in v1:
time: 203 us; the launch traced here: 202 us
  waiting for transfers between devices  78.4 us (39%)
  Pallas kernels  48.1 us (24%)
  blocking collectives  44.3 us (22%)
  between operations  13.2 us (7%)
  starting transfers between devices  10.2 us (5%)
  local copies, waits for them, and re-layouts  6 us (3%)
    all_to_all x2, blocking collectives, exchange(): lax.all_to_all(packed, 'row', split_axis=0, concat_axis=0, tiled=True)  44.3 us
    reduce_scatter x3, waiting for transfers between devices, scatter(): return lax.psum_scatter(part, 'z', scatter_dimension=0, tiled=True)  36.9 us
    ppermute x1, waiting for transfers between devices, on_device(): other1 = swap(far1)  34.6 us
    pallas_call x3, Pallas kernels, ladder(): pl.pallas_call(ladder_kernel, grid=(steps,), in_specs=[pl.BlockSpec(order...  31.5 us
    pallas_call x1, Pallas kernels, mask(): pl.pallas_call(mask_kernel, grid=(slab // pair,), in_specs=[smem, smem, s...  8.32 us
    pallas_call x2, Pallas kernels, pack(): pl.pallas_call(pack_kernel, grid=(steps,), in_specs=[pl.BlockSpec((count...  7.24 us
    all_to_all x1, waiting for transfers between devices, exchange(): lax.all_to_all(packed, 'row', split_axis=0, concat_axis=0, tiled=True)  6.72 us
    all_to_all x1, starting transfers between devices, exchange(): lax.all_to_all(packed, 'row', split_axis=0, concat_axis=0, tiled=True)  6.32 us
  transfers between devices with their start and end apart: 7, of which 3 were waited for; matrix products, arithmetic and copies ran while one was open for 2% of the time, Pallas kernels for 16%

profile of v1, /device:TPU:2, one launch (start us, length us, event | category | flops | bytes accessed | tf_op | source)
XLA Modules:
  0.0 201.7 jit_solution(15531774090277801575)
XLA Ops:
  6.5 2.0 copy-done
  8.5 0.9 copy-done.2
  9.5 2.9 %shard_map.73 = bf16[768,768]{1,0:T(8,128)(2,1)} custom-call(bf16[192,576]{1,0:T(8,128)(2,1)S(1)} %copy-done.2, bf16[12,192,768]{2,1,0:T(8,128)(2,1)S(1)} %copy-done), custom_call_target="tpu_custom_call" | custom-call | flops 679477248 | bytes 4718592 | tf_op jit(solution)/shard_map/pallas_call | solution.py:56
  12.3 6.3 %all-to-all-start = ((bf16[16,48,768]{2,1,0:T(8,128)(2,1)}), bf16[16,48,768]{2,1,0:T(8,128)(2,1)}, u32[]{:S(2)}, u32[]{:S(2)}) async-start(bf16[16,48,768]{2,1,0:T(8,128)(2,1)} %bitcast), calls=%async_computation | async-start | bytes 2359296 | tf_op jit(solution)/shard_map/all_to_all | solution.py:196
  18.7 0.0 reduce-scatter.4.cloned.1.call-start
  18.8 0.0 copy-start.6
  18.8 8.3 %shard_map.75.weight_ref = bf16[1536,2048]{1,0:T(8,128)(2,1)} custom-call(s32[6]{0:T(128)S(1)} %copy-done.4, s32[16]{0:T(128)S(1)} %copy-done.5, s32[1]{0:T(128)} %bitcast.2.me_ref, bf16[768,2048]{1,0:T(8,128)(2,1)S(1)} %copy-done.1, bf16[768,2048]{1,0:T(8,128)(2,1)} %minus_ref.1), custom_call_target="tpu_custom_call" | custom-call | bytes 12582912 | tf_op jit(solution)/shard_map/pallas_call | solution.py:98
  27.1 4.4 %shard_map.74 = (bf16[768,768]{1,0:T(8,128)(2,1)S(1)}, bf16[768,768]{1,0:T(8,128)(2,1)S(1)}) custom-call(bf16[384,576]{1,0:T(8,128)(2,1)S(1)} %copy-done.6, bf16[12,192,768]{2,1,0:T(8,128)(2,1)} %own_ref.5), custom_call_target="tpu_custom_call" | custom-call | flops 1358954496 | bytes 5898240 | tf_op jit(solution)/shard_map/pallas_call | solution.py:56
  31.5 6.7 %all-to-all-done = bf16[16,48,768]{2,1,0:T(8,128)(2,1)} async-done(((bf16[16,48,768]{2,1,0:T(8,128)(2,1)}), bf16[16,48,768]{2,1,0:T(8,128)(2,1)}, u32[]{:S(2)}, u32[]{:S(2)}) %all-to-all-start) | async-done | bytes 1179680 | tf_op jit(solution)/shard_map/all_to_all | solution.py:196
  38.2 11.1 %shard_map.76 = bf16[8,2,768,128]{3,2,1,0:T(8,128)(2,1)} custom-call(bf16[192,192]{1,0:T(8,128)(2,1)S(1)} %copy-done.7, bf16[12,192,768]{2,1,0:T(8,128)(2,1)} %own_ref.5, bf16[768,768]{1,0:T(8,128)(2,1)} %bitcast.1.received_ref, bf16[1536,2048]{1,0:T(8,128)(2,1)} %shard_map.75.weight_ref), custom_call_target="tpu_custom_call" | custom-call | flops 4831838208 | bytes 11796480 | tf_op jit(solution)/shard_map/pallas_call | solution.py:161
  49.3 0.0 reduce-scatter.4.cloned.1.call-update
  49.4 0.0 reduce-scatter.8.cloned.1.call-start
  49.4 22.1 %all_to_all.35 = bf16[16,48,768]{2,1,0:T(8,128)(2,1)S(1)} all-to-all(bf16[16,48,768]{2,1,0:T(8,128)(2,1)S(1)} %bitcast.17), channel_id=1, replica_groups=mesh['row'=16,'z'=8,'xl'=2] {'row'}, dimensions={0} | all-to-all | bytes 2359296 | tf_op jit(solution)/shard_map/all_to_all | solution.py:196
  71.5 22.2 %all_to_all.36 = bf16[16,48,768]{2,1,0:T(8,128)(2,1)S(1)} all-to-all(bf16[16,48,768]{2,1,0:T(8,128)(2,1)S(1)} %bitcast.16), channel_id=1, replica_groups=mesh['row'=16,'z'=8,'xl'=2] {'row'}, dimensions={0} | all-to-all | bytes 2359296 | tf_op jit(solution)/shard_map/all_to_all | solution.py:196
  93.7 10.8 %shard_map.78 = bf16[8,2,768,128]{3,2,1,0:T(8,128)(2,1)} custom-call(bf16[192,192]{1,0:T(8,128)(2,1)S(1)} %copy-done.8, bf16[12,192,768]{2,1,0:T(8,128)(2,1)} %own_ref.5, bf16[768,768]{1,0:T(8,128)(2,1)S(1)} %bitcast.19, bf16[1536,2048]{1,0:T(8,128)(2,1)} %shard_map.75.weight_ref), custom_call_target="tpu_custom_call" | custom-call | flops 4831838208 | bytes 11796480 | tf_op jit(solution)/shard_map/pallas_call | solution.py:161
  104.4 0.0 reduce-scatter.8.cloned.1.call-update
  104.5 0.0 reduce-scatter.6.cloned.1.call-start
  104.5 9.6 %shard_map.77 = (bf16[8,768,128]{2,1,0:T(8,128)(2,1)S(1)}, bf16[8,768,128]{2,1,0:T(8,128)(2,1)S(1)}) custom-call(bf16[192,192]{1,0:T(8,128)(2,1)S(1)} %copy-done.8, bf16[12,192,768]{2,1,0:T(8,128)(2,1)} %own_ref.5, bf16[768,768]{1,0:T(8,128)(2,1)S(1)} %bitcast.18, bf16[1536,2048]{1,0:T(8,128)(2,1)} %shard_map.75.weight_ref), custom_call_target="tpu_custom_call" | custom-call | flops 4831838208 | bytes 11796480 | tf_op jit(solution)/shard_map/pallas_call | solution.py:161
  114.1 1.5 collective-permute-start.1
  115.6 34.6 %collective-permute-done.1 = bf16[8,768,128]{2,1,0:T(8,128)(2,1)S(1)} collective-permute-done((bf16[8,768,128]{2,1,0:T(8,128)(2,1)S(1)}, bf16[8,768,128]{2,1,0:T(8,128)(2,1)S(1)}, u32[]{:S(2)}, u32[]{:S(2)}) %collective-permute-start.1) | collective-permute-done | bytes 1572896 | tf_op jit(solution)/shard_map/ppermute | solution.py:213
  150.3 1.6 add_convert_fusion
  151.9 0.0 reduce-scatter.6.cloned.1.call-update
  151.9 0.0 reduce-scatter.4.cloned.1.call-done
  151.9 1.1 slice_bitcast_fusion.2
  153.0 1.5 collective-permute-start
  154.5 1.0 slice_bitcast_fusion
  155.5 0.7 collective-permute-start.2
  156.2 36.9 %reduce-scatter.6.cloned.1.call-done = bf16[1,768,128]{2,1,0:T(8,128)(2,1)} async-done(((bf16[8,768,128]{2,1,0:T(8,128)(2,1)}), bf16[1,768,128]{2,1,0:T(8,128)(2,1)}) %reduce-scatter.6.cloned.1.call-update) | async-done | bytes 196624 | tf_op jit(solution)/shard_map/reduce_scatter | solution.py:199
  193.1 0.0 collective-permute-done.a1
  193.1 0.0 collective-permute-done.2.c1
  193.1 0.9 copy-done.3
  194.1 1.1 shard_map.79
  (15 shorter events, 0.0 us)
Async XLA Ops:
  6.5 2.0 copy-start
  8.5 0.9 copy-start.2
  9.5 9.2 %copy-start.1 = (bf16[768,2048]{1,0:T(8,128)(2,1)S(1)}, bf16[768,2048]{1,0:T(8,128)(2,1)}, u32[]{:S(2)}) copy-start(bf16[768,2048]{1,0:T(8,128)(2,1)} %plus_ref.1) | copy-start | bytes 9437188
  12.3 6.4 %copy-start.4 = (s32[6]{0:T(128)S(1)}, s32[6]{0:T(128)}, u32[]{:S(2)}) copy-start(s32[6]{0:T(128)} %cd_ref.1) | copy-start | bytes 76
  12.3 6.4 %copy-start.5 = (s32[16]{0:T(128)S(1)}, s32[16]{0:T(128)}, u32[]{:S(2)}) copy-start(s32[16]{0:T(128)} %ab_ref.1) | copy-start | bytes 196
  12.3 25.9 %all-to-all-start = ((bf16[16,48,768]{2,1,0:T(8,128)(2,1)}), bf16[16,48,768]{2,1,0:T(8,128)(2,1)}, u32[]{:S(2)}, u32[]{:S(2)}) async-start(bf16[16,48,768]{2,1,0:T(8,128)(2,1)} %bitcast), calls=%async_computation | async-start | bytes 2359296 | tf_op jit(solution)/shard_map/all_to_all | solution.py:196
  18.7 133.2 %reduce-scatter.4.cloned.1.call-start = ((), (), s32[]{:S(2)}) async-start(), calls=%async_computation.6 | async-start | bytes 3538944 | tf_op jit(solution)/shard_map/reduce_scatter | solution.py:199
  18.8 8.3 %copy-start.6 = (bf16[384,576]{1,0:T(8,128)(2,1)S(1)}, bf16[384,576]{1,0:T(8,128)(2,1)}, u32[]{:S(2)}) copy-start(bf16[384,576]{1,0:T(8,128)(2,1)} %constant.13.order_ref) | copy-start | bytes 1327108
  27.1 11.1 %copy-start.7 = (bf16[192,192]{1,0:T(8,128)(2,1)S(1)}, bf16[192,192]{1,0:T(8,128)(2,1)}, u32[]{:S(2)}) copy-start(bf16[192,192]{1,0:T(8,128)(2,1)} %constant.9.clone.order_ref) | copy-start | bytes 221188
  49.4 105.1 %reduce-scatter.8.cloned.1.call-start = ((), (), s32[]{:S(2)}) async-start(), calls=%async_computation.8 | async-start | bytes 3538944 | tf_op jit(solution)/shard_map/reduce_scatter | solution.py:199
  71.5 22.2 %copy-start.8 = (bf16[192,192]{1,0:T(8,128)(2,1)S(1)}, bf16[192,192]{1,0:T(8,128)(2,1)}, u32[]{:S(2)}) copy-start(bf16[192,192]{1,0:T(8,128)(2,1)} %constant.9.clone.order_ref) | copy-start | bytes 221188
  104.5 88.7 %reduce-scatter.6.cloned.1.call-start = ((), (), s32[]{:S(2)}) async-start(), calls=%async_computation.7 | async-start | bytes 1769472 | tf_op jit(solution)/shard_map/reduce_scatter | solution.py:199
  114.1 36.2 %collective-permute-start.1 = (bf16[8,768,128]{2,1,0:T(8,128)(2,1)S(1)}, bf16[8,768,128]{2,1,0:T(8,128)(2,1)S(1)}, u32[]{:S(2)}, u32[]{:S(2)}) collective-permute-start(bf16[8,768,128]{2,1,0:T(8,128)(2,1)S(1)} %get-tuple-element.23), channel_id=1, source_target_pairs={{0,1},{1,0},{2,3},{3,2},{4,5},{5,4},{6,7},{7,6},{8,9},{9,8},{10,11... | collective-permute-start | bytes 4718600 | tf_op jit(solution)/shard_map/ppermute | solution.py:213
  153.0 40.2 %collective-permute-start = (bf16[768,128]{1,0:T(8,128)(2,1)S(1)}, bf16[768,128]{1,0:T(8,128)(2,1)S(1)}, u32[]{:S(2)}, u32[]{:S(2)}) collective-permute-start(bf16[768,128]{1,0:T(8,128)(2,1)S(1)} %get-tuple-element.27), channel_id=1, source_target_pairs={{0,1},{1,0},{2,3},{3,2},{4,5},{5,4},{6,7},{7,6},{8,9},{9,8},{10,11... | collective-permute-start | bytes 589832 | tf_op jit(solution)/shard_map/ppermute | solution.py:218
  155.5 37.6 %collective-permute-start.2 = (bf16[768,128]{1,0:T(8,128)(2,1)S(1)}, bf16[768,128]{1,0:T(8,128)(2,1)S(1)}, u32[]{:S(2)}, u32[]{:S(2)}) collective-permute-start(bf16[768,128]{1,0:T(8,128)(2,1)S(1)} %get-tuple-element.25), channel_id=1, source_target_pairs={{0,1},{1,0},{2,3},{3,2},{4,5},{5,4},{6,7},{7,6},{8,9},{9,8},{10,11... | collective-permute-start | bytes 589832 | tf_op jit(solution)/shard_map/ppermute | solution.py:219
  193.1 0.9 copy-start.3
Sparse Core Ops, SparseCore 0:
  49.5 45.7 reduce-scatter.3
  104.6 46.2 reduce-scatter.7
  153.5 39.6 reduce-scatter.5

commit v2 on v1

v2 whole, which is shorter than its diff:
```python
import functools

import jax
import jax.numpy as jnp
import numpy as np
from jax import lax
from jax.experimental import pallas as pl
from jax.experimental.pallas import tpu as pltpu
from jax.sharding import Mesh
from jax.sharding import PartitionSpec as P

TILE = 128
GROUP = 4
N_X = 2
PAIR = N_X * TILE
FIRST = 5


def params(mib=16):
    return pltpu.CompilerParams(vmem_limit_bytes=mib * 2**20)


def send_order(rows):
    return [
        (i * GROUP + r) * rows + chunk * GROUP + jl
        for chunk in range(rows // GROUP)
        for r in range(GROUP)
        for jl in range(GROUP)
        for i in range(rows)
    ]


def receive_order(rows):
    return [
        (s * GROUP + i) * rows + jl
        for i in range(GROUP)
        for s in range(GROUP)
        for jl in range(rows)
    ]


def column(places):
    return jnp.asarray(np.array(places, np.int32)[:, None])


def picker(places, width):
    lanes = lax.broadcasted_iota(jnp.int32, (places.shape[0], width), 1)
    return jnp.where(lanes == places, 1.0, 0.0).astype(jnp.bfloat16)


def pack_kernel(order_ref, *refs):
    count = 4
    amp_refs, out_refs = refs[:count], refs[count:]
    block = jnp.concatenate(
        [r[...].reshape(r.shape[0] * r.shape[1], r.shape[2]) for r in amp_refs], 0
    )
    per = out_refs[0].shape[0]
    for c, out_ref in enumerate(out_refs):
        order = picker(order_ref[c * per : (c + 1) * per, :], block.shape[0])
        out_ref[...] = jnp.dot(order, block, preferred_element_type=jnp.float32).astype(
            out_ref.dtype
        )


def pack(amplitudes, order, mib):
    rows, occ, width = amplitudes.shape
    steps = occ // (GROUP * rows)
    per = GROUP * GROUP * rows
    count = order.shape[0] // per
    return pl.pallas_call(
        pack_kernel,
        grid=(steps,),
        in_specs=[pl.BlockSpec(order.shape, lambda q: (0, 0))]
        + [
            pl.BlockSpec((rows // 4, GROUP * rows, width), lambda q, k=k: (k, q, 0))
            for k in range(4)
        ],
        out_specs=[pl.BlockSpec((per, width), lambda q: (q, 0))] * count,
        out_shape=[jax.ShapeDtypeStruct((steps * per, width), jnp.bfloat16)] * count,
        compiler_params=params(mib),
        cost_estimate=pl.CostEstimate(
            flops=2 * count * steps * per * GROUP * rows * rows * width,
            bytes_accessed=2 * (rows * occ * width + count * steps * per * width),
            transcendentals=0,
        ),
    )(order, *[amplitudes] * 4)


def mask_kernel(cd_ref, ab_ref, me_ref, plus_ref, minus_ref, out_ref):
    p = pl.program_id(0)
    me = me_ref[0]
    for q in range(out_ref.shape[0] * N_X):
        z, w = q // N_X, q % N_X
        lanes = pl.ds(pl.multiple_of((w ^ me) * TILE, TILE), TILE)
        kept = cd_ref[p] == ab_ref[q]

        @pl.when(kept)
        def _():
            for half, ref in enumerate((plus_ref, minus_ref)):
                out_ref[z, half, :, lanes] = ref[:, q * TILE : (q + 1) * TILE]

        @pl.when(jnp.logical_not(kept))
        def _():
            for half in range(2):
                out_ref[z, half, :, lanes] = jnp.zeros((TILE, TILE), out_ref.dtype)


def mask(cd_irrep, ab_irrep, me, plus, minus):
    width, slab = plus.shape
    smem = pl.BlockSpec(memory_space=pltpu.SMEM)
    masked = pl.pallas_call(
        mask_kernel,
        grid=(width // TILE,),
        in_specs=[smem] * 3 + [pl.BlockSpec((TILE, slab), lambda p: (p, 0))] * 2,
        out_specs=pl.BlockSpec((slab // PAIR, 2, TILE, PAIR), lambda p: (0, 0, p, 0)),
        out_shape=jax.ShapeDtypeStruct((slab // PAIR, 2, width, PAIR), jnp.bfloat16),
        compiler_params=params(),
        cost_estimate=pl.CostEstimate(
            flops=0, bytes_accessed=8 * width * slab, transcendentals=0
        ),
    )(cd_irrep, ab_irrep, me, plus, minus)
    return masked.reshape(slab // PAIR, 2 * width, PAIR)


def ladder_kernel(target_ref, order_ref, own_ref, received_ref, weight_ref, *refs):
    out_refs, both = refs[:-1], refs[-1]
    group, occ, width = own_ref.shape
    span = order_ref.shape[0]
    piece = span // group
    step = pl.program_id(0)

    @pl.when(step == 0)
    def _():
        order = picker(order_ref[...], span)
        for q in range(occ // piece):
            other = jnp.dot(
                order,
                received_ref[q * span : (q + 1) * span, :],
                preferred_element_type=jnp.float32,
            )
            for i in range(group):
                cols = slice(q * piece, (q + 1) * piece)
                own = own_ref[i, cols, :].astype(jnp.float32)
                swap = other[i * piece : (i + 1) * piece]
                rows = slice(i * occ + q * piece, i * occ + (q + 1) * piece)
                both[rows, :width] = (own + swap).astype(jnp.bfloat16)
                both[rows, width:] = (own - swap).astype(jnp.bfloat16)

    term = 0.5 * jnp.dot(both[...], weight_ref[0], preferred_element_type=jnp.float32)
    near = term[:, :TILE].astype(jnp.bfloat16)
    far = term[:, TILE:].astype(jnp.bfloat16)
    if len(out_refs) == 1:
        out_refs[0][0, 0] = near
        out_refs[0][0, 1] = far
    else:
        near_ref, early_ref, late_ref = out_refs
        near_ref[0] = near

        @pl.when(step < FIRST)
        def _():
            early_ref[0] = far

        @pl.when(step >= FIRST)
        def _():
            late_ref[0] = far


def ladder(targets, order, amplitudes, received, weights, chunk, apart):
    _, occ, width = amplitudes.shape
    rows = GROUP * occ
    steps = weights.shape[0]
    if apart:
        counts = (steps, FIRST, steps - FIRST)
        out = [jax.ShapeDtypeStruct((n, rows, TILE), jnp.bfloat16) for n in counts]
        block = (1, rows, TILE)
        out_specs = [
            pl.BlockSpec(block, lambda g, t: (g, 0, 0)),
            pl.BlockSpec(block, lambda g, t: (jnp.minimum(g, FIRST - 1), 0, 0)),
            pl.BlockSpec(block, lambda g, t: (jnp.maximum(g - FIRST, 0), 0, 0)),
        ]
    else:
        out = jax.ShapeDtypeStruct((steps, N_X, rows, TILE), jnp.bfloat16)
        out_specs = pl.BlockSpec((1, N_X, rows, TILE), lambda g, t: (g, 0, 0, 0))
    return pl.pallas_call(
        ladder_kernel,
        grid_spec=pltpu.PrefetchScalarGridSpec(
            num_scalar_prefetch=1,
            grid=(steps,),
            in_specs=[
                pl.BlockSpec(order.shape, lambda g, t: (0, 0)),
                pl.BlockSpec((GROUP, occ, width), lambda g, t: (chunk, 0, 0)),
                pl.BlockSpec((rows, width), lambda g, t: (0, 0)),
                pl.BlockSpec((1, 2 * width, PAIR), lambda g, t: (t[g], 0, 0)),
            ],
            out_specs=out_specs,
            scratch_shapes=[pltpu.VMEM((rows, 2 * width), jnp.bfloat16)],
        ),
        out_shape=out,
        compiler_params=params(),
        cost_estimate=pl.CostEstimate(
            flops=4 * rows * width * steps * PAIR,
            bytes_accessed=4 * rows * width + 4 * width * steps * PAIR + 2 * rows * steps * PAIR,
            transcendentals=0,
        ),
    )(targets, order, amplitudes, received, weights)


def finish_kernel(*refs):
    out_ref = refs[-1]
    at = 0
    for names in ((0, 1), (2, 3, 4, 5), (6, 7)):
        total = 0.0
        for n in names:
            part = refs[n][...].astype(jnp.float32)
            total = total + part.reshape(part.shape[-2:])
        rows = total.shape[0]
        out_ref[:, at : at + rows] = total.T.astype(out_ref.dtype)
        at += rows


def finish(sum0, last0, near1, late1, up1, down1, sum2, last2):
    rows = last0.shape[0]
    whole = pl.BlockSpec((rows, TILE), lambda g: (0, 0))
    last = near1.shape[0] - 1
    late = late1.shape[0] - 1
    scattered = pl.BlockSpec((1, 1, rows, TILE), lambda g: (0, 0, 0, 0))
    return pl.pallas_call(
        finish_kernel,
        grid=(1,),
        in_specs=[
            scattered,
            whole,
            pl.BlockSpec((1, rows, TILE), lambda g: (last, 0, 0)),
            pl.BlockSpec((1, rows, TILE), lambda g: (late, 0, 0)),
            whole,
            whole,
            scattered,
            whole,
        ],
        out_specs=pl.BlockSpec((TILE, 3 * rows), lambda g: (0, 0)),
        out_shape=jax.ShapeDtypeStruct((TILE, 3 * rows), jnp.bfloat16),
        compiler_params=params(),
    )(sum0, last0, near1, late1, up1, down1, sum2, last2)


def add(*parts):
    total = parts[0].astype(jnp.float32)
    for part in parts[1:]:
        total = total + part.astype(jnp.float32)
    return total.astype(jnp.bfloat16)


def on_device(n_z, order_out, order_in, amplitudes, integral_plus, integral_minus, cd_irrep, ab_irrep):
    me = lax.axis_index("xl").reshape(1).astype(jnp.int32)
    place = lax.axis_index("z").astype(jnp.int32)
    half = n_z // 2
    away = [half]
    for d in range(half - 1, 0, -1):
        away += [d, -d]
    away.append(0)
    fixed = jnp.arange(n_z, dtype=jnp.int32)
    turned = (place + jnp.array(away, jnp.int32)) % n_z
    swap = functools.partial(lax.ppermute, axis_name="xl", perm=[(0, 1), (1, 0)])
    up = functools.partial(
        lax.ppermute, axis_name="z", perm=[(k, (k + 1) % n_z) for k in range(n_z)]
    )
    down = functools.partial(
        lax.ppermute, axis_name="z", perm=[((k + 1) % n_z, k) for k in range(n_z)]
    )
    per = GROUP * GROUP * amplitudes.shape[0]

    def exchange(packed):
        return lax.all_to_all(packed, "row", split_axis=0, concat_axis=0, tiled=True)

    def scatter(part):
        return lax.psum_scatter(part, "z", scatter_dimension=0, tiled=True)

    (packed0,) = pack(amplitudes, order_out[:per], 60)
    received0 = exchange(packed0)
    packed1, packed2 = pack(amplitudes, order_out[per:], 16)
    weights = mask(cd_irrep, ab_irrep, me, integral_plus, integral_minus)
    received0, packed1, packed2, weights = lax.optimization_barrier(
        (received0, packed1, packed2, weights)
    )
    part0 = ladder(fixed, order_in, amplitudes, received0, weights, 0, False)
    sum0 = scatter(part0)
    received1 = exchange(packed1)
    received1, packed2, _ = lax.optimization_barrier((received1, packed2, part0))
    near1, early1, late1 = ladder(turned, order_in, amplitudes, received1, weights, 1, True)
    early1 = swap(early1)
    late1 = swap(late1)
    received2 = exchange(packed2)
    received2, early1 = lax.optimization_barrier((received2, early1))
    sum2 = scatter(ladder(fixed, order_in, amplitudes, received2, weights, 2, False))

    middle = near1.shape[1] // 2
    top = ((0, middle), (0, 0))
    bottom = ((middle, 0), (0, 0))

    def send(goes_up, goes_down):
        goes_up, goes_down = lax.optimization_barrier((goes_up, goes_down))
        return lax.optimization_barrier((up(goes_up), down(goes_down)))

    goes_up, goes_down = send(
        add(near1[0, :middle], early1[0, :middle]), add(near1[0, middle:], early1[0, middle:])
    )
    goes_up, goes_down = jnp.pad(goes_up, top), jnp.pad(goes_down, bottom)
    for step in range(1, half):
        a, b = 2 * step - 1, 2 * step
        if step == half - 2:
            goes_up, goes_down, late1 = lax.optimization_barrier((goes_up, goes_down, late1))
        far_a, far_b = (early1[n] if n < FIRST else late1[n - FIRST] for n in (a, b))
        goes_up, goes_down = send(
            add(near1[a], far_a, goes_up), add(near1[b], far_b, goes_down)
        )

    last0 = swap(sum0[0, 1])
    last2 = swap(sum2[0, 1])
    return finish(sum0, last0, near1, late1, goes_up, goes_down, sum2, last2)


def solution(mesh):
    rows, cols = mesh.shape["row"], mesh.shape["col"]
    n_z = cols // N_X
    fine = Mesh(mesh.devices.reshape(rows, n_z, N_X), ("row", "z", "xl"))

    def program(amplitudes, integral_plus, integral_minus, cd_irrep, ab_irrep):
        own = amplitudes.shape[0] // rows
        order_out = column(send_order(own))
        order_in = column(receive_order(own))
        col = ("z", "xl")
        return jax.shard_map(
            functools.partial(on_device, n_z),
            mesh=fine,
            in_specs=(P(), P(), P("row", None, col), P(col, None), P(col, None), P(col), P()),
            out_specs=P(col, "row"),
            check_vma=False,
        )(order_out, order_in, amplitudes, integral_plus, integral_minus, cd_irrep, ab_irrep)

    return program
```

time: 203 us -> 211 us (1.039)
  blocking collectives: 44.3 us -> 0 us
  starting transfers between devices: 10.2 us -> 36.6 us
  local copies, waits for them, and re-layouts: 6 us -> 29.9 us
  Pallas kernels: 48.1 us -> 38.5 us
  waiting for transfers between devices: 78.4 us -> 87 us
    all_to_all x2 -> x0, blocking collectives: 44.3 us -> none  [exchange(): lax.all_to_all(packed, 'row', split_axis=0, concat_axis=0, tiled=True)]
    unnamed x18 -> x48, local copies, waits for them, and re-layouts: 3.9 us -> 28 us
    reduce_scatter x3 -> x2, waiting for transfers between devices: 36.9 us -> 14.9 us  [scatter(): return lax.psum_scatter(part, 'z', scatter_dimension=0, tiled=True)]
    ppermute x1 -> x10, starting transfers between devices: 1.53 us -> 19.7 us  [the longest x8 16.9 us: send(): return lax.optimization_barrier((up(goes_up), down(goes_down)))]
    all_to_all x1 -> x3, waiting for transfers between devices: 6.72 us -> 24.1 us  [exchange(): lax.all_to_all(packed, 'row', split_axis=0, concat_axis=0, tiled=True)]
    pallas_call x7, Pallas kernels: 48.1 us -> 38.5 us  [the longest x3 26.3 us: ladder(): pl.pallas_call(ladder_kernel, grid_spec=pltpu.PrefetchScalarGridSpec(num_...]
    all_to_all x1 -> x3, starting transfers between devices: 6.32 us -> 15.1 us  [exchange(): lax.all_to_all(packed, 'row', split_axis=0, concat_axis=0, tiled=True)]
    ppermute x1 -> x10, waiting for transfers between devices: 34.6 us -> 42.9 us  [the longest x1 22.6 us: on_device(): early1 = swap(early1)]
  transfers between devices with their start and end apart: 7 -> 17, of which waited for: 3 -> 10; matrix products, arithmetic and copies ran while one was open for 2% -> 3% of each run, Pallas kernels for 16% -> 11%
where the time goes in v2:
time: 211 us; the launch traced here: 209 us
  waiting for transfers between devices  87 us (41%)
  Pallas kernels  38.5 us (18%)
  starting transfers between devices  36.6 us (17%)
  local copies, waits for them, and re-layouts  29.9 us (14%)
  between operations  13.6 us (6%)
  other arithmetic  3.5 us (2%)
    unnamed x48, local copies, waits for them, and re-layouts  28 us
    pallas_call x3, Pallas kernels, ladder(): pl.pallas_call(ladder_kernel, grid_spec=pltpu.PrefetchScalarGridSpec(num_...  26.3 us
    all_to_all x3, waiting for transfers between devices, exchange(): lax.all_to_all(packed, 'row', split_axis=0, concat_axis=0, tiled=True)  24.1 us
    ppermute x1, waiting for transfers between devices, on_device(): early1 = swap(early1)  22.6 us
    ppermute x8, waiting for transfers between devices, send(): return lax.optimization_barrier((up(goes_up), down(goes_down)))  20.4 us
    ppermute x8, starting transfers between devices, send(): return lax.optimization_barrier((up(goes_up), down(goes_down)))  16.9 us
    all_to_all x3, starting transfers between devices, exchange(): lax.all_to_all(packed, 'row', split_axis=0, concat_axis=0, tiled=True)  15.1 us
    reduce_scatter x2, waiting for transfers between devices, scatter(): return lax.psum_scatter(part, 'z', scatter_dimension=0, tiled=True)  14.9 us
  transfers between devices with their start and end apart: 17, of which 10 were waited for; matrix products, arithmetic and copies ran while one was open for 3% of the time, Pallas kernels for 11%

profile of v2, /device:TPU:2, one launch (start us, length us, event | category | flops | bytes accessed | tf_op | source)
XLA Modules:
  0.0 209.2 jit_solution(3278508916369532881)
XLA Ops:
  6.5 4.9 %shard_map.82 = bf16[768,768]{1,0:T(8,128)(2,1)} custom-call(s32[192,1]{1,0:T(8,128)} %constant.41.order_ref, bf16[12,192,768]{2,1,0:T(8,128)(2,1)} %own_ref.5, bf16[12,192,768]{2,1,0:T(8,128)(2,1)} %own_ref.5, bf16[12,192,768]{2,1,0:T(8,128)(2,1)} %own_ref.5, bf16[12,192,768]{2,1,0:T(8,128)(2,1)} %own_ref.5), custom_call_target="tpu_custom_call" | custom-call | flops 679477248 | bytes 4718592 | tf_op jit(solution)/shard_map/pallas_call | solution.py:70
  11.4 6.3 %all-to-all-start = ((bf16[16,48,768]{2,1,0:T(8,128)(2,1)}), bf16[16,48,768]{2,1,0:T(8,128)(2,1)}, u32[]{:S(2)}, u32[]{:S(2)}) async-start(bf16[16,48,768]{2,1,0:T(8,128)(2,1)} %bitcast.45), calls=%async_computation | async-start | bytes 2359296 | tf_op jit(solution)/shard_map/all_to_all | solution.py:273
  17.8 1.9 copy-done.9
  19.7 1.9 copy-done.10
  21.6 3.2 %shard_map.84 = bf16[8,2,768,256]{3,2,1,0:T(8,128)(2,1)S(1)} custom-call(s32[6]{0:T(128)S(1)} %copy-done.16, s32[16]{0:T(128)S(1)} %copy-done.17, s32[1]{0:T(128)} %bitcast.2.me_ref, bf16[768,2048]{1,0:T(8,128)(2,1)S(1)} %copy-done.9, bf16[768,2048]{1,0:T(8,128)(2,1)S(1)} %copy-done.10), custom_call_target="tpu_custom_call" | custom-call | bytes 12582912 | tf_op jit(solution)/shard_map/pallas_call | solution.py:111
  24.9 2.6 %copy-done.1 = bf16[8,2,768,256]{3,2,1,0:T(8,128)(2,1)} copy-done((bf16[8,2,768,256]{3,2,1,0:T(8,128)(2,1)}, bf16[8,2,768,256]{3,2,1,0:T(8,128)(2,1)S(1)}, u32[]{:S(2)}) %copy-start.1) | copy-done | bytes 6291480
  27.5 3.0 %shard_map.83 = (bf16[768,768]{1,0:T(8,128)(2,1)S(1)}, bf16[768,768]{1,0:T(8,128)(2,1)S(1)}) custom-call(s32[384,1]{1,0:T(8,128)S(1)} %copy-done.15, bf16[12,192,768]{2,1,0:T(8,128)(2,1)S(1)} %copy-done, bf16[12,192,768]{2,1,0:T(8,128)(2,1)S(1)} %copy-done, bf16[12,192,768]{2,1,0:T(8,128)(2,1)S(1)} %copy-done, bf16[12,192,768]{2,1,0:T(8,128)(2,1)S(1)} %copy-done), custom_call_target="tpu_custom_call" | custom-call | flops 1358954496 | bytes 5898240 | tf_op jit(solution)/shard_map/pallas_call | solution.py:70
  32.7 4.6 %all-to-all-done = bf16[16,48,768]{2,1,0:T(8,128)(2,1)} async-done(((bf16[16,48,768]{2,1,0:T(8,128)(2,1)}), bf16[16,48,768]{2,1,0:T(8,128)(2,1)}, u32[]{:S(2)}, u32[]{:S(2)}) %all-to-all-start) | async-done | bytes 1179680 | tf_op jit(solution)/shard_map/all_to_all | solution.py:273
  37.3 2.8 %copy-done.2 = bf16[8,2,768,256]{3,2,1,0:T(8,128)(2,1)S(1)} copy-done((bf16[8,2,768,256]{3,2,1,0:T(8,128)(2,1)S(1)}, bf16[8,2,768,256]{3,2,1,0:T(8,128)(2,1)}, u32[]{:S(2)}) %copy-start.2) | copy-done | bytes 6291480
  41.0 8.7 %shard_map.85 = bf16[8,2,768,128]{3,2,1,0:T(8,128)(2,1)S(1)} custom-call(s32[8]{0:T(128)S(1)} %iota.5.target_ref, s32[192,1]{1,0:T(8,128)S(1)} %copy-done.20, bf16[12,192,768]{2,1,0:T(8,128)(2,1)S(1)} %copy-done, bf16[768,768]{1,0:T(8,128)(2,1)} %bitcast.1.received_ref, bf16[8,1536,256]{2,1,0:T(8,128)(2,1)S(1)} %bitcast.40), custom_call_target="tpu_custom_call" | custom-call | flops 4831838208 | bytes 11796480 | tf_op jit(solution)/shard_map/pallas_call | solution.py:184
  49.7 1.6 copy-done.7
  51.3 4.4 %all-to-all-start.1 = ((bf16[16,48,768]{2,1,0:T(8,128)(2,1)}), bf16[16,48,768]{2,1,0:T(8,128)(2,1)}, u32[]{:S(2)}, u32[]{:S(2)}) async-start(bf16[16,48,768]{2,1,0:T(8,128)(2,1)} %bitcast.44), calls=%async_computation.2 | async-start | bytes 2359296 | tf_op jit(solution)/shard_map/all_to_all | solution.py:273
  55.8 19.5 %all-to-all-done.1 = bf16[16,48,768]{2,1,0:T(8,128)(2,1)} async-done(((bf16[16,48,768]{2,1,0:T(8,128)(2,1)}), bf16[16,48,768]{2,1,0:T(8,128)(2,1)}, u32[]{:S(2)}, u32[]{:S(2)}) %all-to-all-start.1) | async-done | bytes 1179680 | tf_op jit(solution)/shard_map/all_to_all | solution.py:273
  75.2 4.4 %all-to-all-start.2 = ((bf16[16,48,768]{2,1,0:T(8,128)(2,1)}), bf16[16,48,768]{2,1,0:T(8,128)(2,1)}, u32[]{:S(2)}, u32[]{:S(2)}) async-start(bf16[16,48,768]{2,1,0:T(8,128)(2,1)} %bitcast.43), calls=%async_computation.3 | async-start | bytes 2359296 | tf_op jit(solution)/shard_map/all_to_all | solution.py:273
  79.7 2.9 %copy-done.3 = bf16[8,2,768,256]{3,2,1,0:T(8,128)(2,1)S(1)} copy-done((bf16[8,2,768,256]{3,2,1,0:T(8,128)(2,1)S(1)}, bf16[8,2,768,256]{3,2,1,0:T(8,128)(2,1)}, u32[]{:S(2)}) %copy-start.3) | copy-done | bytes 6291480
  83.4 8.9 %shard_map.86 = (bf16[8,768,128]{2,1,0:T(8,128)(2,1)S(1)}, bf16[5,768,128]{2,1,0:T(8,128)(2,1)S(1)}, bf16[3,768,128]{2,1,0:T(8,128)(2,1)S(1)}) custom-call(s32[8]{0:T(128)S(1)} %and_select_fusion.target_ref, s32[192,1]{1,0:T(8,128)S(1)} %copy-done.21, bf16[12,192,768]{2,1,0:T(8,128)(2,1)S(1)} %copy-done, bf16[768,768]{1,0:T(8,128)(2,1)} %bitcast.6.received_ref, ...), custom_call_target="tpu_custom_call" | custom-call | flops 4831838208 | bytes 11796480 | tf_op jit(solution)/shard_map/pallas_call | solution.py:184
  95.8 22.6 %collective-permute-done.1 = bf16[5,768,128]{2,1,0:T(8,128)(2,1)} collective-permute-done((bf16[5,768,128]{2,1,0:T(8,128)(2,1)S(1)}, bf16[5,768,128]{2,1,0:T(8,128)(2,1)}, u32[]{:S(2)}, u32[]{:S(2)}) %collective-permute-start.1) | collective-permute-done | bytes 983072 | tf_op jit(solution)/shard_map/ppermute | solution.py:290
  118.4 2.8 %copy-done.4 = bf16[8,2,768,256]{3,2,1,0:T(8,128)(2,1)S(1)} copy-done((bf16[8,2,768,256]{3,2,1,0:T(8,128)(2,1)S(1)}, bf16[8,2,768,256]{3,2,1,0:T(8,128)(2,1)}, u32[]{:S(2)}) %copy-start.4) | copy-done | bytes 6291480
  122.1 8.7 %shard_map.87 = bf16[8,2,768,128]{3,2,1,0:T(8,128)(2,1)S(1)} custom-call(s32[8]{0:T(128)S(1)} %iota.6.target_ref, s32[192,1]{1,0:T(8,128)S(1)} %copy-done.22, bf16[12,192,768]{2,1,0:T(8,128)(2,1)S(1)} %copy-done, bf16[768,768]{1,0:T(8,128)(2,1)} %bitcast.8.received_ref, bf16[8,1536,256]{2,1,0:T(8,128)(2,1)S(1)} %bitcast.42), custom_call_target="tpu_custom_call" | custom-call | flops 4831838208 | bytes 11796480 | tf_op jit(solution)/shard_map/pallas_call | solution.py:184
  130.8 1.7 copy-done.8
  133.5 1.4 collective-permute-start.6
  135.9 2.0 collective-permute-start.2
  137.9 4.0 %collective-permute-start.3 = (bf16[384,128]{1,0:T(8,128)(2,1)S(1)}, bf16[384,128]{1,0:T(8,128)(2,1)S(1)}, u32[]{:S(2)}, u32[]{:S(2)}) collective-permute-start(bf16[384,128]{1,0:T(8,128)(2,1)S(1)} %get-tuple-element.49), channel_id=1, source_target_pairs={{2,0},{4,2},{6,4},{8,6},{10,8},{12,10},{14,12},{0,14},{3,1},{5,3},... | collective-permute-start | bytes 294920 | tf_op jit(solution)/shard_map/ppermute | solution.py:302
  142.0 2.5 %collective-permute-done.2 = bf16[384,128]{1,0:T(8,128)(2,1)S(1)} collective-permute-done((bf16[384,128]{1,0:T(8,128)(2,1)S(1)}, bf16[384,128]{1,0:T(8,128)(2,1)S(1)}, u32[]{:S(2)}, u32[]{:S(2)}) %collective-permute-start.2) | collective-permute-done | bytes 98336 | tf_op jit(solution)/shard_map/ppermute | solution.py:302
  145.7 3.4 %collective-permute-start.5 = (bf16[768,128]{1,0:T(8,128)(2,1)S(1)}, bf16[768,128]{1,0:T(8,128)(2,1)S(1)}, u32[]{:S(2)}, u32[]{:S(2)}) collective-permute-start(bf16[768,128]{1,0:T(8,128)(2,1)S(1)} %get-tuple-element.53), channel_id=1, source_target_pairs={{2,0},{4,2},{6,4},{8,6},{10,8},{12,10},{14,12},{0,14},{3,1},{5,3},... | collective-permute-start | bytes 589832 | tf_op jit(solution)/shard_map/ppermute | solution.py:302
  149.1 6.3 %collective-permute-done.4 = bf16[768,128]{1,0:T(8,128)(2,1)S(1)} collective-permute-done((bf16[768,128]{1,0:T(8,128)(2,1)S(1)}, bf16[768,128]{1,0:T(8,128)(2,1)S(1)}, u32[]{:S(2)}, u32[]{:S(2)}) %collective-permute-start.4) | collective-permute-done | bytes 196640 | tf_op jit(solution)/shard_map/ppermute | solution.py:302
  155.4 2.0 collective-permute-done.5
  158.5 2.9 %collective-permute-start.7 = (bf16[768,128]{1,0:T(8,128)(2,1)S(1)}, bf16[768,128]{1,0:T(8,128)(2,1)S(1)}, u32[]{:S(2)}, u32[]{:S(2)}) collective-permute-start(bf16[768,128]{1,0:T(8,128)(2,1)S(1)} %get-tuple-element.60), channel_id=1, source_target_pairs={{0,2},{2,4},{4,6},{6,8},{8,10},{10,12},{12,14},{14,0},{1,3},{3,5},... | collective-permute-start | bytes 589832 | tf_op jit(solution)/shard_map/ppermute | solution.py:302
  162.4 8.5 %collective-permute-done.7 = bf16[768,128]{1,0:T(8,128)(2,1)S(1)} collective-permute-done((bf16[768,128]{1,0:T(8,128)(2,1)S(1)}, bf16[768,128]{1,0:T(8,128)(2,1)S(1)}, u32[]{:S(2)}, u32[]{:S(2)}) %collective-permute-start.7) | collective-permute-done | bytes 196640 | tf_op jit(solution)/shard_map/ppermute | solution.py:302
  172.2 2.9 %collective-permute-start.9 = (bf16[768,128]{1,0:T(8,128)(2,1)S(1)}, bf16[768,128]{1,0:T(8,128)(2,1)S(1)}, u32[]{:S(2)}, u32[]{:S(2)}) collective-permute-start(bf16[768,128]{1,0:T(8,128)(2,1)S(1)} %get-tuple-element.64), channel_id=1, source_target_pairs={{0,2},{2,4},{4,6},{6,8},{8,10},{10,12},{12,14},{14,0},{1,3},{3,5},... | collective-permute-start | bytes 589832 | tf_op jit(solution)/shard_map/ppermute | solution.py:302
  177.3 14.9 %reduce-scatter.5.cloned.1.call-done.refs_6_ = bf16[1,2,768,128]{3,2,1,0:T(8,128)(2,1)} async-done(((bf16[8,2,768,128]{3,2,1,0:T(8,128)(2,1)}), bf16[1,2,768,128]{3,2,1,0:T(8,128)(2,1)}) %reduce-scatter.5.cloned.1.call-update) | async-done | bytes 393232 | tf_op jit(solution)/shard_map/reduce_scatter | solution.py:276
  194.2 5.1 %collective-permute-done.11.refs_7_ = bf16[768,128]{1,0:T(8,128)(2,1)S(1)} collective-permute-done((bf16[768,128]{1,0:T(8,128)(2,1)S(1)}, bf16[768,128]{1,0:T(8,128)(2,1)S(1)}, u32[]{:S(2)}, u32[]{:S(2)}) %collective-permute-start.11) | collective-permute-done | bytes 196640 | tf_op jit(solution)/shard_map/ppermute | solution.py:318
  (68 shorter events, 22.3 us)
Async XLA Ops:
  11.4 6.4 %copy-start.16 = (s32[6]{0:T(128)S(1)}, s32[6]{0:T(128)}, u32[]{:S(2)}) copy-start(s32[6]{0:T(128)} %cd_ref.1) | copy-start | bytes 76
  11.4 6.4 %copy-start.17 = (s32[16]{0:T(128)S(1)}, s32[16]{0:T(128)}, u32[]{:S(2)}) copy-start(s32[16]{0:T(128)} %ab_ref.1) | copy-start | bytes 196
  11.4 25.9 %all-to-all-start = ((bf16[16,48,768]{2,1,0:T(8,128)(2,1)}), bf16[16,48,768]{2,1,0:T(8,128)(2,1)}, u32[]{:S(2)}, u32[]{:S(2)}) async-start(bf16[16,48,768]{2,1,0:T(8,128)(2,1)} %bitcast.45), calls=%async_computation | async-start | bytes 2359296 | tf_op jit(solution)/shard_map/all_to_all | solution.py:273
  17.8 157.9 %reduce-scatter.3.cloned.1.call-start = ((), (), s32[]{:S(2)}) async-start(), calls=%async_computation.5 | async-start | bytes 3538944 | tf_op jit(solution)/shard_map/reduce_scatter | solution.py:276
  17.8 1.9 copy-start.9
  19.7 1.9 copy-start.10
  21.6 5.9 %copy-start = (bf16[12,192,768]{2,1,0:T(8,128)(2,1)S(1)}, bf16[12,192,768]{2,1,0:T(8,128)(2,1)}, u32[]{:S(2)}) copy-start(bf16[12,192,768]{2,1,0:T(8,128)(2,1)} %own_ref.5) | copy-start | bytes 10616836
  21.6 5.9 %copy-start.15 = (s32[384,1]{1,0:T(8,128)S(1)}, s32[384,1]{1,0:T(8,128)}, u32[]{:S(2)}) copy-start(s32[384,1]{1,0:T(8,128)} %constant.42.order_ref) | copy-start | bytes 4612
  24.9 2.7 %copy-start.1 = (bf16[8,2,768,256]{3,2,1,0:T(8,128)(2,1)}, bf16[8,2,768,256]{3,2,1,0:T(8,128)(2,1)S(1)}, u32[]{:S(2)}) copy-start(bf16[8,2,768,256]{3,2,1,0:T(8,128)(2,1)S(1)} %shard_map.84) | copy-start | bytes 18874372
  37.3 2.8 %copy-start.2 = (bf16[8,2,768,256]{3,2,1,0:T(8,128)(2,1)S(1)}, bf16[8,2,768,256]{3,2,1,0:T(8,128)(2,1)}, u32[]{:S(2)}) copy-start(bf16[8,2,768,256]{3,2,1,0:T(8,128)(2,1)} %copy-done.1) | copy-start | bytes 18874372
  49.7 1.6 copy-start.7
  51.3 4.4 %copy-start.23 = (s32[8]{0:T(128)S(1)}, s32[8]{0:T(128)}, u32[]{:S(2)}) copy-start(s32[8]{0:T(128)} %constant.32.clone) | copy-start | bytes 100
  51.3 23.9 %all-to-all-start.1 = ((bf16[16,48,768]{2,1,0:T(8,128)(2,1)}), bf16[16,48,768]{2,1,0:T(8,128)(2,1)}, u32[]{:S(2)}, u32[]{:S(2)}) async-start(bf16[16,48,768]{2,1,0:T(8,128)(2,1)} %bitcast.44), calls=%async_computation.2 | async-start | bytes 2359296 | tf_op jit(solution)/shard_map/all_to_all | solution.py:273
  75.2 43.2 %all-to-all-start.2 = ((bf16[16,48,768]{2,1,0:T(8,128)(2,1)}), bf16[16,48,768]{2,1,0:T(8,128)(2,1)}, u32[]{:S(2)}, u32[]{:S(2)}) async-start(bf16[16,48,768]{2,1,0:T(8,128)(2,1)} %bitcast.43), calls=%async_computation.3 | async-start | bytes 2359296 | tf_op jit(solution)/shard_map/all_to_all | solution.py:273
  79.6 112.5 %reduce-scatter.5.cloned.1.call-start = ((), (), s32[]{:S(2)}) async-start(), calls=%async_computation.6 | async-start | bytes 3538944 | tf_op jit(solution)/shard_map/reduce_scatter | solution.py:276
  79.7 2.9 %copy-start.3 = (bf16[8,2,768,256]{3,2,1,0:T(8,128)(2,1)S(1)}, bf16[8,2,768,256]{3,2,1,0:T(8,128)(2,1)}, u32[]{:S(2)}) copy-start(bf16[8,2,768,256]{3,2,1,0:T(8,128)(2,1)} %copy-done.1) | copy-start | bytes 18874372
  92.3 1.2 copy-start.5
  94.4 24.0 %collective-permute-start.1 = (bf16[5,768,128]{2,1,0:T(8,128)(2,1)S(1)}, bf16[5,768,128]{2,1,0:T(8,128)(2,1)}, u32[]{:S(2)}, u32[]{:S(2)}) collective-permute-start(bf16[5,768,128]{2,1,0:T(8,128)(2,1)S(1)} %get-tuple-element.46), channel_id=1, source_target_pairs={{0,1},{1,0},{2,3},{3,2},{4,5},{5,4},{6,7},{7,6},{8,9},{9,8},{10,11... | collective-permute-start | bytes 2949128 | tf_op jit(solution)/shard_map/ppermute | solution.py:290
  118.4 2.8 %copy-start.4 = (bf16[8,2,768,256]{3,2,1,0:T(8,128)(2,1)S(1)}, bf16[8,2,768,256]{3,2,1,0:T(8,128)(2,1)}, u32[]{:S(2)}) copy-start(bf16[8,2,768,256]{3,2,1,0:T(8,128)(2,1)} %copy-done.1) | copy-start | bytes 18874372
  130.8 1.7 copy-start.8
  132.4 2.5 %copy-start.6 = (bf16[8,768,128]{2,1,0:T(8,128)(2,1)S(1)}, bf16[8,768,128]{2,1,0:T(8,128)(2,1)}, u32[]{:S(2)}) copy-start(bf16[8,768,128]{2,1,0:T(8,128)(2,1)} %copy-done.5) | copy-start | bytes 4718596
  133.5 23.9 %collective-permute-start.6 = (bf16[3,768,128]{2,1,0:T(8,128)(2,1)S(1)}, bf16[3,768,128]{2,1,0:T(8,128)(2,1)S(1)}, u32[]{:S(2)}, u32[]{:S(2)}) collective-permute-start(bf16[3,768,128]{2,1,0:T(8,128)(2,1)S(1)} %copy-done.19), channel_id=1, source_target_pairs={{0,1},{1,0},{2,3},{3,2},{4,5},{5,4},{6,7},{7,6},{8,9},{9,8},{10,11... | collective-permute-start | bytes 1769480 | tf_op jit(solution)/shard_map/ppermute | solution.py:291
  135.9 8.5 %collective-permute-start.2 = (bf16[384,128]{1,0:T(8,128)(2,1)S(1)}, bf16[384,128]{1,0:T(8,128)(2,1)S(1)}, u32[]{:S(2)}, u32[]{:S(2)}) collective-permute-start(bf16[384,128]{1,0:T(8,128)(2,1)S(1)} %get-tuple-element.48), channel_id=1, source_target_pairs={{0,2},{2,4},{4,6},{6,8},{8,10},{10,12},{12,14},{14,0},{1,3},{3,5},... | collective-permute-start | bytes 294920 | tf_op jit(solution)/shard_map/ppermute | solution.py:302
  137.9 6.5 %collective-permute-start.3 = (bf16[384,128]{1,0:T(8,128)(2,1)S(1)}, bf16[384,128]{1,0:T(8,128)(2,1)S(1)}, u32[]{:S(2)}, u32[]{:S(2)}) collective-permute-start(bf16[384,128]{1,0:T(8,128)(2,1)S(1)} %get-tuple-element.49), channel_id=1, source_target_pairs={{2,0},{4,2},{6,4},{8,6},{10,8},{12,10},{14,12},{0,14},{3,1},{5,3},... | collective-permute-start | bytes 294920 | tf_op jit(solution)/shard_map/ppermute | solution.py:302
  145.6 9.8 %collective-permute-start.4 = (bf16[768,128]{1,0:T(8,128)(2,1)S(1)}, bf16[768,128]{1,0:T(8,128)(2,1)S(1)}, u32[]{:S(2)}, u32[]{:S(2)}) collective-permute-start(bf16[768,128]{1,0:T(8,128)(2,1)S(1)} %get-tuple-element.52), channel_id=1, source_target_pairs={{0,2},{2,4},{4,6},{6,8},{8,10},{10,12},{12,14},{14,0},{1,3},{3,5},... | collective-permute-start | bytes 589832 | tf_op jit(solution)/shard_map/ppermute | solution.py:302
  145.7 11.6 %collective-permute-start.5 = (bf16[768,128]{1,0:T(8,128)(2,1)S(1)}, bf16[768,128]{1,0:T(8,128)(2,1)S(1)}, u32[]{:S(2)}, u32[]{:S(2)}) collective-permute-start(bf16[768,128]{1,0:T(8,128)(2,1)S(1)} %get-tuple-element.53), channel_id=1, source_target_pairs={{2,0},{4,2},{6,4},{8,6},{10,8},{12,10},{14,12},{0,14},{3,1},{5,3},... | collective-permute-start | bytes 589832 | tf_op jit(solution)/shard_map/ppermute | solution.py:302
  158.5 12.4 %collective-permute-start.7 = (bf16[768,128]{1,0:T(8,128)(2,1)S(1)}, bf16[768,128]{1,0:T(8,128)(2,1)S(1)}, u32[]{:S(2)}, u32[]{:S(2)}) collective-permute-start(bf16[768,128]{1,0:T(8,128)(2,1)S(1)} %get-tuple-element.60), channel_id=1, source_target_pairs={{0,2},{2,4},{4,6},{6,8},{8,10},{10,12},{12,14},{14,0},{1,3},{3,5},... | collective-permute-start | bytes 589832 | tf_op jit(solution)/shard_map/ppermute | solution.py:302
  161.5 10.5 %collective-permute-start.8 = (bf16[768,128]{1,0:T(8,128)(2,1)S(1)}, bf16[768,128]{1,0:T(8,128)(2,1)S(1)}, u32[]{:S(2)}, u32[]{:S(2)}) collective-permute-start(bf16[768,128]{1,0:T(8,128)(2,1)S(1)} %get-tuple-element.61), channel_id=1, source_target_pairs={{2,0},{4,2},{6,4},{8,6},{10,8},{12,10},{14,12},{0,14},{3,1},{5,3},... | collective-permute-start | bytes 589832 | tf_op jit(solution)/shard_map/ppermute | solution.py:302
  172.2 22.0 %collective-permute-start.9 = (bf16[768,128]{1,0:T(8,128)(2,1)S(1)}, bf16[768,128]{1,0:T(8,128)(2,1)S(1)}, u32[]{:S(2)}, u32[]{:S(2)}) collective-permute-start(bf16[768,128]{1,0:T(8,128)(2,1)S(1)} %get-tuple-element.64), channel_id=1, source_target_pairs={{0,2},{2,4},{4,6},{6,8},{8,10},{10,12},{12,14},{14,0},{1,3},{3,5},... | collective-permute-start | bytes 589832 | tf_op jit(solution)/shard_map/ppermute | solution.py:302
  175.1 19.1 %collective-permute-start.10 = (bf16[768,128]{1,0:T(8,128)(2,1)S(1)}, bf16[768,128]{1,0:T(8,128)(2,1)S(1)}, u32[]{:S(2)}, u32[]{:S(2)}) collective-permute-start(bf16[768,128]{1,0:T(8,128)(2,1)S(1)} %get-tuple-element.65), channel_id=1, source_target_pairs={{2,0},{4,2},{6,4},{8,6},{10,8},{12,10},{14,12},{0,14},{3,1},{5,3},... | collective-permute-start | bytes 589832 | tf_op jit(solution)/shard_map/ppermute | solution.py:302
  176.6 17.6 %collective-permute-start = (bf16[768,128]{1,0:T(8,128)(2,1)S(1)}, bf16[768,128]{1,0:T(8,128)(2,1)S(1)}, u32[]{:S(2)}, u32[]{:S(2)}) collective-permute-start(bf16[768,128]{1,0:T(8,128)(2,1)S(1)} %slice_bitcast_fusion.1), channel_id=1, source_target_pairs={{0,1},{1,0},{2,3},{3,2},{4,5},{5,4},{6,7},{7,6},{8,9},{9,8},{10,11... | collective-permute-start | bytes 589832 | tf_op jit(solution)/shard_map/ppermute | solution.py:317
  193.1 6.2 %collective-permute-start.11 = (bf16[768,128]{1,0:T(8,128)(2,1)S(1)}, bf16[768,128]{1,0:T(8,128)(2,1)S(1)}, u32[]{:S(2)}, u32[]{:S(2)}) collective-permute-start(bf16[768,128]{1,0:T(8,128)(2,1)S(1)} %slice_bitcast_fusion), channel_id=1, source_target_pairs={{0,1},{1,0},{2,3},{3,2},{4,5},{5,4},{6,7},{7,6},{8,9},{9,8},{10,11... | collective-permute-start | bytes 589832 | tf_op jit(solution)/shard_map/ppermute | solution.py:318
  (9 other events, 8.6 us)
Sparse Core Ops, SparseCore 0:
  51.4 46.0 reduce-scatter.2
  132.6 59.5 reduce-scatter.4

commit v3 on v0

v3 whole, which is shorter than its diff:
```python
import functools

import jax
import jax.numpy as jnp
import numpy as np
from jax import lax
from jax.experimental import pallas as pl
from jax.experimental.pallas import tpu as pltpu
from jax.sharding import Mesh
from jax.sharding import PartitionSpec as P

TILE = 128
N_X = 2
PAIR = N_X * TILE
N_S = 4
N_IRREP = 4
CUTS = 2
VMEM = 60 * 2**20


def params():
    return pltpu.CompilerParams(vmem_limit_bytes=VMEM)


def send_order(rows, first, n_i):
    return column(
        (i * N_S + s) * rows + first + jl
        for s in range(N_S)
        for jl in range(n_i)
        for i in range(rows)
    )


def receive_order(rows, chunk, first, n_i):
    return column(
        (s * chunk + first + i) * rows + jl
        for i in range(n_i)
        for s in range(N_S)
        for jl in range(rows)
    )


def column(places):
    return jnp.asarray(np.array(list(places), np.int32)[:, None])


def pack_kernel(order_ref, *refs):
    amp_refs, out_ref = refs[:-1], refs[-1]
    block = jnp.concatenate(
        [r[...].reshape(r.shape[0] * r.shape[1], r.shape[2]) for r in amp_refs], 0
    )
    order = picker(order_ref[...], block.shape[0])
    out_ref[...] = jnp.dot(order, block, preferred_element_type=jnp.float32).astype(out_ref.dtype)


def pack(order, amplitudes):
    rows, occ, width = amplitudes.shape
    wide = N_S * rows
    steps = occ // wide
    per = order.shape[0]
    parts = 4
    return pl.pallas_call(
        pack_kernel,
        grid=(steps,),
        in_specs=[pl.BlockSpec(order.shape, lambda q: (0, 0))]
        + [
            pl.BlockSpec((rows // parts, wide, width), lambda q, k=k: (k, q, 0))
            for k in range(parts)
        ],
        out_specs=pl.BlockSpec((per, width), lambda q: (q, 0)),
        out_shape=jax.ShapeDtypeStruct((steps * per, width), jnp.bfloat16),
        compiler_params=params(),
        cost_estimate=pl.CostEstimate(
            flops=0, bytes_accessed=4 * rows * occ * width, transcendentals=0
        ),
    )(order, *[amplitudes] * parts)


def picker(places, width):
    lanes = lax.broadcasted_iota(jnp.int32, (places.shape[0], width), 1)
    return jnp.where(lanes == places, 1.0, 0.0).astype(jnp.bfloat16)

def ladder_kernel(joined, row_block, first, me_ref, cd_ref, ab_ref, order_ref, amp_ref, got_ref, plus_ref, minus_ref, *refs):
    n_out = 1 if joined else 2
    out_refs = refs[:n_out]
    own, got, held, both, packed, staged, lists, counts, load_sem, out_sem = refs[n_out:]
    n_i, occ, width = own.shape
    kt = width // TILE
    tiles = staged.shape[0]
    me = me_ref[0]
    loads = [
        pltpu.make_async_copy(amp_ref.at[first : first + n_i], own, load_sem.at[0]),
        pltpu.make_async_copy(got_ref, got, load_sem.at[1]),
        pltpu.make_async_copy(plus_ref, held.at[0], load_sem.at[2]),
        pltpu.make_async_copy(minus_ref, held.at[1], load_sem.at[3]),
    ]
    for copy in loads:
        copy.start()

    def of_irrep(g, carry):
        begin, step = carry

        def tile_of(p, n):
            same = cd_ref[p] == g

            @pl.when(same)
            def _():
                lists[begin + n] = p

            return n + same.astype(jnp.int32)

        n = lax.fori_loop(0, kt, tile_of, 0)
        counts[g] = n
        counts[N_IRREP + g] = begin

        def target(q, carry):
            step, waiting = carry
            same = ab_ref[q] == g
            pair = same & (waiting >= 0)
            alone = same & (waiting < 0)

            @pl.when(alone)
            def _():
                lists[kt + 3 * step] = g
                lists[kt + 3 * step + 1] = q
                lists[kt + 3 * step + 2] = q

            @pl.when(pair)
            def _():
                lists[kt + 3 * step + 2] = q

            return (
                jnp.where(pair, step + 1, step),
                jnp.where(same, jnp.where(pair, -1, q), waiting),
            )

        step, waiting = lax.fori_loop(0, tiles, target, (step, -1))
        return begin + n, jnp.where(waiting >= 0, step + 1, step)

    _, steps = lax.fori_loop(0, N_IRREP, of_irrep, (0, 0))

    span = order_ref.shape[0]
    piece = span // n_i
    received = got.shape[0] * piece // occ
    order = picker(order_ref[...], received)
    loads[0].wait()
    loads[1].wait()
    for q in range(occ // piece):
        other = jnp.dot(
            order, got[q * received : (q + 1) * received, :], preferred_element_type=jnp.float32
        )
        mine = own[:, q * piece : (q + 1) * piece, :].reshape(span, width).astype(jnp.float32)
        summed = (mine + other).astype(jnp.bfloat16).reshape(n_i, piece, width)
        differed = (mine - other).astype(jnp.bfloat16).reshape(n_i, piece, width)
        own_rows = slice(q * piece, (q + 1) * piece)
        both[:, own_rows, :width] = summed
        both[:, own_rows, width:] = differed
    loads[2].wait()
    loads[3].wait()

    def out_copy(q):
        z, w = q // N_X, (q % N_X) ^ me
        return z, w, lambda dst: pltpu.make_async_copy(staged.at[q], dst, out_sem.at[q])

    def start(q):
        z, w, copy = out_copy(q)
        if joined:
            copy(out_refs[0].at[z, w]).start()
        else:

            @pl.when(w == 0)
            def _():
                copy(out_refs[0].at[z]).start()

            @pl.when(w == 1)
            def _():
                copy(out_refs[1].at[z]).start()

    rows = n_i * occ

    @pl.loop(0, steps)
    def _(step):
        g, a, b = (lists[kt + 3 * step + k] for k in range(3))
        n, begin = counts[g], counts[N_IRREP + g]

        @pl.loop(0, n)
        def _(k):
            p = lists[begin + k]
            for half in range(2):
                for w, q in enumerate((a, b)):
                    packed[half, pl.ds(pl.multiple_of(k * TILE, TILE), TILE), w * TILE : (w + 1) * TILE] = held[
                        half,
                        pl.ds(pl.multiple_of(p * TILE, TILE), TILE),
                        pl.ds(pl.multiple_of(q * TILE, TILE), TILE),
                    ]

        @pl.when(n == 0)
        def _():
            zero = jnp.zeros(staged.shape[1:], staged.dtype)
            staged[a] = zero
            staged[b] = zero

        for size in range(1, kt + 1):

            @pl.when(n == size)
            def _():
                weights = [packed[half, : size * TILE, :] for half in range(2)]
                for r in range(0, rows, row_block):
                    terms = []
                    for half in range(2):
                        left = jnp.concatenate(
                            [
                                both.reshape(rows, 2 * width)[
                                    r : r + row_block,
                                    pl.ds(
                                        pl.multiple_of(half * width + lists[begin + k] * TILE, TILE),
                                        TILE,
                                    ),
                                ]
                                for k in range(size)
                            ],
                            1,
                        )
                        terms.append(left)
                    term = 0.5 * jnp.dot(
                        jnp.concatenate(terms, 1),
                        jnp.concatenate(weights, 0),
                        preferred_element_type=jnp.float32,
                    )
                    staged[a, r : r + row_block] = term[:, :TILE].astype(staged.dtype)
                    staged[b, r : r + row_block] = term[:, TILE:].astype(staged.dtype)

        start(a)

        @pl.when(b != a)
        def _():
            start(b)

    @pl.loop(0, tiles)
    def _(q):
        z, w, copy = out_copy(q)
        copy(out_refs[0].at[z, w] if joined else out_refs[0].at[z]).wait()


def ladder(me, cd_irrep, ab_irrep, order, amplitudes, received, plus, minus, first, n_i, slots, cost=4e6):
    _, occ, width = amplitudes.shape
    rows = n_i * occ
    tiles = plus.shape[1] // TILE
    n_z = tiles // N_X
    if slots:
        shapes = [(n_z, slots, rows, TILE)]
    else:
        shapes = [(n_z, rows, TILE)] * N_X
    smem = pl.BlockSpec(memory_space=pltpu.SMEM)
    hbm = pl.BlockSpec(memory_space=pl.ANY)
    dma = pltpu.SemaphoreType.DMA
    bf16 = jnp.bfloat16
    return pl.pallas_call(
        functools.partial(ladder_kernel, bool(slots), rows // 2, first),
        in_specs=[smem] * 3 + [pl.BlockSpec(memory_space=pltpu.VMEM)] + [hbm] * 4,
        out_specs=[hbm] * len(shapes),
        out_shape=[jax.ShapeDtypeStruct(s, bf16) for s in shapes],
        scratch_shapes=[
            pltpu.VMEM((n_i, occ, width), bf16),
            pltpu.VMEM(received.shape, bf16),
            pltpu.VMEM((2,) + plus.shape, bf16),
            pltpu.VMEM((n_i, occ, 2 * width), bf16),
            pltpu.VMEM((2, width, PAIR), bf16),
            pltpu.VMEM((tiles, rows, TILE), bf16),
            pltpu.SMEM((width // TILE + 3 * tiles,), jnp.int32),
            pltpu.SMEM((2 * N_IRREP,), jnp.int32),
            dma((4,)),
            dma((tiles,)),
        ],
        compiler_params=params(),
        cost_estimate=pl.CostEstimate(
            flops=0, bytes_accessed=int(cost), transcendentals=0
        ),
    )(me, cd_irrep, ab_irrep, order, amplitudes, received, plus, minus)

def finish_kernel(*refs):
    parts, out_ref = refs[:-1], refs[-1]
    terms = [[parts[0], parts[1]], [parts[4]], [parts[2], parts[3]]]
    at = 0
    for names in terms:
        total = 0.0
        for ref in names:
            part = ref[...].astype(jnp.float32)
            total = total + part.reshape(part.shape[-2:])
        rows = total.shape[0]
        out_ref[:, at : at + rows] = total.T.astype(out_ref.dtype)
        at += rows


def finish(sum0, far0, sum1, far1):
    n0, n1 = far0.shape[0], far1.shape[0]

    def slot(ref, k):
        return pl.BlockSpec((1, 1) + ref.shape[2:], lambda g: (0, k, 0, 0))

    return pl.pallas_call(
        finish_kernel,
        grid=(1,),
        in_specs=[
            slot(sum0, 0),
            pl.BlockSpec(far0.shape, lambda g: (0, 0)),
            slot(sum1, 0),
            pl.BlockSpec(far1.shape, lambda g: (0, 0)),
            slot(sum1, 2),
        ],
        out_specs=pl.BlockSpec((TILE, n0 + 2 * n1), lambda g: (0, 0)),
        out_shape=jax.ShapeDtypeStruct((TILE, n0 + 2 * n1), jnp.bfloat16),
        compiler_params=params(),
    )(sum0, far0, sum1, far1, sum1)


def on_device(amplitudes, plus, minus, cd_irrep, ab_irrep):
    rows = amplitudes.shape[0]
    me = lax.axis_index("xl").reshape(1).astype(jnp.int32)
    swap = functools.partial(lax.ppermute, axis_name="xl", perm=[(0, 1), (1, 0)])
    chunk = rows // CUTS
    part = chunk // 2

    def exchange(packed):
        return lax.all_to_all(packed, "row", split_axis=0, concat_axis=0, tiled=True)

    def scatter(terms):
        return lax.psum_scatter(terms, "z", scatter_dimension=0, tiled=True)

    def product(received, cut, first, n_i, slots, cost=4e6):
        return ladder(
            me,
            cd_irrep,
            ab_irrep,
            receive_order(rows, chunk, first, n_i),
            amplitudes,
            received,
            plus,
            minus,
            cut * chunk + first,
            n_i,
            slots,
            cost,
        )

    packed0 = pack(send_order(rows, 0, chunk), amplitudes)
    received0 = exchange(packed0)
    packed0, later = lax.optimization_barrier((packed0, amplitudes))
    packed1 = pack(send_order(rows, chunk, chunk), later)
    received0, packed1 = lax.optimization_barrier((received0, packed1))
    received1 = exchange(packed1)
    (terms0,) = product(received0, 0, 0, chunk, 2, COST0)
    sum0 = scatter(terms0)
    received1, _ = lax.optimization_barrier((received1, terms0))
    near1, far1 = product(received1, 1, 0, part, 0)
    far1 = swap(far1)
    received1, _ = lax.optimization_barrier((received1, near1))
    (terms1,) = product(received1, 1, part, part, 3)
    added = (near1.astype(jnp.float32) + far1.astype(jnp.float32)).astype(jnp.bfloat16)
    sum1 = scatter(lax.dynamic_update_slice(terms1, added[:, None], (0, 2, 0, 0)))
    return finish(sum0, swap(sum0[0, 1]), sum1, swap(sum1[0, 1]))


COST0 = 4e6


def solution(mesh):
    rows, cols = mesh.shape["row"], mesh.shape["col"]
    fine = Mesh(mesh.devices.reshape(rows, cols // N_X, N_X), ("row", "z", "xl"))
    col = ("z", "xl")
    return jax.shard_map(
        on_device,
        mesh=fine,
        in_specs=(P("row", None, col), P(col, None), P(col, None), P(col), P()),
        out_specs=P(col, "row"),
        check_vma=False,
    )
```

time: 362 us -> 190 us (0.52)
  waiting for transfers between devices: 260 us -> 91.5 us
  Pallas kernels: 0 us -> 41.3 us
  local copies, waits for them, and re-layouts: 36.6 us -> 5.19 us
  matrix products: 30.3 us -> 0 us
  blocking collectives: 0 us -> 29 us
  other arithmetic: 12.9 us -> 1.35 us
    reduce_scatter x1 -> x2, waiting for transfers between devices: 203 us -> 47.3 us  [scatter(): return lax.psum_scatter(terms, 'z', scatter_dimension=0, tiled=True)]
    pallas_call x0 -> x6, Pallas kernels: none -> 41.3 us  [the longest x3 28.4 us: ladder(): pl.pallas_call(functools.partial(ladder_kernel, bool(slots), rows // 2, f...]
    all_to_all x1, waiting for transfers between devices: 57.2 us -> 20.6 us  [exchange(): lax.all_to_all(packed, 'row', split_axis=0, concat_axis=0, tiled=True)]
    dot_general x2 -> x0, matrix products: 30.3 us -> none  [the longest x1 17.4 us: on_device(): lax.dot_general(minus_kept, amp_minus, (((0,), (1,)), ((), ())), preferre...]
    convert_element_type x3 -> x0, local copies, waits for them, and re-layouts: 29.8 us -> none  [on_device(): swapped = jnp.swapaxes(received, 0, 1).astype(jnp.float32)]
    all_to_all x0 -> x1, blocking collectives: none -> 29 us  [exchange(): lax.all_to_all(packed, 'row', split_axis=0, concat_axis=0, tiled=True)]
    ppermute x0 -> x3, waiting for transfers between devices: none -> 23.6 us  [the longest x1 18.6 us: on_device(): far1 = swap(far1)]
    convert_element_type x3 -> x0, other arithmetic: 12.9 us -> none  [the longest x1 6.52 us: on_device(): amp_minus = (wide - swapped).astype(jnp.bfloat16).reshape(own_rows, width)]
  transfers between devices with their start and end apart: 2 -> 6, of which waited for: 2 -> 4; matrix products, arithmetic and copies ran while one was open for 0% -> 2% of each run, Pallas kernels for 0% -> 12%
where the time goes in v3:
time: 190 us; the launch traced here: 189 us
  waiting for transfers between devices  91.5 us (48%)
  Pallas kernels  41.3 us (22%)
  blocking collectives  29 us (15%)
  between operations  13.5 us (7%)
  starting transfers between devices  7.51 us (4%)
  local copies, waits for them, and re-layouts  5.19 us (3%)
    reduce_scatter x2, waiting for transfers between devices, scatter(): return lax.psum_scatter(terms, 'z', scatter_dimension=0, tiled=True)  47.3 us
    all_to_all x1, blocking collectives, exchange(): lax.all_to_all(packed, 'row', split_axis=0, concat_axis=0, tiled=True)  29 us
    pallas_call x3, Pallas kernels, ladder(): pl.pallas_call(functools.partial(ladder_kernel, bool(slots), rows // 2, f...  28.4 us
    all_to_all x1, waiting for transfers between devices, exchange(): lax.all_to_all(packed, 'row', split_axis=0, concat_axis=0, tiled=True)  20.6 us
    ppermute x1, waiting for transfers between devices, on_device(): far1 = swap(far1)  18.6 us
    pallas_call x2, Pallas kernels, pack(): pl.pallas_call(pack_kernel, grid=(steps,), in_specs=[pl.BlockSpec(order.s...  10.5 us
    all_to_all x1, starting transfers between devices, exchange(): lax.all_to_all(packed, 'row', split_axis=0, concat_axis=0, tiled=True)  6.13 us
    ppermute x2, waiting for transfers between devices, on_device(): return finish(sum0, swap(sum0[0, 1]), sum1, swap(sum1[0, 1]))  5.08 us
  transfers between devices with their start and end apart: 6, of which 4 were waited for; matrix products, arithmetic and copies ran while one was open for 2% of the time, Pallas kernels for 12%

profile of v3, /device:TPU:2, one launch (start us, length us, event | category | flops | bytes accessed | tf_op | source)
XLA Modules:
  0.0 189.4 jit_solution(7611912198694637412)
XLA Ops:
  6.5 5.2 %shard_map.100 = bf16[1152,768]{1,0:T(8,128)(2,1)} custom-call(s32[288,1]{1,0:T(8,128)} %constant.18.clone.order_ref, bf16[12,192,768]{2,1,0:T(8,128)(2,1)} %amp_ref.5, bf16[12,192,768]{2,1,0:T(8,128)(2,1)} %amp_ref.5, bf16[12,192,768]{2,1,0:T(8,128)(2,1)} %amp_ref.5, bf16[12,192,768]{2,1,0:T(8,128)(2,1)} %amp_ref.5), custom_call_target="tpu_custom_call" | custom-call | bytes 7077888 | tf_op jit(solution)/shard_map/pallas_call | solution.py:62
  11.8 6.1 %all-to-all-start = ((bf16[16,72,768]{2,1,0:T(8,128)(2,1)}), bf16[16,72,768]{2,1,0:T(8,128)(2,1)S(1)}, u32[]{:S(2)}, u32[]{:S(2)}) async-start(bf16[16,72,768]{2,1,0:T(8,128)(2,1)} %bitcast.17), calls=%async_computation | async-start | bytes 3538944 | tf_op jit(solution)/shard_map/all_to_all | solution.py:325
  17.9 0.0 reduce-scatter.3.cloned.1.call-start
  17.9 5.3 %shard_map.101 = bf16[1152,768]{1,0:T(8,128)(2,1)} custom-call(s32[288,1]{1,0:T(8,128)} %constant.19.clone.order_ref, bf16[12,192,768]{2,1,0:T(8,128)(2,1)} %amp_ref.5, bf16[12,192,768]{2,1,0:T(8,128)(2,1)} %amp_ref.5, bf16[12,192,768]{2,1,0:T(8,128)(2,1)} %amp_ref.5, bf16[12,192,768]{2,1,0:T(8,128)(2,1)} %amp_ref.5), custom_call_target="tpu_custom_call" | custom-call | bytes 7077888 | tf_op jit(solution)/shard_map/pallas_call | solution.py:62
  23.2 20.6 %all-to-all-done = bf16[16,72,768]{2,1,0:T(8,128)(2,1)S(1)} async-done(((bf16[16,72,768]{2,1,0:T(8,128)(2,1)}), bf16[16,72,768]{2,1,0:T(8,128)(2,1)S(1)}, u32[]{:S(2)}, u32[]{:S(2)}) %all-to-all-start) | async-done | bytes 1769504 | tf_op jit(solution)/shard_map/all_to_all | solution.py:325
  43.8 0.0 copy-start
  43.8 1.2 copy-done
  45.0 10.5 %shard_map.102 = bf16[8,2,1152,128]{3,2,1,0:T(8,128)(2,1)} custom-call(s32[1]{0:T(128)} %bitcast.me_ref, s32[6]{0:T(128)} %cd_ref.5, s32[16]{0:T(128)} %ab_ref.5, s32[288,1]{1,0:T(8,128)} %constant.20.clone.order_ref, bf16[12,192,768]{2,1,0:T(8,128)(2,1)} %amp_ref.5, bf16[1152,768]{1,0:T(8,128)(2,1)} %bitcast.15, bf16[768,2048]{1,0:T(8,128)(2,1)} %plus_ref.5, ...), custom_call_target="tpu_custom_call" | custom-call | bytes 4000000 | tf_op jit(solution)/shard_map/pallas_call | solution.py:258
  55.5 0.0 copy-start.1
  55.5 0.0 reduce-scatter.3.cloned.1.call-update
  55.6 0.0 reduce-scatter.5.cloned.1.call-start
  55.6 1.4 copy-done.1
  57.0 29.0 %all_to_all.24 = bf16[16,72,768]{2,1,0:T(8,128)(2,1)} all-to-all(bf16[16,72,768]{2,1,0:T(8,128)(2,1)S(1)} %bitcast.16), channel_id=1, replica_groups=mesh['row'=16,'z'=8,'xl'=2] {'row'}, dimensions={0} | all-to-all | bytes 3538944 | tf_op jit(solution)/shard_map/all_to_all | solution.py:325
  86.0 8.9 %shard_map.103 = (bf16[8,576,128]{2,1,0:T(8,128)(2,1)}, bf16[8,576,128]{2,1,0:T(8,128)(2,1)}) custom-call(s32[1]{0:T(128)} %bitcast.me_ref, s32[6]{0:T(128)} %cd_ref.5, s32[16]{0:T(128)} %ab_ref.5, s32[144,1]{1,0:T(8,128)} %constant.21.clone.order_ref, bf16[12,192,768]{2,1,0:T(8,128)(2,1)} %amp_ref.5, bf16[1152,768]{1,0:T(8,128)(2,1)} %bitcast.13, ...), custom_call_target="tpu_custom_call" | custom-call | bytes 4000000 | tf_op jit(solution)/shard_map/pallas_call | solution.py:258
  94.9 0.3 collective-permute-start.1
  95.2 0.0 copy-start.2
  95.2 9.0 %shard_map.104 = bf16[8,3,576,128]{3,2,1,0:T(8,128)(2,1)} custom-call(s32[1]{0:T(128)} %bitcast.me_ref, s32[6]{0:T(128)} %cd_ref.5, s32[16]{0:T(128)} %ab_ref.5, s32[144,1]{1,0:T(8,128)} %constant.22.clone.order_ref, bf16[12,192,768]{2,1,0:T(8,128)(2,1)} %amp_ref.5, bf16[1152,768]{1,0:T(8,128)(2,1)} %bitcast.14, bf16[768,2048]{1,0:T(8,128)(2,1)} %plus_ref.5, ...), custom_call_target="tpu_custom_call" | custom-call | bytes 4000000 | tf_op jit(solution)/shard_map/pallas_call | solution.py:258
  104.2 18.6 %collective-permute-done.1 = bf16[8,576,128]{2,1,0:T(8,128)(2,1)S(1)} collective-permute-done((bf16[8,576,128]{2,1,0:T(8,128)(2,1)}, bf16[8,576,128]{2,1,0:T(8,128)(2,1)S(1)}, u32[]{:S(2)}, u32[]{:S(2)}) %collective-permute-start.1) | collective-permute-done | bytes 1179680 | tf_op jit(solution)/shard_map/ppermute | solution.py:356
  122.8 0.0 copy-done.2
  122.8 1.4 fusion.1
  124.1 0.0 reduce-scatter.5.cloned.1.call-update
  124.2 0.0 reduce-scatter.3.cloned.1.call-done.refs_0_
  124.2 1.0 slice_bitcast_fusion
  125.2 0.4 collective-permute-start
  125.6 47.3 %reduce-scatter.5.cloned.1.call-done.refs_2_.refs_4_ = bf16[1,3,576,128]{3,2,1,0:T(8,128)(2,1)} async-done(((bf16[8,3,576,128]{3,2,1,0:T(8,128)(2,1)}), bf16[1,3,576,128]{3,2,1,0:T(8,128)(2,1)}) %reduce-scatter.5.cloned.1.call-update) | async-done | bytes 442384 | tf_op jit(solution)/shard_map/reduce_scatter | solution.py:328
  172.8 0.9 slice_bitcast_fusion.1
  173.7 0.6 collective-permute-start.2
  174.4 0.0 collective-permute-done.refs_1_
  174.4 5.1 %collective-permute-done.2.refs_3_ = bf16[576,128]{1,0:T(8,128)(2,1)S(1)} collective-permute-done((bf16[576,128]{1,0:T(8,128)(2,1)S(1)}, bf16[576,128]{1,0:T(8,128)(2,1)S(1)}, u32[]{:S(2)}, u32[]{:S(2)}) %collective-permute-start.2) | collective-permute-done | bytes 147488 | tf_op jit(solution)/shard_map/ppermute | solution.py:361
  179.5 0.0 copy-done.3
  179.5 0.7 copy-done.4
  180.1 2.4 %shard_map.105 = bf16[128,2304]{1,0:T(8,128)(2,1)} custom-call(bf16[1,2,1152,128]{3,2,1,0:T(8,128)(2,1)} %reduce-scatter.3.cloned.1.call-done.refs_0_, bf16[1152,128]{1,0:T(8,128)(2,1)} %copy-done.3, bf16[1,3,576,128]{3,2,1,0:T(8,128)(2,1)} %reduce-scatter.5.cloned.1.call-done.refs_2_.refs_4_, bf16[576,128]{1,0:T(8,128)(2,1)} %copy-done.4, ...), custom_call_target="tpu_custom_call" | custom-call | tf_op jit(solution)/shard_map/pallas_call | solution.py:301
  (2 shorter events, 0.0 us)
Async XLA Ops:
  11.8 32.1 %all-to-all-start = ((bf16[16,72,768]{2,1,0:T(8,128)(2,1)}), bf16[16,72,768]{2,1,0:T(8,128)(2,1)S(1)}, u32[]{:S(2)}, u32[]{:S(2)}) async-start(bf16[16,72,768]{2,1,0:T(8,128)(2,1)} %bitcast.17), calls=%async_computation | async-start | bytes 3538944 | tf_op jit(solution)/shard_map/all_to_all | solution.py:325
  17.9 106.3 %reduce-scatter.3.cloned.1.call-start = ((), (), s32[]{:S(2)}) async-start(), calls=%async_computation.4 | async-start | bytes 5308416 | tf_op jit(solution)/shard_map/reduce_scatter | solution.py:328
  43.8 1.2 copy-start
  55.5 1.5 copy-start.1
  55.6 117.3 %reduce-scatter.5.cloned.1.call-start = ((), (), s32[]{:S(2)}) async-start(), calls=%async_computation.5 | async-start | bytes 3981312 | tf_op jit(solution)/shard_map/reduce_scatter | solution.py:328
  94.9 27.8 %collective-permute-start.1 = (bf16[8,576,128]{2,1,0:T(8,128)(2,1)}, bf16[8,576,128]{2,1,0:T(8,128)(2,1)S(1)}, u32[]{:S(2)}, u32[]{:S(2)}) collective-permute-start(bf16[8,576,128]{2,1,0:T(8,128)(2,1)} %get-tuple-element.18), channel_id=1, source_target_pairs={{0,1},{1,0},{2,3},{3,2},{4,5},{5,4},{6,7},{7,6},{8,9},{9,8},{10,11... | collective-permute-start | bytes 3538952 | tf_op jit(solution)/shard_map/ppermute | solution.py:356
  95.2 27.5 %copy-start.2 = (bf16[8,576,128]{2,1,0:T(8,128)(2,1)S(1)}, bf16[8,576,128]{2,1,0:T(8,128)(2,1)}, u32[]{:S(2)}) copy-start(bf16[8,576,128]{2,1,0:T(8,128)(2,1)} %get-tuple-element.16) | copy-start | bytes 3538948
  125.2 49.2 %collective-permute-start = (bf16[1152,128]{1,0:T(8,128)(2,1)S(1)}, bf16[1152,128]{1,0:T(8,128)(2,1)S(1)}, u32[]{:S(2)}, u32[]{:S(2)}) collective-permute-start(bf16[1152,128]{1,0:T(8,128)(2,1)S(1)} %slice_bitcast_fusion), channel_id=1, source_target_pairs={{0,1},{1,0},{2,3},{3,2},{4,5},{5,4},{6,7},{7,6},{8,9},{9,8},{10,11... | collective-permute-start | bytes 884744 | tf_op jit(solution)/shard_map/ppermute | solution.py:361
  173.7 5.7 %collective-permute-start.2 = (bf16[576,128]{1,0:T(8,128)(2,1)S(1)}, bf16[576,128]{1,0:T(8,128)(2,1)S(1)}, u32[]{:S(2)}, u32[]{:S(2)}) collective-permute-start(bf16[576,128]{1,0:T(8,128)(2,1)S(1)} %slice_bitcast_fusion.1), channel_id=1, source_target_pairs={{0,1},{1,0},{2,3},{3,2},{4,5},{5,4},{6,7},{7,6},{8,9},{9,8},{10,11... | collective-permute-start | bytes 442376 | tf_op jit(solution)/shard_map/ppermute | solution.py:361
  174.4 5.1 %copy-start.3 = (bf16[1152,128]{1,0:T(8,128)(2,1)}, bf16[1152,128]{1,0:T(8,128)(2,1)S(1)}, u32[]{:S(2)}) copy-start(bf16[1152,128]{1,0:T(8,128)(2,1)S(1)} %collective-permute-done.refs_1_) | copy-start | bytes 884740
  179.5 0.7 copy-start.4
Sparse Core Ops, SparseCore 0:
  55.7 59.7 reduce-scatter.2
  124.3 48.4 reduce-scatter.4

commit v4 on v3

v4 whole, which is shorter than its diff:
```python
import functools

import jax
import jax.numpy as jnp
import numpy as np
from jax import lax
from jax.experimental import pallas as pl
from jax.experimental.pallas import tpu as pltpu
from jax.sharding import Mesh
from jax.sharding import PartitionSpec as P

TILE = 128
N_X = 2
PAIR = N_X * TILE
N_S = 4
N_IRREP = 4
BUNDLE = 4
CUTS = 2
EARLY = 2


def params(mib=60):
    return pltpu.CompilerParams(vmem_limit_bytes=mib * 2**20)


def send_order(rows, first, n_i):
    return column(
        (i * N_S + s) * rows + first + jl
        for s in range(N_S)
        for jl in range(n_i)
        for i in range(rows)
    )


def receive_order(rows, chunk, first, n_i):
    return column(
        (s * chunk + first + i) * rows + jl
        for i in range(n_i)
        for s in range(N_S)
        for jl in range(rows)
    )


def column(places):
    return jnp.asarray(np.array(list(places), np.int32)[:, None])


def pack_kernel(order_ref, amp_ref, out_ref, held, sent, in_sem, out_sem):
    rows, occ, width = amp_ref.shape
    per = order_ref.shape[0]
    steps = held.shape[0]
    wide = occ // steps
    loads = [
        pltpu.make_async_copy(amp_ref.at[:, q * wide : (q + 1) * wide, :], held.at[q], in_sem.at[q])
        for q in range(steps)
    ]
    stores = [
        pltpu.make_async_copy(sent.at[q], out_ref.at[q * per : (q + 1) * per, :], out_sem.at[q])
        for q in range(steps)
    ]
    for copy in loads:
        copy.start()
    order = picker(order_ref[...], rows * wide)
    for q in range(steps):
        loads[q].wait()
        block = held[q].reshape(rows * wide, width)
        sent[q] = jnp.dot(order, block, preferred_element_type=jnp.float32).astype(sent.dtype)
        stores[q].start()
    for copy in stores:
        copy.wait()


def pack(order, amplitudes):
    rows, occ, width = amplitudes.shape
    wide = N_S * rows
    steps = occ // wide
    per = order.shape[0]
    hbm = pl.BlockSpec(memory_space=pl.ANY)
    return pl.pallas_call(
        pack_kernel,
        in_specs=[pl.BlockSpec(memory_space=pltpu.VMEM), hbm],
        out_specs=hbm,
        out_shape=jax.ShapeDtypeStruct((steps * per, width), jnp.bfloat16),
        scratch_shapes=[
            pltpu.VMEM((steps, rows, wide, width), jnp.bfloat16),
            pltpu.VMEM((steps, per, width), jnp.bfloat16),
            pltpu.SemaphoreType.DMA((steps,)),
            pltpu.SemaphoreType.DMA((steps,)),
        ],
        compiler_params=params(),
        cost_estimate=pl.CostEstimate(
            flops=0, bytes_accessed=4 * rows * occ * width, transcendentals=0
        ),
    )(order, amplitudes)


def picker(places, width):
    lanes = lax.broadcasted_iota(jnp.int32, (places.shape[0], width), 1)
    return jnp.where(lanes == places, 1.0, 0.0).astype(jnp.bfloat16)

def match_kernel(cd_ref, ab_ref, plus_ref, minus_ref, lists, out_ref, held, packed, in_sem, out_sem):
    kt = cd_ref.shape[0]
    tiles = ab_ref.shape[0]
    loads = [
        pltpu.make_async_copy(plus_ref, held.at[0], in_sem.at[0]),
        pltpu.make_async_copy(minus_ref, held.at[1], in_sem.at[1]),
    ]
    for copy in loads:
        copy.start()
    there = 2 * N_IRREP
    first_step = there + 2 * kt + 2

    def of_irrep(g, carry):
        begin, step, block = carry

        def tile_of(p, n):
            same = cd_ref[p] == g

            @pl.when(same)
            def _():
                lists[there + p] = begin + n
                lists[there + kt + begin + n] = p

            return n + same.astype(jnp.int32)

        n = lax.fori_loop(0, kt, tile_of, 0)
        lists[g] = n
        lists[N_IRREP + g] = begin

        def target(q, carry):
            step, waiting, block = carry
            same = ab_ref[q] == g
            alone = same & (waiting < 0)
            second = same & (waiting >= 0)

            @pl.when(alone)
            def _():
                for k, value in enumerate((g, q, q, block)):
                    lists[first_step + 4 * step + k] = value

            @pl.when(second)
            def _():
                lists[first_step + 4 * step + 2] = q

            return (
                jnp.where(second, step + 1, step),
                jnp.where(same, jnp.where(second, -1, q), waiting),
                jnp.where(alone, block + n, block),
            )

        step, waiting, block = lax.fori_loop(0, tiles, target, (step, -1, block))
        return begin + n, jnp.where(waiting >= 0, step + 1, step), block

    _, steps, blocks = lax.fori_loop(0, N_IRREP, of_irrep, (0, 0, 0))
    bundles = (blocks + BUNDLE - 1) // BUNDLE
    lists[first_step - 2] = bundles
    lists[first_step - 1] = steps
    for copy in loads:
        copy.wait()

    @pl.loop(0, steps)
    def _(step):
        g, a, b, block = (lists[first_step + 4 * step + k] for k in range(4))
        begin = lists[N_IRREP + g]

        @pl.loop(0, lists[g])
        def _(k):
            p = pl.ds(pl.multiple_of(lists[there + kt + begin + k] * TILE, TILE), TILE)
            for half in range(2):
                for w, q in enumerate((a, b)):
                    packed[block + k, half * TILE : (half + 1) * TILE, w * TILE : (w + 1) * TILE] = (
                        held[half, p, pl.ds(pl.multiple_of(q * TILE, TILE), TILE)]
                    )

    def store(k):
        where = pl.ds(k * BUNDLE, BUNDLE)
        return pltpu.make_async_copy(packed.at[where], out_ref.at[where], out_sem.at[k])

    @pl.loop(0, bundles)
    def _(k):
        store(k).start()

    @pl.loop(0, bundles)
    def _(k):
        store(k).wait()


def match(cd_irrep, ab_irrep, plus, minus):
    width, slab = plus.shape
    kt, tiles = width // TILE, slab // TILE
    steps = (tiles + N_IRREP) // 2
    smem = pl.BlockSpec(memory_space=pltpu.SMEM)
    hbm = pl.BlockSpec(memory_space=pl.ANY)
    blocks = (tiles + 1) // N_X * kt
    shape = (blocks, PAIR, PAIR)
    return pl.pallas_call(
        match_kernel,
        in_specs=[smem, smem, hbm, hbm],
        out_specs=[smem, hbm],
        out_shape=[
            jax.ShapeDtypeStruct((2 * N_IRREP + 2 * kt + 2 + 4 * steps,), jnp.int32),
            jax.ShapeDtypeStruct(shape, jnp.bfloat16),
        ],
        scratch_shapes=[
            pltpu.VMEM((2, width, slab), jnp.bfloat16),
            pltpu.VMEM(shape, jnp.bfloat16),
            pltpu.SemaphoreType.DMA((2,)),
            pltpu.SemaphoreType.DMA((blocks // BUNDLE,)),
        ],
        compiler_params=params(),
        cost_estimate=pl.CostEstimate(
            flops=0, bytes_accessed=8 * width * slab, transcendentals=0
        ),
    )(cd_irrep, ab_irrep, plus, minus)


def ladder_kernel(
    first, me_ref, lists, order_ref, amp_ref, got_ref, weight_ref, *refs
):
    n_out = len(refs) - 8
    out_refs = refs[:n_out]
    own, got, weights, both, staged, load_sem, weight_sem, out_sem = refs[n_out:]
    n_i, occ, width = own.shape
    kt = width // TILE
    tiles, per = staged.shape[:2]
    rows = n_i * occ
    me = me_ref[0]
    there = 2 * N_IRREP
    first_step = there + 2 * kt + 2
    bundles, steps = lists[first_step - 2], lists[first_step - 1]
    loads = [
        pltpu.make_async_copy(amp_ref.at[first : first + n_i], own, load_sem.at[0]),
        pltpu.make_async_copy(got_ref, got, load_sem.at[1]),
    ]
    for copy in loads:
        copy.start()

    def weights_copy(k):
        where = pl.ds(k * BUNDLE, BUNDLE)
        return pltpu.make_async_copy(weight_ref.at[where], weights.at[where], weight_sem.at[k])

    @pl.loop(0, bundles)
    def _(k):
        weights_copy(k).start()

    span = order_ref.shape[0]
    piece = span // n_i
    received = got.shape[0] * piece // occ
    order = picker(order_ref[...], received)
    for copy in loads:
        copy.wait()
    for q in range(occ // piece):
        other = jnp.dot(
            order, got[q * received : (q + 1) * received, :], preferred_element_type=jnp.float32
        )
        mine = own[:, q * piece : (q + 1) * piece, :].reshape(span, width).astype(jnp.float32)
        for half, value in enumerate((mine + other, mine - other)):
            value = value.astype(jnp.bfloat16).reshape(n_i, piece, width)
            for p in range(kt):
                lanes = pl.ds(pl.multiple_of(lists[there + p] * PAIR + half * TILE, TILE), TILE)
                both[:, q * piece : (q + 1) * piece, lanes] = value[:, :, p * TILE : (p + 1) * TILE]

    def out_copy(q, dst):
        return pltpu.make_async_copy(staged.at[q], dst, out_sem)

    def start(q):
        z, w = q // N_X, (q % N_X) ^ me
        if n_out == 1:
            out_copy(q, out_refs[0].at[z, pl.ds(w * per, per)]).start()
        else:
            for k in range(N_X):

                @pl.when(w == k)
                def _():
                    out_copy(q, out_refs[k].at[z]).start()

    @pl.loop(0, bundles)
    def _(k):
        weights_copy(k).wait()

    @pl.loop(0, steps)
    def _(step):
        g, a, b, block = (lists[first_step + 4 * step + k] for k in range(4))
        n, begin = lists[g], lists[N_IRREP + g]

        @pl.when(n == 0)
        def _():
            zero = jnp.zeros(staged.shape[1:], staged.dtype)
            staged[a] = zero
            staged[b] = zero

        for size in range(1, kt + 1):

            @pl.when(n == size)
            def _():
                lanes = pl.ds(pl.multiple_of(begin * PAIR, PAIR), size * PAIR)
                left = both[:, :, lanes].reshape(rows, size * PAIR)
                right = weights[pl.ds(block, size)].reshape(size * PAIR, PAIR)
                term = 0.5 * jnp.dot(left, right, preferred_element_type=jnp.float32)
                staged[a] = term[:, :TILE].astype(staged.dtype).reshape(staged.shape[1:])
                staged[b] = term[:, TILE:].astype(staged.dtype).reshape(staged.shape[1:])

        start(a)

        @pl.when(b != a)
        def _():
            start(b)

    pltpu.make_async_copy(staged, staged, out_sem).wait()


def ladder(me, lists, order, amplitudes, received, weights, first, n_i, n_z, per, slots):
    _, occ, width = amplitudes.shape
    rows = n_i * occ
    tiles = n_z * N_X
    blocks = weights.shape[0]
    if slots:
        shapes = [(n_z, slots, rows // per, TILE)]
    else:
        shapes = [(n_z, per, rows // per, TILE)] * N_X
    smem = pl.BlockSpec(memory_space=pltpu.SMEM)
    hbm = pl.BlockSpec(memory_space=pl.ANY)
    dma = pltpu.SemaphoreType.DMA
    bf16 = jnp.bfloat16
    return pl.pallas_call(
        functools.partial(ladder_kernel, first),
        in_specs=[smem, smem, pl.BlockSpec(memory_space=pltpu.VMEM), hbm, hbm, hbm],
        out_specs=[hbm] * len(shapes),
        out_shape=[jax.ShapeDtypeStruct(s, bf16) for s in shapes],
        scratch_shapes=[
            pltpu.VMEM((n_i, occ, width), bf16),
            pltpu.VMEM(received.shape, bf16),
            pltpu.VMEM(weights.shape, bf16),
            pltpu.VMEM((n_i, occ, 2 * width), bf16),
            pltpu.VMEM((tiles, per, rows // per, TILE), bf16),
            dma((2,)),
            dma((blocks // BUNDLE,)),
            dma,
        ],
        compiler_params=params(50),
        cost_estimate=pl.CostEstimate(
            flops=0, bytes_accessed=8 * rows * (width + n_z * TILE), transcendentals=0
        ),
    )(me, lists, order, amplitudes, received, weights)


def finish_kernel(near, far, *refs):
    out_ref = refs[-1]
    total = near[...].astype(jnp.float32).reshape(-1, TILE) + far[...].astype(jnp.float32)
    if len(refs) > 1:
        early = refs[0][...].astype(jnp.float32).reshape(-1, TILE)
        total = jnp.concatenate([early, total], 0)
    out_ref[...] = total.T.astype(out_ref.dtype)


def slots(ref, count, k):
    return pl.BlockSpec((1, count) + ref.shape[2:], lambda g: (0, k, 0, 0))


def finish_first(near, far):
    rows = far.shape[0]
    return pl.pallas_call(
        finish_kernel,
        grid=(1,),
        in_specs=[slots(near, 1, 0), pl.BlockSpec(far.shape, lambda g: (0, 0))],
        out_specs=pl.BlockSpec((TILE, rows), lambda g: (0, 0)),
        out_shape=jax.ShapeDtypeStruct((TILE, CUTS * rows), jnp.bfloat16),
        compiler_params=params(57),
    )(near, far)


def finish_last(done, sum1, far):
    unit = sum1.shape[2]
    per = far.shape[0] // unit
    return pl.pallas_call(
        lambda done_ref, *refs: finish_kernel(*refs),
        grid=(1,),
        in_specs=[
            pl.BlockSpec(memory_space=pl.ANY),
            slots(sum1, per, 0),
            pl.BlockSpec(far.shape, lambda g: (0, 0)),
            slots(sum1, 1, N_X * per),
        ],
        out_specs=pl.BlockSpec((TILE, done.shape[1] // CUTS), lambda g: (0, 1)),
        out_shape=jax.ShapeDtypeStruct(done.shape, jnp.bfloat16),
        input_output_aliases={0: 0},
        compiler_params=params(57),
    )(done, sum1, far, sum1)


def on_device(amplitudes, plus, minus, cd_irrep, ab_irrep):
    rows = amplitudes.shape[0]
    me = lax.axis_index("xl").reshape(1).astype(jnp.int32)
    swap = functools.partial(lax.ppermute, axis_name="xl", perm=[(0, 1), (1, 0)])
    chunk = rows // CUTS

    def exchange(packed):
        return lax.all_to_all(packed, "row", split_axis=0, concat_axis=0, tiled=True)

    def scatter(terms):
        return lax.psum_scatter(terms, "z", scatter_dimension=0, tiled=True)

    def product(received, cut, first, n_i, per, slots):
        return ladder(
            me,
            lists,
            receive_order(rows, chunk, first, n_i),
            amplitudes,
            received,
            weights,
            cut * chunk + first,
            n_i,
            plus.shape[1] // PAIR,
            per,
            slots,
        )

    packed0 = pack(send_order(rows, 0, chunk), amplitudes)
    received0 = exchange(packed0)
    packed0, later = lax.optimization_barrier((packed0, amplitudes))
    packed1 = pack(send_order(rows, chunk, chunk), later)
    packed0, first_plus = lax.optimization_barrier((packed0, plus))
    lists, weights = match(cd_irrep, ab_irrep, first_plus, minus)
    received0, packed1, weights = lax.optimization_barrier((received0, packed1, weights))
    received1 = exchange(packed1)
    (terms0,) = product(received0, 0, 0, chunk, 1, N_X)
    sum0 = scatter(terms0)
    received1, _ = lax.optimization_barrier((received1, terms0))
    near1, far1 = product(received1, 1, 0, EARLY, 1, 0)
    far1 = swap(far1)
    received1, _ = lax.optimization_barrier((received1, near1))
    per = chunk // EARLY - 1
    (terms1,) = product(received1, 1, EARLY, chunk - EARLY, per, N_X * per + 1)
    added = (near1.astype(jnp.float32) + far1.astype(jnp.float32)).astype(jnp.bfloat16)
    sum1 = scatter(lax.dynamic_update_slice(terms1, added, (0, N_X * per, 0, 0)))
    done = finish_first(sum0, swap(sum0[0, 1]))
    last1 = swap(sum1[0, per : 2 * per].reshape(-1, TILE))
    return finish_last(done, sum1, last1)


def solution(mesh):
    rows, cols = mesh.shape["row"], mesh.shape["col"]
    fine = Mesh(mesh.devices.reshape(rows, cols // N_X, N_X), ("row", "z", "xl"))
    col = ("z", "xl")
    return jax.shard_map(
        on_device,
        mesh=fine,
        in_specs=(P("row", None, col), P(col, None), P(col, None), P(col), P()),
        out_specs=P(col, "row"),
        check_vma=False,
    )
```

time: 190 us -> 185 us (0.974)
  waiting for transfers between devices: 91.5 us -> 83.3 us
  starting transfers between devices: 7.51 us -> 9.91 us
  Pallas kernels: 41.3 us -> 43.3 us
    ppermute x1, waiting for transfers between devices: 18.6 us -> 10.4 us  [on_device(): far1 = swap(far1)]
    reduce_scatter x2, waiting for transfers between devices: 47.3 us -> 55 us  [scatter(): return lax.psum_scatter(terms, 'z', scatter_dimension=0, tiled=True)]
    all_to_all x1, waiting for transfers between devices: 20.6 us -> 14.4 us  [exchange(): lax.all_to_all(packed, 'row', split_axis=0, concat_axis=0, tiled=True)]
    ppermute x1, starting transfers between devices: 0.3 us -> 2.38 us  [on_device(): far1 = swap(far1)]
    pallas_call x6 -> x8, Pallas kernels: 41.3 us -> 43.3 us  [the longest x3 22.6 us: ladder(): pl.pallas_call(functools.partial(ladder_kernel, first), in_specs=[smem, s...]
  transfers between devices with their start and end apart: 6 -> 6, of which waited for: 4 -> 5; matrix products, arithmetic and copies ran while one was open for 2% -> 2% of each run, Pallas kernels for 12% -> 15%
where the time goes in v4:
time: 185 us
  waiting for transfers between devices  83.3 us (45%)
  Pallas kernels  43.3 us (23%)
  blocking collectives  28.4 us (15%)
  between operations  13.5 us (7%)
  starting transfers between devices  9.91 us (5%)
  local copies, waits for them, and re-layouts  5.32 us (3%)
    reduce_scatter x2, waiting for transfers between devices, scatter(): return lax.psum_scatter(terms, 'z', scatter_dimension=0, tiled=True)  55 us
    all_to_all x1, blocking collectives, exchange(): lax.all_to_all(packed, 'row', split_axis=0, concat_axis=0, tiled=True)  28.4 us
    pallas_call x3, Pallas kernels, ladder(): pl.pallas_call(functools.partial(ladder_kernel, first), in_specs=[smem, s...  22.6 us
    all_to_all x1, waiting for transfers between devices, exchange(): lax.all_to_all(packed, 'row', split_axis=0, concat_axis=0, tiled=True)  14.4 us
    pallas_call x2, Pallas kernels, pack(): pl.pallas_call(pack_kernel, in_specs=[pl.BlockSpec(memory_space=pltpu.VME...  10.8 us
    ppermute x1, waiting for transfers between devices, on_device(): far1 = swap(far1)  10.4 us
    all_to_all x1, starting transfers between devices, exchange(): lax.all_to_all(packed, 'row', split_axis=0, concat_axis=0, tiled=True)  6.15 us
    pallas_call x1, Pallas kernels, match(): pl.pallas_call(match_kernel, in_specs=[smem, smem, hbm, hbm], out_specs=[...  6.03 us
  transfers between devices with their start and end apart: 6, of which 5 were waited for; matrix products, arithmetic and copies ran while one was open for 2% of the time, Pallas kernels for 15%

profile of v4, /device:TPU:2, one launch (start us, length us, event | category | flops | bytes accessed | tf_op | source)
XLA Modules:
  0.0 185.0 jit_solution(14741188084235970710)
XLA Ops:
  6.5 5.4 %shard_map.101 = bf16[1152,768]{1,0:T(8,128)(2,1)} custom-call(s32[288,1]{1,0:T(8,128)} %constant.18.clone.order_ref, bf16[12,192,768]{2,1,0:T(8,128)(2,1)} %amp_ref.8), custom_call_target="tpu_custom_call" | custom-call | bytes 7077888 | tf_op jit(solution)/shard_map/pallas_call | solution.py:79
  11.9 6.1 %all-to-all-start = ((bf16[16,72,768]{2,1,0:T(8,128)(2,1)}), bf16[16,72,768]{2,1,0:T(8,128)(2,1)S(1)}, u32[]{:S(2)}, u32[]{:S(2)}) async-start(bf16[16,72,768]{2,1,0:T(8,128)(2,1)} %bitcast.12), calls=%async_computation | async-start | bytes 3538944 | tf_op jit(solution)/shard_map/all_to_all | solution.py:398
  18.1 0.0 reduce-scatter.3.cloned.1.call-start
  18.1 5.4 %shard_map.102 = bf16[1152,768]{1,0:T(8,128)(2,1)} custom-call(s32[288,1]{1,0:T(8,128)} %constant.19.clone.order_ref, bf16[12,192,768]{2,1,0:T(8,128)(2,1)} %amp_ref.8), custom_call_target="tpu_custom_call" | custom-call | bytes 7077888 | tf_op jit(solution)/shard_map/pallas_call | solution.py:79
  23.6 0.0 copy-start
  23.6 6.0 %shard_map.100 = (s32[62]{0:T(128)}, bf16[48,256,256]{2,1,0:T(8,128)(2,1)}) custom-call(s32[6]{0:T(128)} %cd_ref.1, s32[16]{0:T(128)} %ab_ref.1, bf16[768,2048]{1,0:T(8,128)(2,1)} %plus_ref, bf16[768,2048]{1,0:T(8,128)(2,1)} %minus_ref.1), custom_call_target="tpu_custom_call" | custom-call | bytes 12582912 | tf_op jit(solution)/shard_map/pallas_call | solution.py:196
  29.6 14.4 %all-to-all-done = bf16[16,72,768]{2,1,0:T(8,128)(2,1)S(1)} async-done(((bf16[16,72,768]{2,1,0:T(8,128)(2,1)}), bf16[16,72,768]{2,1,0:T(8,128)(2,1)S(1)}, u32[]{:S(2)}, u32[]{:S(2)}) %all-to-all-start) | async-done | bytes 1769504 | tf_op jit(solution)/shard_map/all_to_all | solution.py:398
  44.0 0.6 copy-done.3
  44.6 8.5 %shard_map.103 = bf16[8,2,1152,128]{3,2,1,0:T(8,128)(2,1)} custom-call(s32[1]{0:T(128)} %bitcast.me_ref, s32[62]{0:T(128)S(1)} %copy-done.3, s32[288,1]{1,0:T(8,128)S(1)} %copy-done, bf16[12,192,768]{2,1,0:T(8,128)(2,1)} %amp_ref.8, bf16[1152,768]{1,0:T(8,128)(2,1)S(1)} %bitcast.10, bf16[48,256,256]{2,1,0:T(8,128)(2,1)} %get-tuple-element.19.weight_ref), custom_call_target="tpu_custom_call" | custom-call | bytes 16515072 | tf_op jit(solution)/shard_map/pallas_call | solution.py:325
  53.1 0.0 copy-start.2
  53.1 0.0 reduce-scatter.3.cloned.1.call-update
  53.2 0.0 reduce-scatter.5.cloned.1.call-start
  53.2 1.4 copy-done.5
  54.6 28.4 %all_to_all.24 = bf16[16,72,768]{2,1,0:T(8,128)(2,1)S(1)} all-to-all(bf16[16,72,768]{2,1,0:T(8,128)(2,1)S(1)} %bitcast.11), channel_id=1, replica_groups=mesh['row'=16,'z'=8,'xl'=2] {'row'}, dimensions={0} | all-to-all | bytes 3538944 | tf_op jit(solution)/shard_map/all_to_all | solution.py:398
  83.0 7.1 %shard_map.105 = (bf16[8,1,384,128]{3,2,1,0:T(8,128)(2,1)S(1)}, bf16[8,1,384,128]{3,2,1,0:T(8,128)(2,1)S(1)}) custom-call(s32[1]{0:T(128)} %bitcast.me_ref, s32[62]{0:T(128)S(1)} %copy-done.4, s32[96,1]{1,0:T(8,128)S(1)} %copy-done.2, bf16[12,192,768]{2,1,0:T(8,128)(2,1)} %amp_ref.8, bf16[1152,768]{1,0:T(8,128)(2,1)S(1)} %bitcast.8, ...), custom_call_target="tpu_custom_call" | custom-call | bytes 5505024 | tf_op jit(solution)/shard_map/pallas_call | solution.py:325
  90.2 2.4 %collective-permute-start.1 = (bf16[8,1,384,128]{3,2,1,0:T(8,128)(2,1)S(1)}, bf16[8,1,384,128]{3,2,1,0:T(8,128)(2,1)S(1)}, u32[]{:S(2)}, u32[]{:S(2)}) collective-permute-start(bf16[8,1,384,128]{3,2,1,0:T(8,128)(2,1)S(1)} %get-tuple-element.24), channel_id=1, source_target_pairs={{0,1},{1,0},{2,3},{3,2},{4,5},{5,4},{6,7},{7,6},{8,9},{9,8},{10,11... | collective-permute-start | bytes 2359304 | tf_op jit(solution)/shard_map/ppermute | solution.py:430
  92.5 7.0 %shard_map.106 = bf16[8,5,384,128]{3,2,1,0:T(8,128)(2,1)} custom-call(s32[1]{0:T(128)} %bitcast.me_ref, s32[62]{0:T(128)S(1)} %copy-done.4, s32[192,1]{1,0:T(8,128)S(1)} %copy-done.1, bf16[12,192,768]{2,1,0:T(8,128)(2,1)} %amp_ref.8, bf16[1152,768]{1,0:T(8,128)(2,1)S(1)} %bitcast.9, bf16[48,256,256]{2,1,0:T(8,128)(2,1)} %get-tuple-element.19.weight_ref), custom_call_target="tpu_custom_call" | custom-call | bytes 11010048 | tf_op jit(solution)/shard_map/pallas_call | solution.py:325
  99.5 10.4 %collective-permute-done.1 = bf16[8,1,384,128]{3,2,1,0:T(8,128)(2,1)S(1)} collective-permute-done((bf16[8,1,384,128]{3,2,1,0:T(8,128)(2,1)S(1)}, bf16[8,1,384,128]{3,2,1,0:T(8,128)(2,1)S(1)}, u32[]{:S(2)}, u32[]{:S(2)}) %collective-permute-start.1) | collective-permute-done | bytes 786464 | tf_op jit(solution)/shard_map/ppermute | solution.py:430
  109.9 1.1 fusion
  111.0 0.0 reduce-scatter.5.cloned.1.call-update
  111.1 2.6 %reduce-scatter.3.cloned.1.call-done.near = bf16[1,2,1152,128]{3,2,1,0:T(8,128)(2,1)} async-done(((bf16[8,2,1152,128]{3,2,1,0:T(8,128)(2,1)}), bf16[1,2,1152,128]{3,2,1,0:T(8,128)(2,1)}) %reduce-scatter.3.cloned.1.call-update) | async-done | bytes 589840 | tf_op jit(solution)/shard_map/reduce_scatter | solution.py:401
  113.7 1.0 slice_bitcast_fusion
  114.7 0.6 collective-permute-start
  115.3 52.4 %reduce-scatter.5.cloned.1.call-done.refs_0_.refs_2_ = bf16[1,5,384,128]{3,2,1,0:T(8,128)(2,1)} async-done(((bf16[8,5,384,128]{3,2,1,0:T(8,128)(2,1)}), bf16[1,5,384,128]{3,2,1,0:T(8,128)(2,1)}) %reduce-scatter.5.cloned.1.call-update) | async-done | bytes 491536 | tf_op jit(solution)/shard_map/reduce_scatter | solution.py:401
  167.7 0.9 slice.9
  168.7 0.7 collective-permute-start.2
  169.3 0.0 collective-permute-done.far
  169.3 0.7 copy-done.6
  170.1 1.9 %shard_map.104.done_ref = bf16[128,2304]{1,0:T(8,128)(2,1)} custom-call(bf16[1,2,1152,128]{3,2,1,0:T(8,128)(2,1)} %reduce-scatter.3.cloned.1.call-done.near, bf16[1152,128]{1,0:T(8,128)(2,1)} %copy-done.6), custom_call_target="tpu_custom_call" | custom-call | tf_op jit(solution)/shard_map/pallas_call | solution.py:362
  172.0 3.5 %collective-permute-done.2.refs_1_ = bf16[768,128]{1,0:T(8,128)(2,1)S(1)} collective-permute-done((bf16[768,128]{1,0:T(8,128)(2,1)S(1)}, bf16[768,128]{1,0:T(8,128)(2,1)S(1)}, u32[]{:S(2)}, u32[]{:S(2)}) %collective-permute-start.2) | collective-permute-done | bytes 196640 | tf_op jit(solution)/shard_map/ppermute | solution.py:437
  175.5 0.7 copy-done.7
  176.2 2.0 %shard_map.107 = bf16[128,2304]{1,0:T(8,128)(2,1)} custom-call(bf16[128,2304]{1,0:T(8,128)(2,1)} %shard_map.104.done_ref, bf16[1,5,384,128]{3,2,1,0:T(8,128)(2,1)} %reduce-scatter.5.cloned.1.call-done.refs_0_.refs_2_, bf16[768,128]{1,0:T(8,128)(2,1)} %copy-done.7, ...), custom_call_target="tpu_custom_call", output_to_operand_aliasing={{}: (0, {})} | custom-call | tf_op jit(solution)/shard_map/pallas_call | solution.py:375
  (10 shorter events, 0.0 us)
Async XLA Ops:
  11.9 32.1 %all-to-all-start = ((bf16[16,72,768]{2,1,0:T(8,128)(2,1)}), bf16[16,72,768]{2,1,0:T(8,128)(2,1)S(1)}, u32[]{:S(2)}, u32[]{:S(2)}) async-start(bf16[16,72,768]{2,1,0:T(8,128)(2,1)} %bitcast.12), calls=%async_computation | async-start | bytes 3538944 | tf_op jit(solution)/shard_map/all_to_all | solution.py:398
  18.1 95.6 %reduce-scatter.3.cloned.1.call-start = ((), (), s32[]{:S(2)}) async-start(), calls=%async_computation.4 | async-start | bytes 5308416 | tf_op jit(solution)/shard_map/reduce_scatter | solution.py:401
  23.6 20.5 %copy-start = (s32[288,1]{1,0:T(8,128)S(1)}, s32[288,1]{1,0:T(8,128)}, u32[]{:S(2)}) copy-start(s32[288,1]{1,0:T(8,128)} %constant.20.clone.order_ref) | copy-start | bytes 3460
  44.0 0.6 copy-start.3
  53.1 1.5 copy-start.5
  53.1 29.9 %copy-start.2 = (s32[96,1]{1,0:T(8,128)S(1)}, s32[96,1]{1,0:T(8,128)}, u32[]{:S(2)}) copy-start(s32[96,1]{1,0:T(8,128)} %constant.21.clone.order_ref) | copy-start | bytes 1156
  53.1 29.9 %copy-start.4 = (s32[62]{0:T(128)S(1)}, s32[62]{0:T(128)}, u32[]{:S(2)}) copy-start(s32[62]{0:T(128)} %get-tuple-element.15.lists) | copy-start | bytes 748
  53.2 114.6 %reduce-scatter.5.cloned.1.call-start = ((), (), s32[]{:S(2)}) async-start(), calls=%async_computation.5 | async-start | bytes 4423680 | tf_op jit(solution)/shard_map/reduce_scatter | solution.py:401
  83.0 9.5 %copy-start.1 = (s32[192,1]{1,0:T(8,128)S(1)}, s32[192,1]{1,0:T(8,128)}, u32[]{:S(2)}) copy-start(s32[192,1]{1,0:T(8,128)} %constant.22.clone.order_ref) | copy-start | bytes 2308
  90.2 19.8 %collective-permute-start.1 = (bf16[8,1,384,128]{3,2,1,0:T(8,128)(2,1)S(1)}, bf16[8,1,384,128]{3,2,1,0:T(8,128)(2,1)S(1)}, u32[]{:S(2)}, u32[]{:S(2)}) collective-permute-start(bf16[8,1,384,128]{3,2,1,0:T(8,128)(2,1)S(1)} %get-tuple-element.24), channel_id=1, source_target_pairs={{0,1},{1,0},{2,3},{3,2},{4,5},{5,4},{6,7},{7,6},{8,9},{9,8},{10,11... | collective-permute-start | bytes 2359304 | tf_op jit(solution)/shard_map/ppermute | solution.py:430
  114.7 54.7 %collective-permute-start = (bf16[1152,128]{1,0:T(8,128)(2,1)S(1)}, bf16[1152,128]{1,0:T(8,128)(2,1)S(1)}, u32[]{:S(2)}, u32[]{:S(2)}) collective-permute-start(bf16[1152,128]{1,0:T(8,128)(2,1)S(1)} %slice_bitcast_fusion), channel_id=1, source_target_pairs={{0,1},{1,0},{2,3},{3,2},{4,5},{5,4},{6,7},{7,6},{8,9},{9,8},{10,11... | collective-permute-start | bytes 884744 | tf_op jit(solution)/shard_map/ppermute | solution.py:436
  168.7 6.8 %collective-permute-start.2 = (bf16[768,128]{1,0:T(8,128)(2,1)S(1)}, bf16[768,128]{1,0:T(8,128)(2,1)S(1)}, u32[]{:S(2)}, u32[]{:S(2)}) collective-permute-start(bf16[768,128]{1,0:T(8,128)(2,1)S(1)} %bitcast.13), channel_id=1, source_target_pairs={{0,1},{1,0},{2,3},{3,2},{4,5},{5,4},{6,7},{7,6},{8,9},{9,8},{10,11... | collective-permute-start | bytes 589832 | tf_op jit(solution)/shard_map/ppermute | solution.py:437
  169.3 0.7 copy-start.6
  175.5 0.7 copy-start.7
Sparse Core Ops, SparseCore 0:
  53.3 60.3 reduce-scatter.2
  116.3 51.4 reduce-scatter.4

commit v5 on v4

--- a/solution.py
+++ b/solution.py
@@ -15,8 +15,8 @@
 N_S = 4
 N_IRREP = 4
 BUNDLE = 4
-CUTS = 2
-EARLY = 2
+FIRST = 8
+UNIT = 2
 
 
 def params(mib=60):
@@ -364,24 +364,23 @@
         grid=(1,),
         in_specs=[slots(near, 1, 0), pl.BlockSpec(far.shape, lambda g: (0, 0))],
         out_specs=pl.BlockSpec((TILE, rows), lambda g: (0, 0)),
-        out_shape=jax.ShapeDtypeStruct((TILE, CUTS * rows), jnp.bfloat16),
+        out_shape=jax.ShapeDtypeStruct((TILE, 2 * rows), jnp.bfloat16),
         compiler_params=params(57),
     )(near, far)
 
 
 def finish_last(done, sum1, far):
-    unit = sum1.shape[2]
-    per = far.shape[0] // unit
+    early = sum1.shape[1] - N_X
     return pl.pallas_call(
         lambda done_ref, *refs: finish_kernel(*refs),
         grid=(1,),
         in_specs=[
             pl.BlockSpec(memory_space=pl.ANY),
-            slots(sum1, per, 0),
+            slots(sum1, 1, 0),
             pl.BlockSpec(far.shape, lambda g: (0, 0)),
-            slots(sum1, 1, N_X * per),
+            slots(sum1, early, N_X // early),
         ],
-        out_specs=pl.BlockSpec((TILE, done.shape[1] // CUTS), lambda g: (0, 1)),
+        out_specs=pl.BlockSpec((TILE, done.shape[1] // 2), lambda g: (0, 1)),
         out_shape=jax.ShapeDtypeStruct(done.shape, jnp.bfloat16),
         input_output_aliases={0: 0},
         compiler_params=params(57),
@@ -392,7 +391,6 @@
     rows = amplitudes.shape[0]
     me = lax.axis_index("xl").reshape(1).astype(jnp.int32)
     swap = functools.partial(lax.ppermute, axis_name="xl", perm=[(0, 1), (1, 0)])
-    chunk = rows // CUTS
 
     def exchange(packed):
         return lax.all_to_all(packed, "row", split_axis=0, concat_axis=0, tiled=True)
@@ -400,42 +398,46 @@
     def scatter(terms):
         return lax.psum_scatter(terms, "z", scatter_dimension=0, tiled=True)
 
-    def product(received, cut, first, n_i, per, slots):
+    def product(received, begin, count, first, n_i, slots):
         return ladder(
             me,
             lists,
-            receive_order(rows, chunk, first, n_i),
+            receive_order(rows, count, first, n_i),
             amplitudes,
             received,
             weights,
-            cut * chunk + first,
+            begin + first,
             n_i,
             plus.shape[1] // PAIR,
-            per,
+            1,
             slots,
         )
 
-    packed0 = pack(send_order(rows, 0, chunk), amplitudes)
+    rest = rows - FIRST
+    packed0 = pack(send_order(rows, 0, FIRST), amplitudes)
     received0 = exchange(packed0)
     packed0, later = lax.optimization_barrier((packed0, amplitudes))
-    packed1 = pack(send_order(rows, chunk, chunk), later)
+    packed1 = pack(send_order(rows, FIRST, rest), later)
     packed0, first_plus = lax.optimization_barrier((packed0, plus))
     lists, weights = match(cd_irrep, ab_irrep, first_plus, minus)
     received0, packed1, weights = lax.optimization_barrier((received0, packed1, weights))
     received1 = exchange(packed1)
-    (terms0,) = product(received0, 0, 0, chunk, 1, N_X)
+    (terms0,) = product(received0, 0, FIRST, 0, FIRST - UNIT, N_X)
     sum0 = scatter(terms0)
-    received1, _ = lax.optimization_barrier((received1, terms0))
-    near1, far1 = product(received1, 1, 0, EARLY, 1, 0)
+    received0, _ = lax.optimization_barrier((received0, terms0))
+    near0, far0 = product(received0, 0, FIRST, FIRST - UNIT, UNIT, 0)
+    far0 = swap(far0)
+    received1, far0 = lax.optimization_barrier((received1, far0))
+    near1, far1 = product(received1, FIRST, rest, 0, UNIT, 0)
     far1 = swap(far1)
     received1, _ = lax.optimization_barrier((received1, near1))
-    per = chunk // EARLY - 1
-    (terms1,) = product(received1, 1, EARLY, chunk - EARLY, per, N_X * per + 1)
-    added = (near1.astype(jnp.float32) + far1.astype(jnp.float32)).astype(jnp.bfloat16)
-    sum1 = scatter(lax.dynamic_update_slice(terms1, added, (0, N_X * per, 0, 0)))
+    (terms1,) = product(received1, FIRST, rest, UNIT, rest - UNIT, 2 * N_X)
+    for k, (near, far) in enumerate(((near0, far0), (near1, far1))):
+        early = (near.astype(jnp.float32) + far.astype(jnp.float32)).astype(jnp.bfloat16)
+        terms1 = lax.dynamic_update_slice(terms1, early, (0, N_X + k, 0, 0))
+    sum1 = scatter(terms1)
     done = finish_first(sum0, swap(sum0[0, 1]))
-    last1 = swap(sum1[0, per : 2 * per].reshape(-1, TILE))
-    return finish_last(done, sum1, last1)
+    return finish_last(done, sum1, swap(sum1[0, 1]))
 
 
 def solution(mesh):

time: 185 us -> 191 us (1.032)
  blocking collectives: 28.4 us -> 0 us
  waiting for transfers between devices: 83.3 us -> 102 us
  Pallas kernels: 43.3 us -> 53.7 us
  starting transfers between devices: 9.91 us -> 12.6 us
    all_to_all x1 -> x0, blocking collectives: 28.4 us -> none  [exchange(): lax.all_to_all(packed, 'row', split_axis=0, concat_axis=0, tiled=True)]
    ppermute x1 -> x2, waiting for transfers between devices: 3.47 us -> 22.1 us  [the longest x1 20.8 us: on_device(): far0 = swap(far0)]
    pallas_call x3 -> x4, Pallas kernels: 22.6 us -> 32 us  [ladder(): pl.pallas_call(functools.partial(ladder_kernel, first), in_specs=[smem, s...]
    reduce_scatter x2, waiting for transfers between devices: 55 us -> 48.8 us  [scatter(): return lax.psum_scatter(terms, 'z', scatter_dimension=0, tiled=True)]
    all_to_all x1 -> x2, waiting for transfers between devices: 14.4 us -> 20.6 us  [exchange(): lax.all_to_all(packed, 'row', split_axis=0, concat_axis=0, tiled=True)]
    all_to_all x1 -> x2, starting transfers between devices: 6.15 us -> 9.84 us  [exchange(): lax.all_to_all(packed, 'row', split_axis=0, concat_axis=0, tiled=True)]
    unnamed x16 -> x20, local copies, waits for them, and re-layouts: 3.4 us -> 4.57 us
  transfers between devices with their start and end apart: 6 -> 8, of which waited for: 5 -> 5; matrix products, arithmetic and copies ran while one was open for 2% -> 2% of each run, Pallas kernels for 15% -> 19%
where the time goes in v5:
time: 191 us
  waiting for transfers between devices  102 us (53%)
  Pallas kernels  53.7 us (28%)
  between operations  13.6 us (7%)
  starting transfers between devices  12.6 us (7%)
  local copies, waits for them, and re-layouts  6.45 us (3%)
  other arithmetic  2.21 us (1%)
    reduce_scatter x2, waiting for transfers between devices, scatter(): return lax.psum_scatter(terms, 'z', scatter_dimension=0, tiled=True)  48.8 us
    pallas_call x4, Pallas kernels, ladder(): pl.pallas_call(functools.partial(ladder_kernel, first), in_specs=[smem, s...  32 us
    ppermute x1, waiting for transfers between devices, on_device(): far0 = swap(far0)  20.8 us
    all_to_all x2, waiting for transfers between devices, exchange(): lax.all_to_all(packed, 'row', split_axis=0, concat_axis=0, tiled=True)  20.6 us
    pallas_call x2, Pallas kernels, pack(): pl.pallas_call(pack_kernel, in_specs=[pl.BlockSpec(memory_space=pltpu.VME...  10.9 us
    ppermute x1, waiting for transfers between devices, on_device(): far1 = swap(far1)  10.8 us
    all_to_all x2, starting transfers between devices, exchange(): lax.all_to_all(packed, 'row', split_axis=0, concat_axis=0, tiled=True)  9.84 us
    pallas_call x1, Pallas kernels, match(): pl.pallas_call(match_kernel, in_specs=[smem, smem, hbm, hbm], out_specs=[...  6.96 us
  transfers between devices with their start and end apart: 8, of which 5 were waited for; matrix products, arithmetic and copies ran while one was open for 2% of the time, Pallas kernels for 19%

profile of v5, /device:TPU:2, one launch (start us, length us, event | category | flops | bytes accessed | tf_op | source)
XLA Modules:
  0.0 191.0 jit_solution(8531340802077229767)
XLA Ops:
  6.5 6.1 %shard_map.110 = bf16[1536,768]{1,0:T(8,128)(2,1)} custom-call(s32[384,1]{1,0:T(8,128)} %constant.22.clone.order_ref, bf16[12,192,768]{2,1,0:T(8,128)(2,1)} %amp_ref.10), custom_call_target="tpu_custom_call" | custom-call | bytes 7077888 | tf_op jit(solution)/shard_map/pallas_call | solution.py:79
  12.7 6.1 %all-to-all-start = ((bf16[16,96,768]{2,1,0:T(8,128)(2,1)}), bf16[16,96,768]{2,1,0:T(8,128)(2,1)S(1)}, u32[]{:S(2)}, u32[]{:S(2)}) async-start(bf16[16,96,768]{2,1,0:T(8,128)(2,1)} %bitcast.13), calls=%async_computation | async-start | bytes 4718592 | tf_op jit(solution)/shard_map/all_to_all | solution.py:396
  18.8 0.0 reduce-scatter.3.cloned.1.call-start
  18.9 4.8 %shard_map.111 = bf16[768,768]{1,0:T(8,128)(2,1)} custom-call(s32[192,1]{1,0:T(8,128)} %constant.23.clone.order_ref, bf16[12,192,768]{2,1,0:T(8,128)(2,1)} %amp_ref.10), custom_call_target="tpu_custom_call" | custom-call | bytes 7077888 | tf_op jit(solution)/shard_map/pallas_call | solution.py:79
  23.6 7.0 %shard_map.109 = (s32[62]{0:T(128)}, bf16[48,256,256]{2,1,0:T(8,128)(2,1)}) custom-call(s32[6]{0:T(128)} %cd_ref.1, s32[16]{0:T(128)} %ab_ref.1, bf16[768,2048]{1,0:T(8,128)(2,1)} %plus_ref, bf16[768,2048]{1,0:T(8,128)(2,1)} %minus_ref.1), custom_call_target="tpu_custom_call" | custom-call | bytes 12582912 | tf_op jit(solution)/shard_map/pallas_call | solution.py:196
  30.6 20.6 %all-to-all-done = bf16[16,96,768]{2,1,0:T(8,128)(2,1)S(1)} async-done(((bf16[16,96,768]{2,1,0:T(8,128)(2,1)}), bf16[16,96,768]{2,1,0:T(8,128)(2,1)S(1)}, u32[]{:S(2)}, u32[]{:S(2)}) %all-to-all-start) | async-done | bytes 2359328 | tf_op jit(solution)/shard_map/all_to_all | solution.py:396
  51.2 0.7 copy-done.6
  51.9 9.9 %shard_map.112 = bf16[8,2,1152,128]{3,2,1,0:T(8,128)(2,1)} custom-call(s32[1]{0:T(128)} %bitcast.me_ref, s32[62]{0:T(128)S(1)} %copy-done.6, s32[288,1]{1,0:T(8,128)S(1)} %copy-done.2, bf16[12,192,768]{2,1,0:T(8,128)(2,1)} %amp_ref.10, bf16[1536,768]{1,0:T(8,128)(2,1)S(1)} %bitcast.9, bf16[48,256,256]{2,1,0:T(8,128)(2,1)} %get-tuple-element.23.weight_ref), custom_call_target="tpu_custom_call" | custom-call | bytes 16515072 | tf_op jit(solution)/shard_map/pallas_call | solution.py:325
  61.8 3.7 %all-to-all-start.1 = ((bf16[16,48,768]{2,1,0:T(8,128)(2,1)}), bf16[16,48,768]{2,1,0:T(8,128)(2,1)S(1)}, u32[]{:S(2)}, u32[]{:S(2)}) async-start(bf16[16,48,768]{2,1,0:T(8,128)(2,1)} %bitcast.14), calls=%async_computation.2 | async-start | bytes 2359296 | tf_op jit(solution)/shard_map/all_to_all | solution.py:396
  65.5 0.0 reduce-scatter.5.cloned.1.call-start
  65.6 0.8 copy-done.4
  66.4 7.8 %shard_map.114 = (bf16[8,1,384,128]{3,2,1,0:T(8,128)(2,1)S(1)}, bf16[8,1,384,128]{3,2,1,0:T(8,128)(2,1)S(1)}) custom-call(s32[1]{0:T(128)} %bitcast.me_ref, s32[62]{0:T(128)S(1)} %copy-done.7, s32[96,1]{1,0:T(8,128)S(1)} %copy-done.4, bf16[12,192,768]{2,1,0:T(8,128)(2,1)} %amp_ref.10, bf16[1536,768]{1,0:T(8,128)(2,1)S(1)} %bitcast.10, ...), custom_call_target="tpu_custom_call" | custom-call | bytes 5505024 | tf_op jit(solution)/shard_map/pallas_call | solution.py:325
  74.3 0.9 copy-done
  75.2 20.8 %collective-permute-done.1 = bf16[8,1,384,128]{3,2,1,0:T(8,128)(2,1)S(1)} collective-permute-done((bf16[8,1,384,128]{3,2,1,0:T(8,128)(2,1)S(1)}, bf16[8,1,384,128]{3,2,1,0:T(8,128)(2,1)S(1)}, u32[]{:S(2)}, u32[]{:S(2)}) %collective-permute-start.1) | collective-permute-done | bytes 786464 | tf_op jit(solution)/shard_map/ppermute | solution.py:429
  95.9 0.8 copy-done.3
  96.7 7.9 %shard_map.115 = (bf16[8,1,384,128]{3,2,1,0:T(8,128)(2,1)S(1)}, bf16[8,1,384,128]{3,2,1,0:T(8,128)(2,1)S(1)}) custom-call(s32[1]{0:T(128)} %bitcast.me_ref, s32[62]{0:T(128)S(1)} %copy-done.7, s32[96,1]{1,0:T(8,128)S(1)} %copy-done.3, bf16[12,192,768]{2,1,0:T(8,128)(2,1)} %amp_ref.10, bf16[768,768]{1,0:T(8,128)(2,1)S(1)} %bitcast.11, ...), custom_call_target="tpu_custom_call" | custom-call | bytes 5505024 | tf_op jit(solution)/shard_map/pallas_call | solution.py:325
  104.7 1.0 collective-permute-start.2
  105.7 6.4 %shard_map.116 = bf16[8,4,384,128]{3,2,1,0:T(8,128)(2,1)} custom-call(s32[1]{0:T(128)} %bitcast.me_ref, s32[62]{0:T(128)S(1)} %copy-done.7, s32[96,1]{1,0:T(8,128)S(1)} %copy-done.5, bf16[12,192,768]{2,1,0:T(8,128)(2,1)} %amp_ref.10, bf16[768,768]{1,0:T(8,128)(2,1)S(1)} %bitcast.12, bf16[48,256,256]{2,1,0:T(8,128)(2,1)} %get-tuple-element.23.weight_ref), custom_call_target="tpu_custom_call" | custom-call | bytes 5505024 | tf_op jit(solution)/shard_map/pallas_call | solution.py:325
  112.1 1.1 fusion
  113.2 10.8 %collective-permute-done.2 = bf16[8,1,384,128]{3,2,1,0:T(8,128)(2,1)S(1)} collective-permute-done((bf16[8,1,384,128]{3,2,1,0:T(8,128)(2,1)S(1)}, bf16[8,1,384,128]{3,2,1,0:T(8,128)(2,1)S(1)}, u32[]{:S(2)}, u32[]{:S(2)}) %collective-permute-start.2) | collective-permute-done | bytes 786464 | tf_op jit(solution)/shard_map/ppermute | solution.py:432
  124.1 1.1 fusion.1
  125.2 0.0 reduce-scatter.3.cloned.1.call-done.near
  125.3 1.0 slice_bitcast_fusion
  126.2 1.1 collective-permute-start
  127.3 48.8 %reduce-scatter.5.cloned.1.call-done.refs_0_.refs_2_ = bf16[1,4,384,128]{3,2,1,0:T(8,128)(2,1)} async-done(((bf16[8,4,384,128]{3,2,1,0:T(8,128)(2,1)}), bf16[1,4,384,128]{3,2,1,0:T(8,128)(2,1)}) %reduce-scatter.5.cloned.1.call-update) | async-done | bytes 393232 | tf_op jit(solution)/shard_map/reduce_scatter | solution.py:399
  176.1 0.9 slice_bitcast_fusion.1
  177.0 0.6 collective-permute-start.3
  177.6 0.7 copy-done.8
  178.3 1.9 %shard_map.113.done_ref = bf16[128,2304]{1,0:T(8,128)(2,1)} custom-call(bf16[1,2,1152,128]{3,2,1,0:T(8,128)(2,1)} %reduce-scatter.3.cloned.1.call-done.near, bf16[1152,128]{1,0:T(8,128)(2,1)} %copy-done.8), custom_call_target="tpu_custom_call" | custom-call | tf_op jit(solution)/shard_map/pallas_call | solution.py:362
  180.3 1.3 collective-permute-done.3.refs_1_
  181.6 0.6 copy-done.9
  182.3 1.9 shard_map.117
  (19 shorter events, 0.1 us)
Async XLA Ops:
  12.7 38.6 %all-to-all-start = ((bf16[16,96,768]{2,1,0:T(8,128)(2,1)}), bf16[16,96,768]{2,1,0:T(8,128)(2,1)S(1)}, u32[]{:S(2)}, u32[]{:S(2)}) async-start(bf16[16,96,768]{2,1,0:T(8,128)(2,1)} %bitcast.13), calls=%async_computation | async-start | bytes 4718592 | tf_op jit(solution)/shard_map/all_to_all | solution.py:396
  18.8 106.4 %reduce-scatter.3.cloned.1.call-start = ((), (), s32[]{:S(2)}) async-start(), calls=%async_computation.4 | async-start | bytes 5308416 | tf_op jit(solution)/shard_map/reduce_scatter | solution.py:399
  23.6 27.6 %copy-start.2 = (s32[288,1]{1,0:T(8,128)S(1)}, s32[288,1]{1,0:T(8,128)}, u32[]{:S(2)}) copy-start(s32[288,1]{1,0:T(8,128)} %constant.24.clone.order_ref) | copy-start | bytes 3460
  51.2 0.7 copy-start.6
  61.8 3.8 %copy-start.7 = (s32[62]{0:T(128)S(1)}, s32[62]{0:T(128)}, u32[]{:S(2)}) copy-start(s32[62]{0:T(128)} %get-tuple-element.19.lists) | copy-start | bytes 748
  61.8 34.1 %all-to-all-start.1 = ((bf16[16,48,768]{2,1,0:T(8,128)(2,1)}), bf16[16,48,768]{2,1,0:T(8,128)(2,1)S(1)}, u32[]{:S(2)}, u32[]{:S(2)}) async-start(bf16[16,48,768]{2,1,0:T(8,128)(2,1)} %bitcast.14), calls=%async_computation.2 | async-start | bytes 2359296 | tf_op jit(solution)/shard_map/all_to_all | solution.py:396
  65.5 110.6 %reduce-scatter.5.cloned.1.call-start = ((), (), s32[]{:S(2)}) async-start(), calls=%async_computation.5 | async-start | bytes 3538944 | tf_op jit(solution)/shard_map/reduce_scatter | solution.py:399
  65.6 0.8 copy-start.4
  74.2 0.9 copy-start
  75.2 20.8 %collective-permute-start.1 = (bf16[8,1,384,128]{3,2,1,0:T(8,128)(2,1)S(1)}, bf16[8,1,384,128]{3,2,1,0:T(8,128)(2,1)S(1)}, u32[]{:S(2)}, u32[]{:S(2)}) collective-permute-start(bf16[8,1,384,128]{3,2,1,0:T(8,128)(2,1)S(1)} %get-tuple-element.26), channel_id=1, source_target_pairs={{0,1},{1,0},{2,3},{3,2},{4,5},{5,4},{6,7},{7,6},{8,9},{9,8},{10,11... | collective-permute-start | bytes 2359304 | tf_op jit(solution)/shard_map/ppermute | solution.py:429
  95.9 0.8 copy-start.3
  96.7 9.0 %copy-start.5 = (s32[96,1]{1,0:T(8,128)S(1)}, s32[96,1]{1,0:T(8,128)}, u32[]{:S(2)}) copy-start(s32[96,1]{1,0:T(8,128)} %constant.27.clone.order_ref) | copy-start | bytes 1156
  104.7 19.4 %collective-permute-start.2 = (bf16[8,1,384,128]{3,2,1,0:T(8,128)(2,1)S(1)}, bf16[8,1,384,128]{3,2,1,0:T(8,128)(2,1)S(1)}, u32[]{:S(2)}, u32[]{:S(2)}) collective-permute-start(bf16[8,1,384,128]{3,2,1,0:T(8,128)(2,1)S(1)} %get-tuple-element.32), channel_id=1, source_target_pairs={{0,1},{1,0},{2,3},{3,2},{4,5},{5,4},{6,7},{7,6},{8,9},{9,8},{10,11... | collective-permute-start | bytes 2359304 | tf_op jit(solution)/shard_map/ppermute | solution.py:432
  105.7 6.4 %copy-start.1 = (bf16[8,1,384,128]{3,2,1,0:T(8,128)(2,1)S(1)}, bf16[8,1,384,128]{3,2,1,0:T(8,128)(2,1)}, u32[]{:S(2)}) copy-start(bf16[8,1,384,128]{3,2,1,0:T(8,128)(2,1)} %copy-done) | copy-start | bytes 2359300
  126.2 51.4 %collective-permute-start = (bf16[1152,128]{1,0:T(8,128)(2,1)S(1)}, bf16[1152,128]{1,0:T(8,128)(2,1)S(1)}, u32[]{:S(2)}, u32[]{:S(2)}) collective-permute-start(bf16[1152,128]{1,0:T(8,128)(2,1)S(1)} %slice_bitcast_fusion), channel_id=1, source_target_pairs={{0,1},{1,0},{2,3},{3,2},{4,5},{5,4},{6,7},{7,6},{8,9},{9,8},{10,11... | collective-permute-start | bytes 884744 | tf_op jit(solution)/shard_map/ppermute | solution.py:439
  177.0 4.6 %collective-permute-start.3 = (bf16[384,128]{1,0:T(8,128)(2,1)S(1)}, bf16[384,128]{1,0:T(8,128)(2,1)S(1)}, u32[]{:S(2)}, u32[]{:S(2)}) collective-permute-start(bf16[384,128]{1,0:T(8,128)(2,1)S(1)} %slice_bitcast_fusion.1), channel_id=1, source_target_pairs={{0,1},{1,0},{2,3},{3,2},{4,5},{5,4},{6,7},{7,6},{8,9},{9,8},{10,11... | collective-permute-start | bytes 294920 | tf_op jit(solution)/shard_map/ppermute | solution.py:440
  177.6 0.7 copy-start.8
  181.6 0.6 copy-start.9
Sparse Core Ops, SparseCore 0:
  61.9 58.9 reduce-scatter.2
  125.3 50.7 reduce-scatter.4

commit v6 on v5

--- a/solution.py
+++ b/solution.py
@@ -2,7 +2,6 @@
 
 import jax
 import jax.numpy as jnp
-import numpy as np
 from jax import lax
 from jax.experimental import pallas as pl
 from jax.experimental.pallas import tpu as pltpu
@@ -15,6 +14,7 @@
 N_S = 4
 N_IRREP = 4
 BUNDLE = 4
+AHEAD = 2
 FIRST = 8
 UNIT = 2
 
@@ -23,32 +23,30 @@
     return pltpu.CompilerParams(vmem_limit_bytes=mib * 2**20)
 
 
+def digits(count, last, middle):
+    row = lax.broadcasted_iota(jnp.int32, (count, 1), 0)
+
+    def over(value, size):
+        return ((value.astype(jnp.float32) + 0.5) * (1.0 / size)).astype(jnp.int32)
+
+    upper = over(row, last)
+    top = over(upper, middle)
+    return top, upper - top * middle, row - upper * last
+
+
 def send_order(rows, first, n_i):
-    return column(
-        (i * N_S + s) * rows + first + jl
-        for s in range(N_S)
-        for jl in range(n_i)
-        for i in range(rows)
-    )
-
-
-def receive_order(rows, chunk, first, n_i):
-    return column(
-        (s * chunk + first + i) * rows + jl
-        for i in range(n_i)
-        for s in range(N_S)
-        for jl in range(rows)
-    )
-
-
-def column(places):
-    return jnp.asarray(np.array(list(places), np.int32)[:, None])
-
-
-def pack_kernel(order_ref, amp_ref, out_ref, held, sent, in_sem, out_sem):
+    s, jl, i = digits(N_S * n_i * rows, rows, n_i)
+    return (i * N_S + s) * rows + first + jl
+
+
+def receive_order(rows, count, first, n_i):
+    i, s, jl = digits(n_i * N_S * rows, rows, N_S)
+    return (s * count + first + i) * rows + jl
+
+
+def pack_kernel(first, n_i, amp_ref, out_ref, held, sent, in_sem, out_sem):
     rows, occ, width = amp_ref.shape
-    per = order_ref.shape[0]
-    steps = held.shape[0]
+    steps, per = sent.shape[:2]
     wide = occ // steps
     loads = [
         pltpu.make_async_copy(amp_ref.at[:, q * wide : (q + 1) * wide, :], held.at[q], in_sem.at[q])
@@ -58,11 +56,13 @@
         pltpu.make_async_copy(sent.at[q], out_ref.at[q * per : (q + 1) * per, :], out_sem.at[q])
         for q in range(steps)
     ]
-    for copy in loads:
+    for copy in loads[:AHEAD]:
         copy.start()
-    order = picker(order_ref[...], rows * wide)
+    order = picker(send_order(rows, first, n_i), rows * wide)
     for q in range(steps):
         loads[q].wait()
+        if q + AHEAD < steps:
+            loads[q + AHEAD].start()
         block = held[q].reshape(rows * wide, width)
         sent[q] = jnp.dot(order, block, preferred_element_type=jnp.float32).astype(sent.dtype)
         stores[q].start()
@@ -70,15 +70,15 @@
         copy.wait()
 
 
-def pack(order, amplitudes):
+def pack(amplitudes, first, n_i):
     rows, occ, width = amplitudes.shape
     wide = N_S * rows
     steps = occ // wide
-    per = order.shape[0]
+    per = N_S * n_i * rows
     hbm = pl.BlockSpec(memory_space=pl.ANY)
     return pl.pallas_call(
-        pack_kernel,
-        in_specs=[pl.BlockSpec(memory_space=pltpu.VMEM), hbm],
+        functools.partial(pack_kernel, first, n_i),
+        in_specs=[hbm],
         out_specs=hbm,
         out_shape=jax.ShapeDtypeStruct((steps * per, width), jnp.bfloat16),
         scratch_shapes=[
@@ -91,7 +91,7 @@
         cost_estimate=pl.CostEstimate(
             flops=0, bytes_accessed=4 * rows * occ * width, transcendentals=0
         ),
-    )(order, amplitudes)
+    )(amplitudes)
 
 
 def picker(places, width):
@@ -214,9 +214,7 @@
     )(cd_irrep, ab_irrep, plus, minus)
 
 
-def ladder_kernel(
-    first, me_ref, lists, order_ref, amp_ref, got_ref, weight_ref, *refs
-):
+def ladder_kernel(begin_i, first, me_ref, lists, amp_ref, got_ref, weight_ref, *refs):
     n_out = len(refs) - 8
     out_refs = refs[:n_out]
     own, got, weights, both, staged, load_sem, weight_sem, out_sem = refs[n_out:]
@@ -229,7 +227,7 @@
     first_step = there + 2 * kt + 2
     bundles, steps = lists[first_step - 2], lists[first_step - 1]
     loads = [
-        pltpu.make_async_copy(amp_ref.at[first : first + n_i], own, load_sem.at[0]),
+        pltpu.make_async_copy(amp_ref.at[begin_i + first : begin_i + first + n_i], own, load_sem.at[0]),
         pltpu.make_async_copy(got_ref, got, load_sem.at[1]),
     ]
     for copy in loads:
@@ -243,10 +241,11 @@
     def _(k):
         weights_copy(k).start()
 
-    span = order_ref.shape[0]
-    piece = span // n_i
+    local = amp_ref.shape[0]
+    piece = N_S * local
+    span = n_i * piece
     received = got.shape[0] * piece // occ
-    order = picker(order_ref[...], received)
+    order = picker(receive_order(local, received // piece, first, n_i), received)
     for copy in loads:
         copy.wait()
     for q in range(occ // piece):
@@ -309,7 +308,7 @@
     pltpu.make_async_copy(staged, staged, out_sem).wait()
 
 
-def ladder(me, lists, order, amplitudes, received, weights, first, n_i, n_z, per, slots):
+def ladder(me, lists, amplitudes, received, weights, begin, first, n_i, n_z, per, slots):
     _, occ, width = amplitudes.shape
     rows = n_i * occ
     tiles = n_z * N_X
@@ -323,8 +322,8 @@
     dma = pltpu.SemaphoreType.DMA
     bf16 = jnp.bfloat16
     return pl.pallas_call(
-        functools.partial(ladder_kernel, first),
-        in_specs=[smem, smem, pl.BlockSpec(memory_space=pltpu.VMEM), hbm, hbm, hbm],
+        functools.partial(ladder_kernel, begin, first),
+        in_specs=[smem, smem, hbm, hbm, hbm],
         out_specs=[hbm] * len(shapes),
         out_shape=[jax.ShapeDtypeStruct(s, bf16) for s in shapes],
         scratch_shapes=[
@@ -341,7 +340,7 @@
         cost_estimate=pl.CostEstimate(
             flops=0, bytes_accessed=8 * rows * (width + n_z * TILE), transcendentals=0
         ),
-    )(me, lists, order, amplitudes, received, weights)
+    )(me, lists, amplitudes, received, weights)
 
 
 def finish_kernel(near, far, *refs):
@@ -383,7 +382,7 @@
         out_specs=pl.BlockSpec((TILE, done.shape[1] // 2), lambda g: (0, 1)),
         out_shape=jax.ShapeDtypeStruct(done.shape, jnp.bfloat16),
         input_output_aliases={0: 0},
-        compiler_params=params(57),
+        compiler_params=params(16),
     )(done, sum1, far, sum1)
 
 
@@ -398,15 +397,15 @@
     def scatter(terms):
         return lax.psum_scatter(terms, "z", scatter_dimension=0, tiled=True)
 
-    def product(received, begin, count, first, n_i, slots):
+    def product(received, begin, first, n_i, slots):
         return ladder(
             me,
             lists,
-            receive_order(rows, count, first, n_i),
             amplitudes,
             received,
             weights,
-            begin + first,
+            begin,
+            first,
             n_i,
             plus.shape[1] // PAIR,
             1,
@@ -414,24 +413,24 @@
         )
 
     rest = rows - FIRST
-    packed0 = pack(send_order(rows, 0, FIRST), amplitudes)
+    packed0 = pack(amplitudes, 0, FIRST)
     received0 = exchange(packed0)
     packed0, later = lax.optimization_barrier((packed0, amplitudes))
-    packed1 = pack(send_order(rows, FIRST, rest), later)
+    packed1 = pack(later, FIRST, rest)
     packed0, first_plus = lax.optimization_barrier((packed0, plus))
     lists, weights = match(cd_irrep, ab_irrep, first_plus, minus)
     received0, packed1, weights = lax.optimization_barrier((received0, packed1, weights))
     received1 = exchange(packed1)
-    (terms0,) = product(received0, 0, FIRST, 0, FIRST - UNIT, N_X)
+    (terms0,) = product(received0, 0, 0, FIRST - UNIT, N_X)
     sum0 = scatter(terms0)
     received0, _ = lax.optimization_barrier((received0, terms0))
-    near0, far0 = product(received0, 0, FIRST, FIRST - UNIT, UNIT, 0)
+    near0, far0 = product(received0, 0, FIRST - UNIT, UNIT, 0)
     far0 = swap(far0)
-    received1, far0 = lax.optimization_barrier((received1, far0))
-    near1, far1 = product(received1, FIRST, rest, 0, UNIT, 0)
+    received1, _ = lax.optimization_barrier((received1, near0))
+    near1, far1 = product(received1, FIRST, 0, UNIT, 0)
     far1 = swap(far1)
     received1, _ = lax.optimization_barrier((received1, near1))
-    (terms1,) = product(received1, FIRST, rest, UNIT, rest - UNIT, 2 * N_X)
+    (terms1,) = product(received1, FIRST, UNIT, rest - UNIT, 2 * N_X)
     for k, (near, far) in enumerate(((near0, far0), (near1, far1))):
         early = (near.astype(jnp.float32) + far.astype(jnp.float32)).astype(jnp.bfloat16)
         terms1 = lax.dynamic_update_slice(terms1, early, (0, N_X + k, 0, 0))

time: 191 us -> 183 us (0.958)
  Pallas kernels: 53.7 us -> 46.4 us
    ppermute x1, waiting for transfers between devices: 20.8 us -> 0.01 us  [on_device(): far0 = swap(far0)]
    all_to_all x2, waiting for transfers between devices: 20.6 us -> 33.2 us  [exchange(): lax.all_to_all(packed, 'row', split_axis=0, concat_axis=0, tiled=True)]
    pallas_call x6, Pallas kernels: 42.9 us -> 37.4 us  [the longest x4 28 us: ladder(): pl.pallas_call(functools.partial(ladder_kernel, begin, first), in_specs=[...]
    ppermute x1, waiting for transfers between devices: 10.8 us -> 14.4 us  [on_device(): far1 = swap(far1)]
    reduce_scatter x2, waiting for transfers between devices: 48.8 us -> 52.3 us  [scatter(): return lax.psum_scatter(terms, 'z', scatter_dimension=0, tiled=True)]
    unnamed x20 -> x12, local copies, waits for them, and re-layouts: 4.57 us -> 3.24 us
  transfers between devices with their start and end apart: 8 -> 8, of which waited for: 5 -> 6; matrix products, arithmetic and copies ran while one was open for 2% -> 2% of each run, Pallas kernels for 19% -> 17%
where the time goes in v6:
time: 183 us; the launch traced here: 182 us
  waiting for transfers between devices  101 us (55%)
  Pallas kernels  46.4 us (25%)
  starting transfers between devices  13.5 us (7%)
  between operations  13.5 us (7%)
  local copies, waits for them, and re-layouts  5.12 us (3%)
  other arithmetic  2.21 us (1%)
    reduce_scatter x2, waiting for transfers between devices, scatter(): return lax.psum_scatter(terms, 'z', scatter_dimension=0, tiled=True)  52.3 us
    all_to_all x2, waiting for transfers between devices, exchange(): lax.all_to_all(packed, 'row', split_axis=0, concat_axis=0, tiled=True)  33.2 us
    pallas_call x4, Pallas kernels, ladder(): pl.pallas_call(functools.partial(ladder_kernel, begin, first), in_specs=[...  28 us
    ppermute x1, waiting for transfers between devices, on_device(): far1 = swap(far1)  14.4 us
    all_to_all x2, starting transfers between devices, exchange(): lax.all_to_all(packed, 'row', split_axis=0, concat_axis=0, tiled=True)  9.84 us
    pallas_call x2, Pallas kernels, pack(): pl.pallas_call(functools.partial(pack_kernel, first, n_i), in_specs=[hbm]...  9.44 us
    pallas_call x1, Pallas kernels, match(): pl.pallas_call(match_kernel, in_specs=[smem, smem, hbm, hbm], out_specs=[...  6.17 us
  transfers between devices with their start and end apart: 8, of which 6 were waited for; matrix products, arithmetic and copies ran while one was open for 2% of the time, Pallas kernels for 17%

profile of v6, /device:TPU:2, one launch (start us, length us, event | category | flops | bytes accessed | tf_op | source)
XLA Modules:
  0.0 181.9 jit_solution(6228036959140924351)
XLA Ops:
  6.5 5.2 %shard_map.56 = bf16[1536,768]{1,0:T(8,128)(2,1)} custom-call(bf16[12,192,768]{2,1,0:T(8,128)(2,1)} %amp_ref.10), custom_call_target="tpu_custom_call" | custom-call | bytes 7077888 | tf_op jit(solution)/shard_map/pallas_call | solution.py:79
  11.7 6.1 %all-to-all-start = ((bf16[16,96,768]{2,1,0:T(8,128)(2,1)}), bf16[16,96,768]{2,1,0:T(8,128)(2,1)S(1)}, u32[]{:S(2)}, u32[]{:S(2)}) async-start(bf16[16,96,768]{2,1,0:T(8,128)(2,1)} %bitcast.13), calls=%async_computation | async-start | bytes 4718592 | tf_op jit(solution)/shard_map/all_to_all | solution.py:395
  17.9 0.0 reduce-scatter.3.cloned.1.call-start
  17.9 4.2 %shard_map.57 = bf16[768,768]{1,0:T(8,128)(2,1)} custom-call(bf16[12,192,768]{2,1,0:T(8,128)(2,1)} %amp_ref.10), custom_call_target="tpu_custom_call" | custom-call | bytes 7077888 | tf_op jit(solution)/shard_map/pallas_call | solution.py:79
  22.2 6.2 %shard_map.55 = (s32[62]{0:T(128)}, bf16[48,256,256]{2,1,0:T(8,128)(2,1)}) custom-call(s32[6]{0:T(128)} %cd_ref.1, s32[16]{0:T(128)} %ab_ref.1, bf16[768,2048]{1,0:T(8,128)(2,1)} %plus_ref, bf16[768,2048]{1,0:T(8,128)(2,1)} %minus_ref.1), custom_call_target="tpu_custom_call" | custom-call | bytes 12582912 | tf_op jit(solution)/shard_map/pallas_call | solution.py:196
  28.4 22.0 %all-to-all-done = bf16[16,96,768]{2,1,0:T(8,128)(2,1)S(1)} async-done(((bf16[16,96,768]{2,1,0:T(8,128)(2,1)}), bf16[16,96,768]{2,1,0:T(8,128)(2,1)S(1)}, u32[]{:S(2)}, u32[]{:S(2)}) %all-to-all-start) | async-done | bytes 2359328 | tf_op jit(solution)/shard_map/all_to_all | solution.py:395
  50.3 0.6 copy-done.3
  50.9 8.7 %shard_map.58 = bf16[8,2,1152,128]{3,2,1,0:T(8,128)(2,1)} custom-call(s32[1]{0:T(128)} %bitcast.me_ref, s32[62]{0:T(128)S(1)} %copy-done.3, bf16[12,192,768]{2,1,0:T(8,128)(2,1)} %amp_ref.10, bf16[1536,768]{1,0:T(8,128)(2,1)S(1)} %bitcast.9, bf16[48,256,256]{2,1,0:T(8,128)(2,1)} %get-tuple-element.22.weight_ref), custom_call_target="tpu_custom_call" | custom-call | bytes 16515072 | tf_op jit(solution)/shard_map/pallas_call | solution.py:324
  59.6 0.0 reduce-scatter.3.cloned.1.call-update
  59.6 3.7 %all-to-all-start.1 = ((bf16[16,48,768]{2,1,0:T(8,128)(2,1)}), bf16[16,48,768]{2,1,0:T(8,128)(2,1)S(1)}, u32[]{:S(2)}, u32[]{:S(2)}) async-start(bf16[16,48,768]{2,1,0:T(8,128)(2,1)} %bitcast.14), calls=%async_computation.2 | async-start | bytes 2359296 | tf_op jit(solution)/shard_map/all_to_all | solution.py:395
  63.3 0.0 reduce-scatter.5.cloned.1.call-start
  63.4 6.6 %shard_map.60 = (bf16[8,1,384,128]{3,2,1,0:T(8,128)(2,1)S(1)}, bf16[8,1,384,128]{3,2,1,0:T(8,128)(2,1)}) custom-call(s32[1]{0:T(128)} %bitcast.me_ref, s32[62]{0:T(128)S(1)} %copy-done.4, bf16[12,192,768]{2,1,0:T(8,128)(2,1)} %amp_ref.10, bf16[1536,768]{1,0:T(8,128)(2,1)S(1)} %bitcast.10, bf16[48,256,256]{2,1,0:T(8,128)(2,1)} %get-tuple-element.22.weight_ref), custom_call_target="tpu_custom_call" | custom-call | bytes 5505024 | tf_op jit(solution)/shard_map/pallas_call | solution.py:324
  70.0 0.9 copy-done.1
  70.9 1.0 collective-permute-start.1
  71.9 11.3 %all-to-all-done.1 = bf16[16,48,768]{2,1,0:T(8,128)(2,1)S(1)} async-done(((bf16[16,48,768]{2,1,0:T(8,128)(2,1)}), bf16[16,48,768]{2,1,0:T(8,128)(2,1)S(1)}, u32[]{:S(2)}, u32[]{:S(2)}) %all-to-all-start.1) | async-done | bytes 1179680 | tf_op jit(solution)/shard_map/all_to_all | solution.py:395
  83.2 7.1 %shard_map.61 = (bf16[8,1,384,128]{3,2,1,0:T(8,128)(2,1)S(1)}, bf16[8,1,384,128]{3,2,1,0:T(8,128)(2,1)S(1)}) custom-call(s32[1]{0:T(128)} %bitcast.me_ref, s32[62]{0:T(128)S(1)} %copy-done.4, bf16[12,192,768]{2,1,0:T(8,128)(2,1)} %amp_ref.10, bf16[768,768]{1,0:T(8,128)(2,1)S(1)} %bitcast.11, bf16[48,256,256]{2,1,0:T(8,128)(2,1)} %get-tuple-element.22.weight_ref), custom_call_target="tpu_custom_call" | custom-call | bytes 5505024 | tf_op jit(solution)/shard_map/pallas_call | solution.py:324
  90.3 1.2 collective-permute-start.2
  91.5 5.6 %shard_map.62 = bf16[8,4,384,128]{3,2,1,0:T(8,128)(2,1)} custom-call(s32[1]{0:T(128)} %bitcast.me_ref, s32[62]{0:T(128)S(1)} %copy-done.4, bf16[12,192,768]{2,1,0:T(8,128)(2,1)} %amp_ref.10, bf16[768,768]{1,0:T(8,128)(2,1)S(1)} %bitcast.12, bf16[48,256,256]{2,1,0:T(8,128)(2,1)} %get-tuple-element.22.weight_ref), custom_call_target="tpu_custom_call" | custom-call | bytes 5505024 | tf_op jit(solution)/shard_map/pallas_call | solution.py:324
  97.2 1.1 fusion
  98.3 14.4 %collective-permute-done.2 = bf16[8,1,384,128]{3,2,1,0:T(8,128)(2,1)S(1)} collective-permute-done((bf16[8,1,384,128]{3,2,1,0:T(8,128)(2,1)S(1)}, bf16[8,1,384,128]{3,2,1,0:T(8,128)(2,1)S(1)}, u32[]{:S(2)}, u32[]{:S(2)}) %collective-permute-start.2) | collective-permute-done | bytes 786464 | tf_op jit(solution)/shard_map/ppermute | solution.py:431
  112.7 1.1 fusion.1
  113.8 6.0 %reduce-scatter.3.cloned.1.call-done.near = bf16[1,2,1152,128]{3,2,1,0:T(8,128)(2,1)} async-done(((bf16[8,2,1152,128]{3,2,1,0:T(8,128)(2,1)}), bf16[1,2,1152,128]{3,2,1,0:T(8,128)(2,1)}) %reduce-scatter.3.cloned.1.call-update) | async-done | bytes 589840 | tf_op jit(solution)/shard_map/reduce_scatter | solution.py:398
  119.8 1.0 slice_bitcast_fusion
  120.7 0.6 collective-permute-start
  121.4 46.3 %reduce-scatter.5.cloned.1.call-done.refs_0_.refs_2_ = bf16[1,4,384,128]{3,2,1,0:T(8,128)(2,1)} async-done(((bf16[8,4,384,128]{3,2,1,0:T(8,128)(2,1)}), bf16[1,4,384,128]{3,2,1,0:T(8,128)(2,1)}) %reduce-scatter.5.cloned.1.call-update) | async-done | bytes 393232 | tf_op jit(solution)/shard_map/reduce_scatter | solution.py:398
  167.7 0.9 slice_bitcast_fusion.1
  168.6 0.7 collective-permute-start.3
  169.3 0.7 copy-done.5
  170.0 1.9 %shard_map.59.done_ref = bf16[128,2304]{1,0:T(8,128)(2,1)} custom-call(bf16[1,2,1152,128]{3,2,1,0:T(8,128)(2,1)} %reduce-scatter.3.cloned.1.call-done.near, bf16[1152,128]{1,0:T(8,128)(2,1)} %copy-done.5), custom_call_target="tpu_custom_call" | custom-call | tf_op jit(solution)/shard_map/pallas_call | solution.py:361
  171.9 1.2 collective-permute-done.3.refs_1_
  173.2 1.0 copy-done
  174.2 0.9 shard_map.63
  (11 shorter events, 0.0 us)
Async XLA Ops:
  11.7 38.6 %all-to-all-start = ((bf16[16,96,768]{2,1,0:T(8,128)(2,1)}), bf16[16,96,768]{2,1,0:T(8,128)(2,1)S(1)}, u32[]{:S(2)}, u32[]{:S(2)}) async-start(bf16[16,96,768]{2,1,0:T(8,128)(2,1)} %bitcast.13), calls=%async_computation | async-start | bytes 4718592 | tf_op jit(solution)/shard_map/all_to_all | solution.py:395
  17.9 101.9 %reduce-scatter.3.cloned.1.call-start = ((), (), s32[]{:S(2)}) async-start(), calls=%async_computation.4 | async-start | bytes 5308416 | tf_op jit(solution)/shard_map/reduce_scatter | solution.py:398
  50.3 0.6 copy-start.3
  59.6 3.8 %copy-start.4 = (s32[62]{0:T(128)S(1)}, s32[62]{0:T(128)}, u32[]{:S(2)}) copy-start(s32[62]{0:T(128)} %get-tuple-element.18.lists) | copy-start | bytes 748
  59.6 23.6 %all-to-all-start.1 = ((bf16[16,48,768]{2,1,0:T(8,128)(2,1)}), bf16[16,48,768]{2,1,0:T(8,128)(2,1)S(1)}, u32[]{:S(2)}, u32[]{:S(2)}) async-start(bf16[16,48,768]{2,1,0:T(8,128)(2,1)} %bitcast.14), calls=%async_computation.2 | async-start | bytes 2359296 | tf_op jit(solution)/shard_map/all_to_all | solution.py:395
  63.3 104.3 %reduce-scatter.5.cloned.1.call-start = ((), (), s32[]{:S(2)}) async-start(), calls=%async_computation.5 | async-start | bytes 3538944 | tf_op jit(solution)/shard_map/reduce_scatter | solution.py:398
  70.0 0.9 copy-start.1
  70.9 26.2 %collective-permute-start.1 = (bf16[8,1,384,128]{3,2,1,0:T(8,128)(2,1)}, bf16[8,1,384,128]{3,2,1,0:T(8,128)(2,1)S(1)}, u32[]{:S(2)}, u32[]{:S(2)}) collective-permute-start(bf16[8,1,384,128]{3,2,1,0:T(8,128)(2,1)} %get-tuple-element.29), channel_id=1, source_target_pairs={{0,1},{1,0},{2,3},{3,2},{4,5},{5,4},{6,7},{7,6},{8,9},{9,8},{10,11... | collective-permute-start | bytes 2359304 | tf_op jit(solution)/shard_map/ppermute | solution.py:428
  90.3 22.4 %collective-permute-start.2 = (bf16[8,1,384,128]{3,2,1,0:T(8,128)(2,1)S(1)}, bf16[8,1,384,128]{3,2,1,0:T(8,128)(2,1)S(1)}, u32[]{:S(2)}, u32[]{:S(2)}) collective-permute-start(bf16[8,1,384,128]{3,2,1,0:T(8,128)(2,1)S(1)} %get-tuple-element.30), channel_id=1, source_target_pairs={{0,1},{1,0},{2,3},{3,2},{4,5},{5,4},{6,7},{7,6},{8,9},{9,8},{10,11... | collective-permute-start | bytes 2359304 | tf_op jit(solution)/shard_map/ppermute | solution.py:431
  91.5 5.6 %copy-start.2 = (bf16[8,1,384,128]{3,2,1,0:T(8,128)(2,1)S(1)}, bf16[8,1,384,128]{3,2,1,0:T(8,128)(2,1)}, u32[]{:S(2)}) copy-start(bf16[8,1,384,128]{3,2,1,0:T(8,128)(2,1)} %copy-done.1) | copy-start | bytes 2359300
  120.7 48.5 %collective-permute-start = (bf16[1152,128]{1,0:T(8,128)(2,1)S(1)}, bf16[1152,128]{1,0:T(8,128)(2,1)S(1)}, u32[]{:S(2)}, u32[]{:S(2)}) collective-permute-start(bf16[1152,128]{1,0:T(8,128)(2,1)S(1)} %slice_bitcast_fusion), channel_id=1, source_target_pairs={{0,1},{1,0},{2,3},{3,2},{4,5},{5,4},{6,7},{7,6},{8,9},{9,8},{10,11... | collective-permute-start | bytes 884744 | tf_op jit(solution)/shard_map/ppermute | solution.py:438
  168.6 4.6 %collective-permute-start.3 = (bf16[384,128]{1,0:T(8,128)(2,1)S(1)}, bf16[384,128]{1,0:T(8,128)(2,1)S(1)}, u32[]{:S(2)}, u32[]{:S(2)}) collective-permute-start(bf16[384,128]{1,0:T(8,128)(2,1)S(1)} %slice_bitcast_fusion.1), channel_id=1, source_target_pairs={{0,1},{1,0},{2,3},{3,2},{4,5},{5,4},{6,7},{7,6},{8,9},{9,8},{10,11... | collective-permute-start | bytes 294920 | tf_op jit(solution)/shard_map/ppermute | solution.py:439
  169.3 0.7 copy-start.5
  173.2 1.0 copy-start
Sparse Core Ops, SparseCore 0:
  59.7 59.9 reduce-scatter.2
  122.3 45.3 reduce-scatter.4

commit v7 on v6

--- a/solution.py
+++ b/solution.py
@@ -16,7 +16,7 @@
 BUNDLE = 4
 AHEAD = 2
 FIRST = 8
-UNIT = 2
+EARLY = (3, 2)
 
 
 def params(mib=60):
@@ -39,9 +39,9 @@
     return (i * N_S + s) * rows + first + jl
 
 
-def receive_order(rows, count, first, n_i):
+def receive_order(rows, n_i):
     i, s, jl = digits(n_i * N_S * rows, rows, N_S)
-    return (s * count + first + i) * rows + jl
+    return (s * n_i + i) * rows + jl
 
 
 def pack_kernel(first, n_i, amp_ref, out_ref, held, sent, in_sem, out_sem):
@@ -214,20 +214,19 @@
     )(cd_irrep, ab_irrep, plus, minus)
 
 
-def ladder_kernel(begin_i, first, me_ref, lists, amp_ref, got_ref, weight_ref, *refs):
-    n_out = len(refs) - 8
-    out_refs = refs[:n_out]
-    own, got, weights, both, staged, load_sem, weight_sem, out_sem = refs[n_out:]
+def ladder_kernel(begin_i, parts, me_ref, lists, amp_ref, got_ref, weight_ref, *refs):
+    terms, near, far, own, got, weights, both, staged, load_sem, weight_sem, out_sem = refs
+    late, early = parts
     n_i, occ, width = own.shape
     kt = width // TILE
-    tiles, per = staged.shape[:2]
+    tiles = staged.shape[0]
     rows = n_i * occ
     me = me_ref[0]
     there = 2 * N_IRREP
     first_step = there + 2 * kt + 2
     bundles, steps = lists[first_step - 2], lists[first_step - 1]
     loads = [
-        pltpu.make_async_copy(amp_ref.at[begin_i + first : begin_i + first + n_i], own, load_sem.at[0]),
+        pltpu.make_async_copy(amp_ref.at[begin_i : begin_i + n_i], own, load_sem.at[0]),
         pltpu.make_async_copy(got_ref, got, load_sem.at[1]),
     ]
     for copy in loads:
@@ -245,7 +244,7 @@
     piece = N_S * local
     span = n_i * piece
     received = got.shape[0] * piece // occ
-    order = picker(receive_order(local, received // piece, first, n_i), received)
+    order = picker(receive_order(local, n_i), received)
     for copy in loads:
         copy.wait()
     for q in range(occ // piece):
@@ -259,19 +258,17 @@
                 lanes = pl.ds(pl.multiple_of(lists[there + p] * PAIR + half * TILE, TILE), TILE)
                 both[:, q * piece : (q + 1) * piece, lanes] = value[:, :, p * TILE : (p + 1) * TILE]
 
-    def out_copy(q, dst):
-        return pltpu.make_async_copy(staged.at[q], dst, out_sem)
-
     def start(q):
         z, w = q // N_X, (q % N_X) ^ me
-        if n_out == 1:
-            out_copy(q, out_refs[0].at[z, pl.ds(w * per, per)]).start()
-        else:
-            for k in range(N_X):
-
-                @pl.when(w == k)
-                def _():
-                    out_copy(q, out_refs[k].at[z]).start()
+        per = late.stop - late.start
+        pltpu.make_async_copy(
+            staged.at[q, late], terms.at[z, pl.ds(w * per, per)], out_sem
+        ).start()
+        for k, ref in enumerate((near, far)):
+
+            @pl.when(w == k)
+            def _():
+                pltpu.make_async_copy(staged.at[q, early], ref.at[z], out_sem).start()
 
     @pl.loop(0, bundles)
     def _(k):
@@ -308,82 +305,104 @@
     pltpu.make_async_copy(staged, staged, out_sem).wait()
 
 
-def ladder(me, lists, amplitudes, received, weights, begin, first, n_i, n_z, per, slots):
+def ladder(me, lists, amplitudes, received, weights, begin, n_i, n_z, late, early, slots):
     _, occ, width = amplitudes.shape
-    rows = n_i * occ
     tiles = n_z * N_X
     blocks = weights.shape[0]
-    if slots:
-        shapes = [(n_z, slots, rows // per, TILE)]
-    else:
-        shapes = [(n_z, per, rows // per, TILE)] * N_X
+    apart = (n_z, early.stop - early.start, occ, TILE)
     smem = pl.BlockSpec(memory_space=pltpu.SMEM)
     hbm = pl.BlockSpec(memory_space=pl.ANY)
     dma = pltpu.SemaphoreType.DMA
     bf16 = jnp.bfloat16
     return pl.pallas_call(
-        functools.partial(ladder_kernel, begin, first),
+        functools.partial(ladder_kernel, begin, (late, early)),
         in_specs=[smem, smem, hbm, hbm, hbm],
-        out_specs=[hbm] * len(shapes),
-        out_shape=[jax.ShapeDtypeStruct(s, bf16) for s in shapes],
+        out_specs=[hbm] * 3,
+        out_shape=[
+            jax.ShapeDtypeStruct(s, bf16) for s in ((n_z, slots, occ, TILE), apart, apart)
+        ],
         scratch_shapes=[
             pltpu.VMEM((n_i, occ, width), bf16),
             pltpu.VMEM(received.shape, bf16),
             pltpu.VMEM(weights.shape, bf16),
             pltpu.VMEM((n_i, occ, 2 * width), bf16),
-            pltpu.VMEM((tiles, per, rows // per, TILE), bf16),
+            pltpu.VMEM((tiles, n_i, occ, TILE), bf16),
             dma((2,)),
             dma((blocks // BUNDLE,)),
             dma,
         ],
-        compiler_params=params(50),
+        compiler_params=params(48),
         cost_estimate=pl.CostEstimate(
-            flops=0, bytes_accessed=8 * rows * (width + n_z * TILE), transcendentals=0
+            flops=0, bytes_accessed=8 * n_i * occ * (width + n_z * TILE), transcendentals=0
         ),
     )(me, lists, amplitudes, received, weights)
 
 
-def finish_kernel(near, far, *refs):
-    out_ref = refs[-1]
-    total = near[...].astype(jnp.float32).reshape(-1, TILE) + far[...].astype(jnp.float32)
-    if len(refs) > 1:
-        early = refs[0][...].astype(jnp.float32).reshape(-1, TILE)
-        total = jnp.concatenate([early, total], 0)
-    out_ref[...] = total.T.astype(out_ref.dtype)
+def total(*refs):
+    terms = [ref[...].astype(jnp.float32).reshape(-1, TILE) for ref in refs]
+    return functools.reduce(jnp.add, terms)
 
 
 def slots(ref, count, k):
     return pl.BlockSpec((1, count) + ref.shape[2:], lambda g: (0, k, 0, 0))
 
 
-def finish_first(near, far):
-    rows = far.shape[0]
+def finish_first(near, far, n_i, n_all):
+    occ = near.shape[2]
+    rows = n_i * occ
+
+    def kernel(near_ref, far_ref, out_ref):
+        out_ref[...] = total(near_ref, far_ref).T.astype(out_ref.dtype)
+
     return pl.pallas_call(
-        finish_kernel,
+        kernel,
         grid=(1,),
-        in_specs=[slots(near, 1, 0), pl.BlockSpec(far.shape, lambda g: (0, 0))],
+        in_specs=[slots(near, n_i, 0), pl.BlockSpec((rows, TILE), lambda g: (0, 0))],
         out_specs=pl.BlockSpec((TILE, rows), lambda g: (0, 0)),
-        out_shape=jax.ShapeDtypeStruct((TILE, 2 * rows), jnp.bfloat16),
+        out_shape=jax.ShapeDtypeStruct((TILE, n_all * occ), jnp.bfloat16),
         compiler_params=params(57),
     )(near, far)
 
 
-def finish_last(done, sum1, far):
-    early = sum1.shape[1] - N_X
+def finish_last(done, n_done, sum0, far0, sum1, far1):
+    occ = sum1.shape[2]
+    late = far1.shape[0] // occ
+    left = far0.shape[0] // occ - n_done
+    begin = n_done * occ
+    whole = pl.BlockSpec(memory_space=pltpu.VMEM)
+    hbm = pl.BlockSpec(memory_space=pl.ANY)
+
+    def kernel(done_ref, near0_ref, far0_ref, sum1_ref, far1_ref, out_ref, held, sem):
+        summed = sum1_ref[0].astype(jnp.float32)
+        parts = [
+            total(near0_ref, far0_ref),
+            summed[N_X * late :].reshape(-1, TILE),
+            summed[:late].reshape(-1, TILE) + far1_ref[...].astype(jnp.float32),
+        ]
+        held[...] = jnp.concatenate(parts, 0).T.astype(held.dtype)
+        copy = pltpu.make_async_copy(held, out_ref.at[:, begin:], sem)
+        copy.start()
+        copy.wait()
+
     return pl.pallas_call(
-        lambda done_ref, *refs: finish_kernel(*refs),
+        kernel,
         grid=(1,),
         in_specs=[
-            pl.BlockSpec(memory_space=pl.ANY),
-            slots(sum1, 1, 0),
-            pl.BlockSpec(far.shape, lambda g: (0, 0)),
-            slots(sum1, early, N_X // early),
-        ],
-        out_specs=pl.BlockSpec((TILE, done.shape[1] // 2), lambda g: (0, 1)),
+            hbm,
+            slots(sum0, left, n_done // left),
+            pl.BlockSpec((left * occ, TILE), lambda g: (n_done // left, 0)),
+            whole,
+            whole,
+        ],
+        out_specs=hbm,
         out_shape=jax.ShapeDtypeStruct(done.shape, jnp.bfloat16),
+        scratch_shapes=[
+            pltpu.VMEM((TILE, done.shape[1] - begin), jnp.bfloat16),
+            pltpu.SemaphoreType.DMA,
+        ],
         input_output_aliases={0: 0},
-        compiler_params=params(16),
-    )(done, sum1, far, sum1)
+        compiler_params=params(57),
+    )(done, sum0, far0, sum1, far1)
 
 
 def on_device(amplitudes, plus, minus, cd_irrep, ab_irrep):
@@ -397,19 +416,10 @@
     def scatter(terms):
         return lax.psum_scatter(terms, "z", scatter_dimension=0, tiled=True)
 
-    def product(received, begin, first, n_i, slots):
+    def product(received, begin, n_i, late, early, slots):
+        n_z = plus.shape[1] // PAIR
         return ladder(
-            me,
-            lists,
-            amplitudes,
-            received,
-            weights,
-            begin,
-            first,
-            n_i,
-            plus.shape[1] // PAIR,
-            1,
-            slots,
+            me, lists, amplitudes, received, weights, begin, n_i, n_z, late, early, slots
         )
 
     rest = rows - FIRST
@@ -421,22 +431,28 @@
     lists, weights = match(cd_irrep, ab_irrep, first_plus, minus)
     received0, packed1, weights = lax.optimization_barrier((received0, packed1, weights))
     received1 = exchange(packed1)
-    (terms0,) = product(received0, 0, 0, FIRST - UNIT, N_X)
+    n0, n1 = FIRST - EARLY[0], rest - EARLY[1]
+    terms0, near0, far0 = product(
+        received0, 0, FIRST, slice(0, n0), slice(n0, FIRST), N_X * n0
+    )
     sum0 = scatter(terms0)
-    received0, _ = lax.optimization_barrier((received0, terms0))
-    near0, far0 = product(received0, 0, FIRST - UNIT, UNIT, 0)
     far0 = swap(far0)
     received1, _ = lax.optimization_barrier((received1, near0))
-    near1, far1 = product(received1, FIRST, 0, UNIT, 0)
+    terms1, near1, far1 = product(
+        received1, FIRST, rest, slice(EARLY[1], rest), slice(0, EARLY[1]), N_X * n1 + sum(EARLY)
+    )
     far1 = swap(far1)
-    received1, _ = lax.optimization_barrier((received1, near1))
-    (terms1,) = product(received1, FIRST, UNIT, rest - UNIT, 2 * N_X)
-    for k, (near, far) in enumerate(((near0, far0), (near1, far1))):
+    at = N_X * n1
+    for near, far in ((near0, far0), (near1, far1)):
         early = (near.astype(jnp.float32) + far.astype(jnp.float32)).astype(jnp.bfloat16)
-        terms1 = lax.dynamic_update_slice(terms1, early, (0, N_X + k, 0, 0))
+        terms1 = lax.dynamic_update_slice(terms1, early, (0, at, 0, 0))
+        at += near.shape[1]
     sum1 = scatter(terms1)
-    done = finish_first(sum0, swap(sum0[0, 1]))
-    return finish_last(done, sum1, swap(sum1[0, 1]))
+    last0 = swap(sum0[0, n0:].reshape(-1, TILE))
+    n_done = n0 // 2 * 2
+    done = finish_first(sum0, last0, n_done, rows)
+    last1 = swap(sum1[0, n1 : N_X * n1].reshape(-1, TILE))
+    return finish_last(done, n_done, sum0, last0, sum1, last1)
 
 
 def solution(mesh):

time: 183 us -> 196 us (1.071)
  waiting for transfers between devices: 101 us -> 119 us
  Pallas kernels: 46.4 us -> 41 us
    ppermute x1, waiting for transfers between devices: 0.01 us -> 11.4 us  [on_device(): far0 = swap(far0)]
    all_to_all x2, waiting for transfers between devices: 33.2 us -> 40.4 us  [exchange(): lax.all_to_all(packed, 'row', split_axis=0, concat_axis=0, tiled=True)]
    pallas_call x6 -> x4, Pallas kernels: 30.8 us -> 25.4 us  [the longest x2 21.5 us: ladder(): pl.pallas_call(functools.partial(ladder_kernel, begin, (late, early)), in...]
  transfers between devices with their start and end apart: 8 -> 8, of which waited for: 6 -> 6; matrix products, arithmetic and copies ran while one was open for 2% -> 3% of each run, Pallas kernels for 17% -> 11%
where the time goes in v7:
time: 196 us
  waiting for transfers between devices  119 us (61%)
  Pallas kernels  41 us (21%)
  starting transfers between devices  13.9 us (7%)
  between operations  13.5 us (7%)
  local copies, waits for them, and re-layouts  4.9 us (3%)
  other arithmetic  3.81 us (2%)
    reduce_scatter x2, waiting for transfers between devices, scatter(): return lax.psum_scatter(terms, 'z', scatter_dimension=0, tiled=True)  51.4 us
    all_to_all x2, waiting for transfers between devices, exchange(): lax.all_to_all(packed, 'row', split_axis=0, concat_axis=0, tiled=True)  40.4 us
    pallas_call x2, Pallas kernels, ladder(): pl.pallas_call(functools.partial(ladder_kernel, begin, (late, early)), in...  21.5 us
    ppermute x1, waiting for transfers between devices, on_device(): far1 = swap(far1)  13.8 us
    ppermute x1, waiting for transfers between devices, on_device(): far0 = swap(far0)  11.4 us
    all_to_all x2, starting transfers between devices, exchange(): lax.all_to_all(packed, 'row', split_axis=0, concat_axis=0, tiled=True)  9.97 us
    pallas_call x2, Pallas kernels, pack(): pl.pallas_call(functools.partial(pack_kernel, first, n_i), in_specs=[hbm]...  9.44 us
    pallas_call x1, Pallas kernels, match(): pl.pallas_call(match_kernel, in_specs=[smem, smem, hbm, hbm], out_specs=[...  6.13 us
  transfers between devices with their start and end apart: 8, of which 6 were waited for; matrix products, arithmetic and copies ran while one was open for 3% of the time, Pallas kernels for 11%

profile of v7, /device:TPU:2, one launch (start us, length us, event | category | flops | bytes accessed | tf_op | source)
XLA Modules:
  0.0 195.7 jit_solution(16501104369530301024)
XLA Ops:
  6.5 5.2 %shard_map.56 = bf16[1536,768]{1,0:T(8,128)(2,1)} custom-call(bf16[12,192,768]{2,1,0:T(8,128)(2,1)} %amp_ref.6), custom_call_target="tpu_custom_call" | custom-call | bytes 7077888 | tf_op jit(solution)/shard_map/pallas_call | solution.py:79
  11.7 6.1 %all-to-all-start = ((bf16[16,96,768]{2,1,0:T(8,128)(2,1)}), bf16[16,96,768]{2,1,0:T(8,128)(2,1)S(1)}, u32[]{:S(2)}, u32[]{:S(2)}) async-start(bf16[16,96,768]{2,1,0:T(8,128)(2,1)} %bitcast.9), calls=%async_computation | async-start | bytes 4718592 | tf_op jit(solution)/shard_map/all_to_all | solution.py:414
  17.9 0.0 reduce-scatter.3.cloned.1.call-start
  17.9 4.2 %shard_map.57 = bf16[768,768]{1,0:T(8,128)(2,1)} custom-call(bf16[12,192,768]{2,1,0:T(8,128)(2,1)} %amp_ref.6), custom_call_target="tpu_custom_call" | custom-call | bytes 7077888 | tf_op jit(solution)/shard_map/pallas_call | solution.py:79
  22.2 6.1 %shard_map.55 = (s32[62]{0:T(128)}, bf16[48,256,256]{2,1,0:T(8,128)(2,1)}) custom-call(s32[6]{0:T(128)} %cd_ref.1, s32[16]{0:T(128)} %ab_ref.1, bf16[768,2048]{1,0:T(8,128)(2,1)} %plus_ref, bf16[768,2048]{1,0:T(8,128)(2,1)} %minus_ref.1), custom_call_target="tpu_custom_call" | custom-call | bytes 12582912 | tf_op jit(solution)/shard_map/pallas_call | solution.py:196
  28.3 22.0 %all-to-all-done = bf16[16,96,768]{2,1,0:T(8,128)(2,1)S(1)} async-done(((bf16[16,96,768]{2,1,0:T(8,128)(2,1)}), bf16[16,96,768]{2,1,0:T(8,128)(2,1)S(1)}, u32[]{:S(2)}, u32[]{:S(2)}) %all-to-all-start) | async-done | bytes 2359328 | tf_op jit(solution)/shard_map/all_to_all | solution.py:414
  50.3 0.7 copy-done
  51.0 12.9 %shard_map.58 = (bf16[8,10,192,128]{3,2,1,0:T(8,128)(2,1)}, bf16[8,3,192,128]{3,2,1,0:T(8,128)(2,1)S(1)}, bf16[8,3,192,128]{3,2,1,0:T(8,128)(2,1)S(1)}) custom-call(s32[1]{0:T(128)} %bitcast.me_ref, s32[62]{0:T(128)S(1)} %copy-done, bf16[12,192,768]{2,1,0:T(8,128)(2,1)} %amp_ref.6, bf16[1536,768]{1,0:T(8,128)(2,1)S(1)} %bitcast.7, ...), custom_call_target="tpu_custom_call" | custom-call | bytes 22020096 | tf_op jit(solution)/shard_map/pallas_call | solution.py:317
  63.9 1.0 copy-done.2
  65.0 0.0 reduce-scatter.3.cloned.1.call-update
  65.0 3.8 %all-to-all-start.1 = ((bf16[16,48,768]{2,1,0:T(8,128)(2,1)}), bf16[16,48,768]{2,1,0:T(8,128)(2,1)S(1)}, u32[]{:S(2)}, u32[]{:S(2)}) async-start(bf16[16,48,768]{2,1,0:T(8,128)(2,1)} %bitcast.10), calls=%async_computation.2 | async-start | bytes 2359296 | tf_op jit(solution)/shard_map/all_to_all | solution.py:414
  68.8 0.0 reduce-scatter.5.cloned.1.call-start
  68.9 1.4 collective-permute-start.1
  70.3 18.4 %all-to-all-done.1 = bf16[16,48,768]{2,1,0:T(8,128)(2,1)S(1)} async-done(((bf16[16,48,768]{2,1,0:T(8,128)(2,1)}), bf16[16,48,768]{2,1,0:T(8,128)(2,1)S(1)}, u32[]{:S(2)}, u32[]{:S(2)}) %all-to-all-start.1) | async-done | bytes 1179680 | tf_op jit(solution)/shard_map/all_to_all | solution.py:414
  88.7 8.6 %shard_map.60 = (bf16[8,9,192,128]{3,2,1,0:T(8,128)(2,1)}, bf16[8,2,192,128]{3,2,1,0:T(8,128)(2,1)S(1)}, bf16[8,2,192,128]{3,2,1,0:T(8,128)(2,1)S(1)}) custom-call(s32[1]{0:T(128)} %bitcast.me_ref, s32[62]{0:T(128)S(1)} %copy-done.1, bf16[12,192,768]{2,1,0:T(8,128)(2,1)} %amp_ref.6, bf16[768,768]{1,0:T(8,128)(2,1)S(1)} %bitcast.8, ...), custom_call_target="tpu_custom_call" | custom-call | bytes 11010048 | tf_op jit(solution)/shard_map/pallas_call | solution.py:317
  97.3 1.6 collective-permute-start.2
  98.9 11.4 %collective-permute-done.1 = bf16[8,3,192,128]{3,2,1,0:T(8,128)(2,1)} collective-permute-done((bf16[8,3,192,128]{3,2,1,0:T(8,128)(2,1)S(1)}, bf16[8,3,192,128]{3,2,1,0:T(8,128)(2,1)}, u32[]{:S(2)}, u32[]{:S(2)}) %collective-permute-start.1) | collective-permute-done | bytes 1179680 | tf_op jit(solution)/shard_map/ppermute | solution.py:439
  110.3 2.7 %fusion = bf16[8,9,192,128]{3,2,1,0:T(8,128)(2,1)} fusion(bf16[8,9,192,128]{3,2,1,0:T(8,128)(2,1)} %get-tuple-element.27, bf16[8,3,192,128]{3,2,1,0:T(8,128)(2,1)} %collective-permute-done.1, bf16[8,3,192,128]{3,2,1,0:T(8,128)(2,1)S(1)} %get-tuple-element.25), kind=kLoop, calls=%fused_computation.2 | loop fusion | flops 2359296 | bytes 3538944 | tf_op jit(solution)/shard_map/dynamic_update_slice | solution.py:448
  113.0 13.8 %collective-permute-done.2 = bf16[8,2,192,128]{3,2,1,0:T(8,128)(2,1)S(1)} collective-permute-done((bf16[8,2,192,128]{3,2,1,0:T(8,128)(2,1)S(1)}, bf16[8,2,192,128]{3,2,1,0:T(8,128)(2,1)S(1)}, u32[]{:S(2)}, u32[]{:S(2)}) %collective-permute-start.2) | collective-permute-done | bytes 786464 | tf_op jit(solution)/shard_map/ppermute | solution.py:444
  126.7 1.1 fusion.1
  127.9 0.0 reduce-scatter.5.cloned.1.call-update
  127.9 0.0 reduce-scatter.3.cloned.1.call-done.near_ref.near0_ref
  127.9 1.0 slice.8
  128.9 0.3 collective-permute-start
  129.2 51.4 %reduce-scatter.5.cloned.1.call-done.sum1_ref = bf16[1,9,192,128]{3,2,1,0:T(8,128)(2,1)} async-done(((bf16[8,9,192,128]{3,2,1,0:T(8,128)(2,1)}), bf16[1,9,192,128]{3,2,1,0:T(8,128)(2,1)}) %reduce-scatter.5.cloned.1.call-update) | async-done | bytes 442384 | tf_op jit(solution)/shard_map/reduce_scatter | solution.py:417
  180.6 0.9 slice.9
  181.5 0.6 collective-permute-start.3
  182.1 0.7 copy-done.4
  182.8 1.8 shard_map.59.done_ref
  184.6 1.5 collective-permute-done.3.far1_ref
  186.1 0.6 copy-done.5
  186.8 2.0 %shard_map.61 = bf16[128,2304]{1,0:T(8,128)(2,1)} custom-call(bf16[128,2304]{1,0:T(8,128)(2,1)} %shard_map.59.done_ref, bf16[1,10,192,128]{3,2,1,0:T(8,128)(2,1)} %reduce-scatter.3.cloned.1.call-done.near_ref.near0_ref, bf16[960,128]{1,0:T(8,128)(2,1)} %copy-done.4, ...), custom_call_target="tpu_custom_call", output_to_operand_aliasing={{}: (0, {})} | custom-call | tf_op jit(solution)/shard_map/pallas_call | solution.py:387
  (9 shorter events, 0.0 us)
Async XLA Ops:
  11.7 38.6 %all-to-all-start = ((bf16[16,96,768]{2,1,0:T(8,128)(2,1)}), bf16[16,96,768]{2,1,0:T(8,128)(2,1)S(1)}, u32[]{:S(2)}, u32[]{:S(2)}) async-start(bf16[16,96,768]{2,1,0:T(8,128)(2,1)} %bitcast.9), calls=%async_computation | async-start | bytes 4718592 | tf_op jit(solution)/shard_map/all_to_all | solution.py:414
  17.9 110.0 %reduce-scatter.3.cloned.1.call-start = ((), (), s32[]{:S(2)}) async-start(), calls=%async_computation.4 | async-start | bytes 4423680 | tf_op jit(solution)/shard_map/reduce_scatter | solution.py:417
  50.3 0.7 copy-start
  63.9 1.0 copy-start.2
  64.9 3.9 %copy-start.3 = (bf16[8,3,192,128]{3,2,1,0:T(8,128)(2,1)S(1)}, bf16[8,3,192,128]{3,2,1,0:T(8,128)(2,1)}, u32[]{:S(2)}) copy-start(bf16[8,3,192,128]{3,2,1,0:T(8,128)(2,1)} %copy-done.2) | copy-start | bytes 3538948
  65.0 23.7 %copy-start.1 = (s32[62]{0:T(128)S(1)}, s32[62]{0:T(128)}, u32[]{:S(2)}) copy-start(s32[62]{0:T(128)} %get-tuple-element.18.lists) | copy-start | bytes 748
  65.0 23.7 %all-to-all-start.1 = ((bf16[16,48,768]{2,1,0:T(8,128)(2,1)}), bf16[16,48,768]{2,1,0:T(8,128)(2,1)S(1)}, u32[]{:S(2)}, u32[]{:S(2)}) async-start(bf16[16,48,768]{2,1,0:T(8,128)(2,1)} %bitcast.10), calls=%async_computation.2 | async-start | bytes 2359296 | tf_op jit(solution)/shard_map/all_to_all | solution.py:414
  68.8 111.8 %reduce-scatter.5.cloned.1.call-start = ((), (), s32[]{:S(2)}) async-start(), calls=%async_computation.5 | async-start | bytes 3981312 | tf_op jit(solution)/shard_map/reduce_scatter | solution.py:417
  68.9 41.4 %collective-permute-start.1 = (bf16[8,3,192,128]{3,2,1,0:T(8,128)(2,1)S(1)}, bf16[8,3,192,128]{3,2,1,0:T(8,128)(2,1)}, u32[]{:S(2)}, u32[]{:S(2)}) collective-permute-start(bf16[8,3,192,128]{3,2,1,0:T(8,128)(2,1)S(1)} %copy-done.3), channel_id=1, source_target_pairs={{0,1},{1,0},{2,3},{3,2},{4,5},{5,4},{6,7},{7,6},{8,9},{9,8},{10,11... | collective-permute-start | bytes 3538952 | tf_op jit(solution)/shard_map/ppermute | solution.py:439
  97.3 29.4 %collective-permute-start.2 = (bf16[8,2,192,128]{3,2,1,0:T(8,128)(2,1)S(1)}, bf16[8,2,192,128]{3,2,1,0:T(8,128)(2,1)S(1)}, u32[]{:S(2)}, u32[]{:S(2)}) collective-permute-start(bf16[8,2,192,128]{3,2,1,0:T(8,128)(2,1)S(1)} %get-tuple-element.30), channel_id=1, source_target_pairs={{0,1},{1,0},{2,3},{3,2},{4,5},{5,4},{6,7},{7,6},{8,9},{9,8},{10,11... | collective-permute-start | bytes 2359304 | tf_op jit(solution)/shard_map/ppermute | solution.py:444
  128.9 53.2 %collective-permute-start = (bf16[960,128]{1,0:T(8,128)(2,1)S(1)}, bf16[960,128]{1,0:T(8,128)(2,1)S(1)}, u32[]{:S(2)}, u32[]{:S(2)}) collective-permute-start(bf16[960,128]{1,0:T(8,128)(2,1)S(1)} %bitcast.11), channel_id=1, source_target_pairs={{0,1},{1,0},{2,3},{3,2},{4,5},{5,4},{6,7},{7,6},{8,9},{9,8},{10,11... | collective-permute-start | bytes 737288 | tf_op jit(solution)/shard_map/ppermute | solution.py:451
  181.5 4.6 %collective-permute-start.3 = (bf16[384,128]{1,0:T(8,128)(2,1)S(1)}, bf16[384,128]{1,0:T(8,128)(2,1)S(1)}, u32[]{:S(2)}, u32[]{:S(2)}) collective-permute-start(bf16[384,128]{1,0:T(8,128)(2,1)S(1)} %bitcast.12), channel_id=1, source_target_pairs={{0,1},{1,0},{2,3},{3,2},{4,5},{5,4},{6,7},{7,6},{8,9},{9,8},{10,11... | collective-permute-start | bytes 294920 | tf_op jit(solution)/shard_map/ppermute | solution.py:454
  182.1 0.7 copy-start.4
  186.1 0.6 copy-start.5
Sparse Core Ops, SparseCore 0:
  65.1 52.7 reduce-scatter.2
  128.0 52.5 reduce-scatter.4

commit v8 on v6

--- a/solution.py
+++ b/solution.py
@@ -263,7 +263,7 @@
         return pltpu.make_async_copy(staged.at[q], dst, out_sem)
 
     def start(q):
-        z, w = q // N_X, (q % N_X) ^ me
+        z, w = (q // N_X - me_ref[1]) & (tiles // N_X - 1), (q % N_X) ^ me
         if n_out == 1:
             out_copy(q, out_refs[0].at[z, pl.ds(w * per, per)]).start()
         else:
@@ -308,7 +308,7 @@
     pltpu.make_async_copy(staged, staged, out_sem).wait()
 
 
-def ladder(me, lists, amplitudes, received, weights, begin, first, n_i, n_z, per, slots):
+def ladder(place, lists, amplitudes, received, weights, begin, first, n_i, n_z, per, slots):
     _, occ, width = amplitudes.shape
     rows = n_i * occ
     tiles = n_z * N_X
@@ -340,7 +340,7 @@
         cost_estimate=pl.CostEstimate(
             flops=0, bytes_accessed=8 * rows * (width + n_z * TILE), transcendentals=0
         ),
-    )(me, lists, amplitudes, received, weights)
+    )(place, lists, amplitudes, received, weights)
 
 
 def finish_kernel(near, far, *refs):
@@ -368,27 +368,46 @@
     )(near, far)
 
 
-def finish_last(done, sum1, far):
-    early = sum1.shape[1] - N_X
+def finish_last(done, early, up, down, late, far):
+    whole = pl.BlockSpec(memory_space=pltpu.VMEM)
+    hbm = pl.BlockSpec(memory_space=pl.ANY)
+    rows = early.shape[0] + late.shape[0]
+    begin = done.shape[1] - rows
+
+    def kernel(done_ref, early_ref, up_ref, down_ref, late_ref, far_ref, out_ref, held, sem):
+        first = early_ref[...]
+        for ref in (up_ref, down_ref):
+            first = first + ref[...].astype(jnp.float32).reshape(-1, TILE)
+        last = late_ref[...] + far_ref[...].astype(jnp.float32)
+        held[...] = jnp.concatenate([first, last], 0).T.astype(held.dtype)
+        copy = pltpu.make_async_copy(held, out_ref.at[:, begin:], sem)
+        copy.start()
+        copy.wait()
+
     return pl.pallas_call(
-        lambda done_ref, *refs: finish_kernel(*refs),
-        grid=(1,),
-        in_specs=[
-            pl.BlockSpec(memory_space=pl.ANY),
-            slots(sum1, 1, 0),
-            pl.BlockSpec(far.shape, lambda g: (0, 0)),
-            slots(sum1, early, N_X // early),
-        ],
-        out_specs=pl.BlockSpec((TILE, done.shape[1] // 2), lambda g: (0, 1)),
+        kernel,
+        in_specs=[hbm] + [whole] * 5,
+        out_specs=hbm,
         out_shape=jax.ShapeDtypeStruct(done.shape, jnp.bfloat16),
+        scratch_shapes=[pltpu.VMEM((TILE, rows), jnp.bfloat16), pltpu.SemaphoreType.DMA],
         input_output_aliases={0: 0},
         compiler_params=params(16),
-    )(done, sum1, far, sum1)
+    )(done, early, up, down, late, far)
+
+
+def add(*parts):
+    total = parts[0].astype(jnp.float32)
+    for part in parts[1:]:
+        total = total + part.astype(jnp.float32)
+    return total
 
 
 def on_device(amplitudes, plus, minus, cd_irrep, ab_irrep):
     rows = amplitudes.shape[0]
-    me = lax.axis_index("xl").reshape(1).astype(jnp.int32)
+    me, mine = (lax.axis_index(name).astype(jnp.int32) for name in ("xl", "z"))
+    fixed, turned = jnp.stack([me, jnp.zeros_like(me)]), jnp.stack([me, mine])
+    n_z = plus.shape[1] // PAIR
+    half = n_z // 2
     swap = functools.partial(lax.ppermute, axis_name="xl", perm=[(0, 1), (1, 0)])
 
     def exchange(packed):
@@ -397,9 +416,32 @@
     def scatter(terms):
         return lax.psum_scatter(terms, "z", scatter_dimension=0, tiled=True)
 
-    def product(received, begin, first, n_i, slots):
+    up = functools.partial(
+        lax.ppermute, axis_name="z", perm=[(k, (k + 1) % n_z) for k in range(n_z)]
+    )
+    down = functools.partial(
+        lax.ppermute, axis_name="z", perm=[((k + 1) % n_z, k) for k in range(n_z)]
+    )
+
+    def send(*pair):
+        pair = lax.optimization_barrier(tuple(p.astype(jnp.bfloat16) for p in pair))
+        return lax.optimization_barrier((up(pair[0]), down(pair[1])))
+
+    def set_out(terms):
+        first = terms(half)
+        return send(add(*[t[:1] for t in first]), add(*[t[1:] for t in first]))
+
+    def go_on(terms, step, goes_up, goes_down):
+        if step == 1:
+            goes_up = jnp.pad(goes_up, ((0, 1), (0, 0), (0, 0)))
+            goes_down = jnp.pad(goes_down, ((1, 0), (0, 0), (0, 0)))
+        return send(
+            add(goes_up, *terms(half - step)), add(goes_down, *terms(half + step))
+        )
+
+    def product(place, received, begin, first, n_i, slots):
         return ladder(
-            me,
+            place,
             lists,
             amplitudes,
             received,
@@ -407,7 +449,7 @@
             begin,
             first,
             n_i,
-            plus.shape[1] // PAIR,
+            n_z,
             1,
             slots,
         )
@@ -421,22 +463,35 @@
     lists, weights = match(cd_irrep, ab_irrep, first_plus, minus)
     received0, packed1, weights = lax.optimization_barrier((received0, packed1, weights))
     received1 = exchange(packed1)
-    (terms0,) = product(received0, 0, 0, FIRST - UNIT, N_X)
+    (terms0,) = product(fixed, received0, 0, 0, FIRST - UNIT, N_X)
     sum0 = scatter(terms0)
     received0, _ = lax.optimization_barrier((received0, terms0))
-    near0, far0 = product(received0, 0, FIRST - UNIT, UNIT, 0)
+    near0, far0 = product(turned, received0, 0, FIRST - UNIT, UNIT, 0)
     far0 = swap(far0)
     received1, _ = lax.optimization_barrier((received1, near0))
-    near1, far1 = product(received1, FIRST, 0, UNIT, 0)
+    near1, far1 = product(turned, received1, FIRST, 0, UNIT, 0)
     far1 = swap(far1)
     received1, _ = lax.optimization_barrier((received1, near1))
-    (terms1,) = product(received1, FIRST, UNIT, rest - UNIT, 2 * N_X)
-    for k, (near, far) in enumerate(((near0, far0), (near1, far1))):
-        early = (near.astype(jnp.float32) + far.astype(jnp.float32)).astype(jnp.bfloat16)
-        terms1 = lax.dynamic_update_slice(terms1, early, (0, N_X + k, 0, 0))
-    sum1 = scatter(terms1)
+    (terms1,) = product(turned, received1, FIRST, UNIT, rest - UNIT, N_X)
+
+    def late(k):
+        return (terms1[k],)
+
+    def early(k):
+        return [jnp.concatenate(pair, 0) for pair in ((near0[k], near1[k]), (far0[k], far1[k]))]
+
+    late_ring = set_out(late)
+    late_ring, far0, far1 = lax.optimization_barrier((late_ring, far0, far1))
+    early_ring = set_out(early)
+    for step in range(1, half):
+        late_ring = go_on(late, step, *late_ring)
+        early_ring = go_on(early, step, *early_ring)
+    late_sum = add(terms1[0], *late_ring)
+    far_late = swap(late_sum[1].astype(jnp.bfloat16))
     done = finish_first(sum0, swap(sum0[0, 1]))
-    return finish_last(done, sum1, swap(sum1[0, 1]))
+    return finish_last(
+        done, add(*early(0)).reshape(-1, TILE), *early_ring, late_sum[0], far_late
+    )
 
 
 def solution(mesh):

time: 183 us -> 166 us (0.907)
  waiting for transfers between devices: 101 us -> 49.9 us
  starting transfers between devices: 13.5 us -> 49.3 us
    reduce_scatter x2 -> x1, waiting for transfers between devices: 52.3 us -> 0.02 us  [scatter(): return lax.psum_scatter(terms, 'z', scatter_dimension=0, tiled=True)]
    ppermute x1 -> x17, starting transfers between devices: 0.71 us -> 33.6 us  [the longest x16 31.8 us: send(): return lax.optimization_barrier((up(pair[0]), down(pair[1])))]
    ppermute x1, waiting for transfers between devices: 14.4 us -> 2.06 us  [on_device(): far1 = swap(far1)]
    ppermute x1 -> x17, waiting for transfers between devices: 1.24 us -> 11.6 us  [the longest x16 11.6 us: send(): return lax.optimization_barrier((up(pair[0]), down(pair[1])))]
    ppermute x1, waiting for transfers between devices: 0.01 us -> 4.56 us  [on_device(): done = finish_first(sum0, swap(sum0[0, 1]))]
    dynamic_update_slice x2 -> x0, other arithmetic: 2.21 us -> none  [on_device(): terms1 = lax.dynamic_update_slice(terms1, early, (0, N_X + k, 0, 0))]
    ppermute x1, starting transfers between devices: 0.98 us -> 2.88 us  [on_device(): far0 = swap(far0)]
  transfers between devices with their start and end apart: 8 -> 23, of which waited for: 6 -> 12; matrix products, arithmetic and copies ran while one was open for 2% -> 1% of each run, Pallas kernels for 17% -> 20%
where the time goes in v8:
time: 166 us; the launch traced here: 165 us
  waiting for transfers between devices  49.9 us (30%)
  starting transfers between devices  49.3 us (30%)
  Pallas kernels  47.3 us (28%)
  between operations  13.7 us (8%)
  local copies, waits for them, and re-layouts  3.49 us (2%)
    ppermute x16, starting transfers between devices, send(): return lax.optimization_barrier((up(pair[0]), down(pair[1])))  31.8 us
    all_to_all x2, waiting for transfers between devices, exchange(): lax.all_to_all(packed, 'row', split_axis=0, concat_axis=0, tiled=True)  31.7 us
    pallas_call x4, Pallas kernels, ladder(): pl.pallas_call(functools.partial(ladder_kernel, begin, first), in_specs=[...  28.9 us
    ppermute x16, waiting for transfers between devices, send(): return lax.optimization_barrier((up(pair[0]), down(pair[1])))  11.6 us
    all_to_all x2, starting transfers between devices, exchange(): lax.all_to_all(packed, 'row', split_axis=0, concat_axis=0, tiled=True)  9.84 us
    pallas_call x2, Pallas kernels, pack(): pl.pallas_call(functools.partial(pack_kernel, first, n_i), in_specs=[hbm]...  9.47 us
    pallas_call x1, Pallas kernels, match(): pl.pallas_call(match_kernel, in_specs=[smem, smem, hbm, hbm], out_specs=[...  6.14 us
    ppermute x1, waiting for transfers between devices, on_device(): done = finish_first(sum0, swap(sum0[0, 1]))  4.56 us
  transfers between devices with their start and end apart: 23, of which 12 were waited for; matrix products, arithmetic and copies ran while one was open for 1% of the time, Pallas kernels for 20%

profile of v8, /device:TPU:2, one launch (start us, length us, event | category | flops | bytes accessed | tf_op | source)
XLA Modules:
  0.0 164.8 jit_solution(4082301491441877049)
XLA Ops:
  6.5 5.2 %shard_map.56 = bf16[1536,768]{1,0:T(8,128)(2,1)} custom-call(bf16[12,192,768]{2,1,0:T(8,128)(2,1)} %amp_ref.10), custom_call_target="tpu_custom_call" | custom-call | bytes 7077888 | tf_op jit(solution)/shard_map/pallas_call | solution.py:79
  11.8 6.1 %all-to-all-start = ((bf16[16,96,768]{2,1,0:T(8,128)(2,1)}), bf16[16,96,768]{2,1,0:T(8,128)(2,1)S(1)}, u32[]{:S(2)}, u32[]{:S(2)}) async-start(bf16[16,96,768]{2,1,0:T(8,128)(2,1)} %bitcast.117), calls=%async_computation | async-start | bytes 4718592 | tf_op jit(solution)/shard_map/all_to_all | solution.py:414
  17.9 4.3 %shard_map.57 = bf16[768,768]{1,0:T(8,128)(2,1)} custom-call(bf16[12,192,768]{2,1,0:T(8,128)(2,1)} %amp_ref.10), custom_call_target="tpu_custom_call" | custom-call | bytes 7077888 | tf_op jit(solution)/shard_map/pallas_call | solution.py:79
  22.2 6.1 %shard_map.55 = (s32[62]{0:T(128)}, bf16[48,256,256]{2,1,0:T(8,128)(2,1)}) custom-call(s32[6]{0:T(128)} %cd_ref.1, s32[16]{0:T(128)} %ab_ref.1, bf16[768,2048]{1,0:T(8,128)(2,1)} %plus_ref, bf16[768,2048]{1,0:T(8,128)(2,1)} %minus_ref.1), custom_call_target="tpu_custom_call" | custom-call | bytes 12582912 | tf_op jit(solution)/shard_map/pallas_call | solution.py:196
  28.4 21.9 %all-to-all-done = bf16[16,96,768]{2,1,0:T(8,128)(2,1)S(1)} async-done(((bf16[16,96,768]{2,1,0:T(8,128)(2,1)}), bf16[16,96,768]{2,1,0:T(8,128)(2,1)S(1)}, u32[]{:S(2)}, u32[]{:S(2)}) %all-to-all-start) | async-done | bytes 2359328 | tf_op jit(solution)/shard_map/all_to_all | solution.py:414
  51.0 8.5 %shard_map.58 = bf16[8,2,1152,128]{3,2,1,0:T(8,128)(2,1)} custom-call(s32[2]{0:T(128)S(1)} %pad_add_fusion.me_ref, s32[62]{0:T(128)S(1)} %copy-done.2, bf16[12,192,768]{2,1,0:T(8,128)(2,1)} %amp_ref.10, bf16[1536,768]{1,0:T(8,128)(2,1)S(1)} %bitcast.112, bf16[48,256,256]{2,1,0:T(8,128)(2,1)} %get-tuple-element.58.weight_ref), custom_call_target="tpu_custom_call" | custom-call | bytes 16515072 | tf_op jit(solution)/shard_map/pallas_call | solution.py:324
  59.6 3.7 %all-to-all-start.1 = ((bf16[16,48,768]{2,1,0:T(8,128)(2,1)}), bf16[16,48,768]{2,1,0:T(8,128)(2,1)S(1)}, u32[]{:S(2)}, u32[]{:S(2)}) async-start(bf16[16,48,768]{2,1,0:T(8,128)(2,1)} %bitcast.118), calls=%async_computation.2 | async-start | bytes 2359296 | tf_op jit(solution)/shard_map/all_to_all | solution.py:414
  63.4 6.2 %shard_map.60 = (bf16[8,1,384,128]{3,2,1,0:T(8,128)(2,1)S(1)}, bf16[8,1,384,128]{3,2,1,0:T(8,128)(2,1)}) custom-call(s32[2]{0:T(128)S(1)} %pad_add_fusion.1.me_ref, s32[62]{0:T(128)S(1)} %copy-done.3, bf16[12,192,768]{2,1,0:T(8,128)(2,1)} %amp_ref.10, bf16[1536,768]{1,0:T(8,128)(2,1)S(1)} %bitcast.113, bf16[48,256,256]{2,1,0:T(8,128)(2,1)} %get-tuple-element.58.weight_ref), custom_call_target="tpu_custom_call" | custom-call | bytes 5505024 | tf_op jit(solution)/shard_map/pallas_call | solution.py:324
  70.5 2.9 %collective-permute-start.3 = (bf16[8,1,384,128]{3,2,1,0:T(8,128)(2,1)}, bf16[8,1,384,128]{3,2,1,0:T(8,128)(2,1)S(1)}, u32[]{:S(2)}, u32[]{:S(2)}) collective-permute-start(bf16[8,1,384,128]{3,2,1,0:T(8,128)(2,1)} %get-tuple-element.69), channel_id=1, source_target_pairs={{0,1},{1,0},{2,3},{3,2},{4,5},{5,4},{6,7},{7,6},{8,9},{9,8},{10,11... | collective-permute-start | bytes 2359304 | tf_op jit(solution)/shard_map/ppermute | solution.py:470
  73.4 9.8 %all-to-all-done.1 = bf16[16,48,768]{2,1,0:T(8,128)(2,1)S(1)} async-done(((bf16[16,48,768]{2,1,0:T(8,128)(2,1)}), bf16[16,48,768]{2,1,0:T(8,128)(2,1)S(1)}, u32[]{:S(2)}, u32[]{:S(2)}) %all-to-all-start.1) | async-done | bytes 1179680 | tf_op jit(solution)/shard_map/all_to_all | solution.py:414
  83.2 7.1 %shard_map.61 = (bf16[8,1,384,128]{3,2,1,0:T(8,128)(2,1)S(1)}, bf16[8,1,384,128]{3,2,1,0:T(8,128)(2,1)S(1)}) custom-call(s32[2]{0:T(128)S(1)} %pad_add_fusion.1.me_ref, s32[62]{0:T(128)S(1)} %copy-done.3, bf16[12,192,768]{2,1,0:T(8,128)(2,1)} %amp_ref.10, bf16[768,768]{1,0:T(8,128)(2,1)S(1)} %bitcast.114, bf16[48,256,256]{2,1,0:T(8,128)(2,1)} %get-tuple-element.58.weight_ref), custom_call_target="tpu_custom_call" | custom-call | bytes 5505024 | tf_op jit(solution)/shard_map/pallas_call | solution.py:324
  90.3 2.5 %collective-permute-start.4 = (bf16[8,1,384,128]{3,2,1,0:T(8,128)(2,1)S(1)}, bf16[8,1,384,128]{3,2,1,0:T(8,128)(2,1)S(1)}, u32[]{:S(2)}, u32[]{:S(2)}) collective-permute-start(bf16[8,1,384,128]{3,2,1,0:T(8,128)(2,1)S(1)} %get-tuple-element.70), channel_id=1, source_target_pairs={{0,1},{1,0},{2,3},{3,2},{4,5},{5,4},{6,7},{7,6},{8,9},{9,8},{10,11... | collective-permute-start | bytes 2359304 | tf_op jit(solution)/shard_map/ppermute | solution.py:473
  92.9 7.0 %shard_map.62 = bf16[8,2,384,128]{3,2,1,0:T(8,128)(2,1)S(1)} custom-call(s32[2]{0:T(128)S(1)} %pad_add_fusion.1.me_ref, s32[62]{0:T(128)S(1)} %copy-done.3, bf16[12,192,768]{2,1,0:T(8,128)(2,1)} %amp_ref.10, bf16[768,768]{1,0:T(8,128)(2,1)S(1)} %bitcast.115, bf16[48,256,256]{2,1,0:T(8,128)(2,1)} %get-tuple-element.58.weight_ref), custom_call_target="tpu_custom_call" | custom-call | bytes 5505024 | tf_op jit(solution)/shard_map/pallas_call | solution.py:324
  99.9 2.0 %collective-permute-start.1 = (bf16[1,384,128]{2,1,0:T(8,128)(2,1)S(1)}, bf16[1,384,128]{2,1,0:T(8,128)(2,1)S(1)}, u32[]{:S(2)}, u32[]{:S(2)}) collective-permute-start(bf16[1,384,128]{2,1,0:T(8,128)(2,1)S(1)} %get-tuple-element.65), channel_id=1, source_target_pairs={{0,2},{2,4},{4,6},{6,8},{8,10},{10,12},{12,14},{14,0},{1,3},{3,5},... | collective-permute-start | bytes 294920 | tf_op jit(solution)/shard_map/ppermute | solution.py:428
  101.9 4.2 %collective-permute-start.2 = (bf16[1,384,128]{2,1,0:T(8,128)(2,1)S(1)}, bf16[1,384,128]{2,1,0:T(8,128)(2,1)S(1)}, u32[]{:S(2)}, u32[]{:S(2)}) collective-permute-start(bf16[1,384,128]{2,1,0:T(8,128)(2,1)S(1)} %get-tuple-element.66), channel_id=1, source_target_pairs={{2,0},{4,2},{6,4},{8,6},{10,8},{12,10},{14,12},{0,14},{3,1},{5,3},... | collective-permute-start | bytes 294920 | tf_op jit(solution)/shard_map/ppermute | solution.py:428
  106.1 5.2 %collective-permute-done.1 = bf16[1,384,128]{2,1,0:T(8,128)(2,1)S(1)} collective-permute-done((bf16[1,384,128]{2,1,0:T(8,128)(2,1)S(1)}, bf16[1,384,128]{2,1,0:T(8,128)(2,1)S(1)}, u32[]{:S(2)}, u32[]{:S(2)}) %collective-permute-start.1) | collective-permute-done | bytes 98336 | tf_op jit(solution)/shard_map/ppermute | solution.py:428
  111.3 2.1 %collective-permute-done.4 = bf16[8,1,384,128]{3,2,1,0:T(8,128)(2,1)S(1)} collective-permute-done((bf16[8,1,384,128]{3,2,1,0:T(8,128)(2,1)S(1)}, bf16[8,1,384,128]{3,2,1,0:T(8,128)(2,1)S(1)}, u32[]{:S(2)}, u32[]{:S(2)}) %collective-permute-start.4) | collective-permute-done | bytes 786464 | tf_op jit(solution)/shard_map/ppermute | solution.py:473
  113.4 1.5 collective-permute-start.5
  115.0 4.3 %collective-permute-start.6 = (bf16[1,384,128]{2,1,0:T(8,128)(2,1)S(1)}, bf16[1,384,128]{2,1,0:T(8,128)(2,1)S(1)}, u32[]{:S(2)}, u32[]{:S(2)}) collective-permute-start(bf16[1,384,128]{2,1,0:T(8,128)(2,1)S(1)} %fusion.8), channel_id=1, source_target_pairs={{2,0},{4,2},{6,4},{8,6},{10,8},{12,10},{14,12},{0,14},{3,1},{5,3},... | collective-permute-start | bytes 294920 | tf_op jit(solution)/shard_map/ppermute | solution.py:428
  119.4 3.2 %collective-permute-start.14 = (bf16[2,384,128]{2,1,0:T(8,128)(2,1)S(1)}, bf16[2,384,128]{2,1,0:T(8,128)(2,1)S(1)}, u32[]{:S(2)}, u32[]{:S(2)}) collective-permute-start(bf16[2,384,128]{2,1,0:T(8,128)(2,1)S(1)} %get-tuple-element.92), channel_id=1, source_target_pairs={{2,0},{4,2},{6,4},{8,6},{10,8},{12,10},{14,12},{0,14},{3,1},{5,3},... | collective-permute-start | bytes 589832 | tf_op jit(solution)/shard_map/ppermute | solution.py:428
  123.7 3.2 %collective-permute-start.8 = (bf16[2,384,128]{2,1,0:T(8,128)(2,1)S(1)}, bf16[2,384,128]{2,1,0:T(8,128)(2,1)S(1)}, u32[]{:S(2)}, u32[]{:S(2)}) collective-permute-start(bf16[2,384,128]{2,1,0:T(8,128)(2,1)S(1)} %add_convert_fusion.4), channel_id=1, source_target_pairs={{2,0},{4,2},{6,4},{8,6},{10,8},{12,10},{14,12},{0,14},{3,1},{5,3},... | collective-permute-start | bytes 589832 | tf_op jit(solution)/shard_map/ppermute | solution.py:428
  127.9 3.2 %collective-permute-start.16 = (bf16[2,384,128]{2,1,0:T(8,128)(2,1)S(1)}, bf16[2,384,128]{2,1,0:T(8,128)(2,1)S(1)}, u32[]{:S(2)}, u32[]{:S(2)}) collective-permute-start(bf16[2,384,128]{2,1,0:T(8,128)(2,1)S(1)} %get-tuple-element.96), channel_id=1, source_target_pairs={{2,0},{4,2},{6,4},{8,6},{10,8},{12,10},{14,12},{0,14},{3,1},{5,3},... | collective-permute-start | bytes 589832 | tf_op jit(solution)/shard_map/ppermute | solution.py:428
  131.1 1.6 collective-permute-done.7
  133.0 3.2 %collective-permute-start.10 = (bf16[2,384,128]{2,1,0:T(8,128)(2,1)S(1)}, bf16[2,384,128]{2,1,0:T(8,128)(2,1)S(1)}, u32[]{:S(2)}, u32[]{:S(2)}) collective-permute-start(bf16[2,384,128]{2,1,0:T(8,128)(2,1)S(1)} %add_convert_fusion.2), channel_id=1, source_target_pairs={{2,0},{4,2},{6,4},{8,6},{10,8},{12,10},{14,12},{0,14},{3,1},{5,3},... | collective-permute-start | bytes 589832 | tf_op jit(solution)/shard_map/ppermute | solution.py:428
  137.0 2.0 %collective-permute-start.17 = (bf16[2,384,128]{2,1,0:T(8,128)(2,1)S(1)}, bf16[2,384,128]{2,1,0:T(8,128)(2,1)S(1)}, u32[]{:S(2)}, u32[]{:S(2)}) collective-permute-start(bf16[2,384,128]{2,1,0:T(8,128)(2,1)S(1)} %get-tuple-element.99), channel_id=1, source_target_pairs={{0,2},{2,4},{4,6},{6,8},{8,10},{10,12},{12,14},{14,0},{1,3},{3,5},... | collective-permute-start | bytes 589832 | tf_op jit(solution)/shard_map/ppermute | solution.py:428
  139.1 1.3 collective-permute-start.18
  141.4 2.4 %collective-permute-start.11 = (bf16[2,384,128]{2,1,0:T(8,128)(2,1)S(1)}, bf16[2,384,128]{2,1,0:T(8,128)(2,1)S(1)}, u32[]{:S(2)}, u32[]{:S(2)}) collective-permute-start(bf16[2,384,128]{2,1,0:T(8,128)(2,1)S(1)} %get-tuple-element.85), channel_id=1, source_target_pairs={{0,2},{2,4},{4,6},{6,8},{8,10},{10,12},{12,14},{14,0},{1,3},{3,5},... | collective-permute-start | bytes 589832 | tf_op jit(solution)/shard_map/ppermute | solution.py:428
  144.7 1.5 collective-permute-done.17
  146.6 1.0 slice_bitcast_fusion
  148.0 1.8 %collective-permute-start.19 = (bf16[384,128]{1,0:T(8,128)(2,1)S(1)}, bf16[384,128]{1,0:T(8,128)(2,1)S(1)}, u32[]{:S(2)}, u32[]{:S(2)}) collective-permute-start(bf16[384,128]{1,0:T(8,128)(2,1)S(1)} %fusion.9), channel_id=1, source_target_pairs={{0,1},{1,0},{2,3},{3,2},{4,5},{5,4},{6,7},{7,6},{8,9},{9,8},{10,11... | collective-permute-start | bytes 294920 | tf_op jit(solution)/shard_map/ppermute | solution.py:490
  149.8 4.6 %collective-permute-done.far = bf16[1152,128]{1,0:T(8,128)(2,1)S(1)} collective-permute-done((bf16[1152,128]{1,0:T(8,128)(2,1)S(1)}, bf16[1152,128]{1,0:T(8,128)(2,1)S(1)}, u32[]{:S(2)}, u32[]{:S(2)}) %collective-permute-start) | collective-permute-done | bytes 294944 | tf_op jit(solution)/shard_map/ppermute | solution.py:491
  155.1 1.9 %shard_map.59.done_ref = bf16[128,2304]{1,0:T(8,128)(2,1)} custom-call(bf16[1,2,1152,128]{3,2,1,0:T(8,128)(2,1)} %reduce-scatter.2.cloned.1.call-done.near, bf16[1152,128]{1,0:T(8,128)(2,1)} %copy-done.4), custom_call_target="tpu_custom_call" | custom-call | tf_op jit(solution)/shard_map/pallas_call | solution.py:361
  (56 shorter events, 9.5 us)
Async XLA Ops:
  11.8 38.6 %all-to-all-start = ((bf16[16,96,768]{2,1,0:T(8,128)(2,1)}), bf16[16,96,768]{2,1,0:T(8,128)(2,1)S(1)}, u32[]{:S(2)}, u32[]{:S(2)}) async-start(bf16[16,96,768]{2,1,0:T(8,128)(2,1)} %bitcast.117), calls=%async_computation | async-start | bytes 4718592 | tf_op jit(solution)/shard_map/all_to_all | solution.py:414
  17.9 128.7 %reduce-scatter.2.cloned.1.call-start = ((), (), s32[]{:S(2)}) async-start(), calls=%async_computation.3 | async-start | bytes 5308416 | tf_op jit(solution)/shard_map/reduce_scatter | solution.py:417
  50.3 0.7 copy-start.2
  59.6 3.8 %copy-start.3 = (s32[62]{0:T(128)S(1)}, s32[62]{0:T(128)}, u32[]{:S(2)}) copy-start(s32[62]{0:T(128)} %get-tuple-element.54.lists) | copy-start | bytes 748
  59.6 23.6 %all-to-all-start.1 = ((bf16[16,48,768]{2,1,0:T(8,128)(2,1)}), bf16[16,48,768]{2,1,0:T(8,128)(2,1)S(1)}, u32[]{:S(2)}, u32[]{:S(2)}) async-start(bf16[16,48,768]{2,1,0:T(8,128)(2,1)} %bitcast.118), calls=%async_computation.2 | async-start | bytes 2359296 | tf_op jit(solution)/shard_map/all_to_all | solution.py:414
  69.6 0.9 copy-start
  70.5 40.8 %collective-permute-start.3 = (bf16[8,1,384,128]{3,2,1,0:T(8,128)(2,1)}, bf16[8,1,384,128]{3,2,1,0:T(8,128)(2,1)S(1)}, u32[]{:S(2)}, u32[]{:S(2)}) collective-permute-start(bf16[8,1,384,128]{3,2,1,0:T(8,128)(2,1)} %get-tuple-element.69), channel_id=1, source_target_pairs={{0,1},{1,0},{2,3},{3,2},{4,5},{5,4},{6,7},{7,6},{8,9},{9,8},{10,11... | collective-permute-start | bytes 2359304 | tf_op jit(solution)/shard_map/ppermute | solution.py:470
  83.2 9.7 %copy-start.1 = (bf16[8,1,384,128]{3,2,1,0:T(8,128)(2,1)S(1)}, bf16[8,1,384,128]{3,2,1,0:T(8,128)(2,1)}, u32[]{:S(2)}) copy-start(bf16[8,1,384,128]{3,2,1,0:T(8,128)(2,1)} %copy-done) | copy-start | bytes 2359300
  90.3 23.1 %collective-permute-start.4 = (bf16[8,1,384,128]{3,2,1,0:T(8,128)(2,1)S(1)}, bf16[8,1,384,128]{3,2,1,0:T(8,128)(2,1)S(1)}, u32[]{:S(2)}, u32[]{:S(2)}) collective-permute-start(bf16[8,1,384,128]{3,2,1,0:T(8,128)(2,1)S(1)} %get-tuple-element.70), channel_id=1, source_target_pairs={{0,1},{1,0},{2,3},{3,2},{4,5},{5,4},{6,7},{7,6},{8,9},{9,8},{10,11... | collective-permute-start | bytes 2359304 | tf_op jit(solution)/shard_map/ppermute | solution.py:473
  99.9 11.3 %collective-permute-start.1 = (bf16[1,384,128]{2,1,0:T(8,128)(2,1)S(1)}, bf16[1,384,128]{2,1,0:T(8,128)(2,1)S(1)}, u32[]{:S(2)}, u32[]{:S(2)}) collective-permute-start(bf16[1,384,128]{2,1,0:T(8,128)(2,1)S(1)} %get-tuple-element.65), channel_id=1, source_target_pairs={{0,2},{2,4},{4,6},{6,8},{8,10},{10,12},{12,14},{14,0},{1,3},{3,5},... | collective-permute-start | bytes 294920 | tf_op jit(solution)/shard_map/ppermute | solution.py:428
  101.9 9.4 %collective-permute-start.2 = (bf16[1,384,128]{2,1,0:T(8,128)(2,1)S(1)}, bf16[1,384,128]{2,1,0:T(8,128)(2,1)S(1)}, u32[]{:S(2)}, u32[]{:S(2)}) collective-permute-start(bf16[1,384,128]{2,1,0:T(8,128)(2,1)S(1)} %get-tuple-element.66), channel_id=1, source_target_pairs={{2,0},{4,2},{6,4},{8,6},{10,8},{12,10},{14,12},{0,14},{3,1},{5,3},... | collective-permute-start | bytes 294920 | tf_op jit(solution)/shard_map/ppermute | solution.py:428
  113.4 10.0 %collective-permute-start.5 = (bf16[1,384,128]{2,1,0:T(8,128)(2,1)S(1)}, bf16[1,384,128]{2,1,0:T(8,128)(2,1)S(1)}, u32[]{:S(2)}, u32[]{:S(2)}) collective-permute-start(bf16[1,384,128]{2,1,0:T(8,128)(2,1)S(1)} %fusion.7), channel_id=1, source_target_pairs={{0,2},{2,4},{4,6},{6,8},{8,10},{10,12},{12,14},{14,0},{1,3},{3,5},... | collective-permute-start | bytes 294920 | tf_op jit(solution)/shard_map/ppermute | solution.py:428
  115.0 8.5 %collective-permute-start.6 = (bf16[1,384,128]{2,1,0:T(8,128)(2,1)S(1)}, bf16[1,384,128]{2,1,0:T(8,128)(2,1)S(1)}, u32[]{:S(2)}, u32[]{:S(2)}) collective-permute-start(bf16[1,384,128]{2,1,0:T(8,128)(2,1)S(1)} %fusion.8), channel_id=1, source_target_pairs={{2,0},{4,2},{6,4},{8,6},{10,8},{12,10},{14,12},{0,14},{3,1},{5,3},... | collective-permute-start | bytes 294920 | tf_op jit(solution)/shard_map/ppermute | solution.py:428
  119.3 8.4 %collective-permute-start.13 = (bf16[2,384,128]{2,1,0:T(8,128)(2,1)S(1)}, bf16[2,384,128]{2,1,0:T(8,128)(2,1)S(1)}, u32[]{:S(2)}, u32[]{:S(2)}) collective-permute-start(bf16[2,384,128]{2,1,0:T(8,128)(2,1)S(1)} %get-tuple-element.91), channel_id=1, source_target_pairs={{0,2},{2,4},{4,6},{6,8},{8,10},{10,12},{12,14},{14,0},{1,3},{3,5},... | collective-permute-start | bytes 589832 | tf_op jit(solution)/shard_map/ppermute | solution.py:428
  119.4 8.3 %collective-permute-start.14 = (bf16[2,384,128]{2,1,0:T(8,128)(2,1)S(1)}, bf16[2,384,128]{2,1,0:T(8,128)(2,1)S(1)}, u32[]{:S(2)}, u32[]{:S(2)}) collective-permute-start(bf16[2,384,128]{2,1,0:T(8,128)(2,1)S(1)} %get-tuple-element.92), channel_id=1, source_target_pairs={{2,0},{4,2},{6,4},{8,6},{10,8},{12,10},{14,12},{0,14},{3,1},{5,3},... | collective-permute-start | bytes 589832 | tf_op jit(solution)/shard_map/ppermute | solution.py:428
  123.6 9.1 %collective-permute-start.7 = (bf16[2,384,128]{2,1,0:T(8,128)(2,1)S(1)}, bf16[2,384,128]{2,1,0:T(8,128)(2,1)S(1)}, u32[]{:S(2)}, u32[]{:S(2)}) collective-permute-start(bf16[2,384,128]{2,1,0:T(8,128)(2,1)S(1)} %add_convert_fusion.5), channel_id=1, source_target_pairs={{0,2},{2,4},{4,6},{6,8},{8,10},{10,12},{12,14},{14,0},{1,3},{3,5},... | collective-permute-start | bytes 589832 | tf_op jit(solution)/shard_map/ppermute | solution.py:428
  123.7 9.0 %collective-permute-start.8 = (bf16[2,384,128]{2,1,0:T(8,128)(2,1)S(1)}, bf16[2,384,128]{2,1,0:T(8,128)(2,1)S(1)}, u32[]{:S(2)}, u32[]{:S(2)}) collective-permute-start(bf16[2,384,128]{2,1,0:T(8,128)(2,1)S(1)} %add_convert_fusion.4), channel_id=1, source_target_pairs={{2,0},{4,2},{6,4},{8,6},{10,8},{12,10},{14,12},{0,14},{3,1},{5,3},... | collective-permute-start | bytes 589832 | tf_op jit(solution)/shard_map/ppermute | solution.py:428
  127.8 9.1 %collective-permute-start.15 = (bf16[2,384,128]{2,1,0:T(8,128)(2,1)S(1)}, bf16[2,384,128]{2,1,0:T(8,128)(2,1)S(1)}, u32[]{:S(2)}, u32[]{:S(2)}) collective-permute-start(bf16[2,384,128]{2,1,0:T(8,128)(2,1)S(1)} %get-tuple-element.95), channel_id=1, source_target_pairs={{0,2},{2,4},{4,6},{6,8},{8,10},{10,12},{12,14},{14,0},{1,3},{3,5},... | collective-permute-start | bytes 589832 | tf_op jit(solution)/shard_map/ppermute | solution.py:428
  127.9 9.0 %collective-permute-start.16 = (bf16[2,384,128]{2,1,0:T(8,128)(2,1)S(1)}, bf16[2,384,128]{2,1,0:T(8,128)(2,1)S(1)}, u32[]{:S(2)}, u32[]{:S(2)}) collective-permute-start(bf16[2,384,128]{2,1,0:T(8,128)(2,1)S(1)} %get-tuple-element.96), channel_id=1, source_target_pairs={{2,0},{4,2},{6,4},{8,6},{10,8},{12,10},{14,12},{0,14},{3,1},{5,3},... | collective-permute-start | bytes 589832 | tf_op jit(solution)/shard_map/ppermute | solution.py:428
  132.9 8.3 %collective-permute-start.9 = (bf16[2,384,128]{2,1,0:T(8,128)(2,1)S(1)}, bf16[2,384,128]{2,1,0:T(8,128)(2,1)S(1)}, u32[]{:S(2)}, u32[]{:S(2)}) collective-permute-start(bf16[2,384,128]{2,1,0:T(8,128)(2,1)S(1)} %add_convert_fusion.3), channel_id=1, source_target_pairs={{0,2},{2,4},{4,6},{6,8},{8,10},{10,12},{12,14},{14,0},{1,3},{3,5},... | collective-permute-start | bytes 589832 | tf_op jit(solution)/shard_map/ppermute | solution.py:428
  133.0 8.2 %collective-permute-start.10 = (bf16[2,384,128]{2,1,0:T(8,128)(2,1)S(1)}, bf16[2,384,128]{2,1,0:T(8,128)(2,1)S(1)}, u32[]{:S(2)}, u32[]{:S(2)}) collective-permute-start(bf16[2,384,128]{2,1,0:T(8,128)(2,1)S(1)} %add_convert_fusion.2), channel_id=1, source_target_pairs={{2,0},{4,2},{6,4},{8,6},{10,8},{12,10},{14,12},{0,14},{3,1},{5,3},... | collective-permute-start | bytes 589832 | tf_op jit(solution)/shard_map/ppermute | solution.py:428
  137.0 9.1 %collective-permute-start.17 = (bf16[2,384,128]{2,1,0:T(8,128)(2,1)S(1)}, bf16[2,384,128]{2,1,0:T(8,128)(2,1)S(1)}, u32[]{:S(2)}, u32[]{:S(2)}) collective-permute-start(bf16[2,384,128]{2,1,0:T(8,128)(2,1)S(1)} %get-tuple-element.99), channel_id=1, source_target_pairs={{0,2},{2,4},{4,6},{6,8},{8,10},{10,12},{12,14},{14,0},{1,3},{3,5},... | collective-permute-start | bytes 589832 | tf_op jit(solution)/shard_map/ppermute | solution.py:428
  139.1 7.4 %collective-permute-start.18 = (bf16[2,384,128]{2,1,0:T(8,128)(2,1)S(1)}, bf16[2,384,128]{2,1,0:T(8,128)(2,1)S(1)}, u32[]{:S(2)}, u32[]{:S(2)}) collective-permute-start(bf16[2,384,128]{2,1,0:T(8,128)(2,1)S(1)} %get-tuple-element.100), channel_id=1, source_target_pairs={{2,0},{4,2},{6,4},{8,6},{10,8},{12,10},{14,12},{0,14},{3,1},{5,3},... | collective-permute-start | bytes 589832 | tf_op jit(solution)/shard_map/ppermute | solution.py:428
  141.4 8.4 %collective-permute-start.11 = (bf16[2,384,128]{2,1,0:T(8,128)(2,1)S(1)}, bf16[2,384,128]{2,1,0:T(8,128)(2,1)S(1)}, u32[]{:S(2)}, u32[]{:S(2)}) collective-permute-start(bf16[2,384,128]{2,1,0:T(8,128)(2,1)S(1)} %get-tuple-element.85), channel_id=1, source_target_pairs={{0,2},{2,4},{4,6},{6,8},{8,10},{10,12},{12,14},{14,0},{1,3},{3,5},... | collective-permute-start | bytes 589832 | tf_op jit(solution)/shard_map/ppermute | solution.py:428
  143.8 6.0 %collective-permute-start.12 = (bf16[2,384,128]{2,1,0:T(8,128)(2,1)S(1)}, bf16[2,384,128]{2,1,0:T(8,128)(2,1)S(1)}, u32[]{:S(2)}, u32[]{:S(2)}) collective-permute-start(bf16[2,384,128]{2,1,0:T(8,128)(2,1)S(1)} %get-tuple-element.86), channel_id=1, source_target_pairs={{2,0},{4,2},{6,4},{8,6},{10,8},{12,10},{14,12},{0,14},{3,1},{5,3},... | collective-permute-start | bytes 589832 | tf_op jit(solution)/shard_map/ppermute | solution.py:428
  147.6 6.8 %collective-permute-start = (bf16[1152,128]{1,0:T(8,128)(2,1)S(1)}, bf16[1152,128]{1,0:T(8,128)(2,1)S(1)}, u32[]{:S(2)}, u32[]{:S(2)}) collective-permute-start(bf16[1152,128]{1,0:T(8,128)(2,1)S(1)} %slice_bitcast_fusion), channel_id=1, source_target_pairs={{0,1},{1,0},{2,3},{3,2},{4,5},{5,4},{6,7},{7,6},{8,9},{9,8},{10,11... | collective-permute-start | bytes 884744 | tf_op jit(solution)/shard_map/ppermute | solution.py:491
  148.0 9.1 %collective-permute-start.19 = (bf16[384,128]{1,0:T(8,128)(2,1)S(1)}, bf16[384,128]{1,0:T(8,128)(2,1)S(1)}, u32[]{:S(2)}, u32[]{:S(2)}) collective-permute-start(bf16[384,128]{1,0:T(8,128)(2,1)S(1)} %fusion.9), channel_id=1, source_target_pairs={{0,1},{1,0},{2,3},{3,2},{4,5},{5,4},{6,7},{7,6},{8,9},{9,8},{10,11... | collective-permute-start | bytes 294920 | tf_op jit(solution)/shard_map/ppermute | solution.py:490
  154.4 0.7 copy-start.4
Sparse Core Ops, SparseCore 0:
  59.7 63.6 reduce-scatter.1

commit v9 on v8

--- a/solution.py
+++ b/solution.py
@@ -485,10 +485,15 @@
     early_ring = set_out(early)
     for step in range(1, half):
         late_ring = go_on(late, step, *late_ring)
+        if step == half - 1:
+            last0 = swap(sum0[0, 1])
+            early_ring, late_ring, last0 = lax.optimization_barrier(
+                (early_ring, late_ring, last0)
+            )
         early_ring = go_on(early, step, *early_ring)
     late_sum = add(terms1[0], *late_ring)
     far_late = swap(late_sum[1].astype(jnp.bfloat16))
-    done = finish_first(sum0, swap(sum0[0, 1]))
+    done = finish_first(sum0, last0)
     return finish_last(
         done, add(*early(0)).reshape(-1, TILE), *early_ring, late_sum[0], far_late
     )

time: 166 us -> 166 us (level)
  starting transfers between devices: 49.3 us -> 46.4 us
  other arithmetic: 1.04 us -> 3.3 us
  waiting for transfers between devices: 49.9 us -> 47.8 us
    ppermute x1, waiting for transfers between devices: 4.56 us -> 0.01 us  [on_device(): last0 = swap(sum0[0, 1])]
    convert_element_type x10, other arithmetic: 0.78 us -> 3.04 us  [send(): p.astype(jnp.bfloat16)]
    ppermute x16, waiting for transfers between devices: 11.6 us -> 13.4 us  [send(): return lax.optimization_barrier((up(pair[0]), down(pair[1])))]
  transfers between devices with their start and end apart: 23 -> 23, of which waited for: 12 -> 9; matrix products, arithmetic and copies ran while one was open for 1% -> 4% of each run, Pallas kernels for 20% -> 21%
where the time goes in v9:
time: 166 us; the launch traced here: 164 us
  Pallas kernels  48.5 us (29%)
  waiting for transfers between devices  47.8 us (29%)
  starting transfers between devices  46.4 us (28%)
  between operations  13.7 us (8%)
  local copies, waits for them, and re-layouts  4.62 us (3%)
  other arithmetic  3.3 us (2%)
    all_to_all x2, waiting for transfers between devices, exchange(): lax.all_to_all(packed, 'row', split_axis=0, concat_axis=0, tiled=True)  32.6 us
    ppermute x16, starting transfers between devices, send(): return lax.optimization_barrier((up(pair[0]), down(pair[1])))  31.6 us
    pallas_call x4, Pallas kernels, ladder(): pl.pallas_call(functools.partial(ladder_kernel, begin, first), in_specs=[...  30.1 us
    ppermute x16, waiting for transfers between devices, send(): return lax.optimization_barrier((up(pair[0]), down(pair[1])))  13.4 us
    all_to_all x2, starting transfers between devices, exchange(): lax.all_to_all(packed, 'row', split_axis=0, concat_axis=0, tiled=True)  9.84 us
    pallas_call x2, Pallas kernels, pack(): pl.pallas_call(functools.partial(pack_kernel, first, n_i), in_specs=[hbm]...  9.47 us
    pallas_call x1, Pallas kernels, match(): pl.pallas_call(match_kernel, in_specs=[smem, smem, hbm, hbm], out_specs=[...  6.17 us
  transfers between devices with their start and end apart: 23, of which 9 were waited for; matrix products, arithmetic and copies ran while one was open for 4% of the time, Pallas kernels for 21%

profile of v9, /device:TPU:2, one launch (start us, length us, event | category | flops | bytes accessed | tf_op | source)
XLA Modules:
  0.0 164.4 jit_solution(12562344753507824945)
XLA Ops:
  6.5 5.2 %shard_map.56 = bf16[1536,768]{1,0:T(8,128)(2,1)} custom-call(bf16[12,192,768]{2,1,0:T(8,128)(2,1)} %amp_ref.10), custom_call_target="tpu_custom_call" | custom-call | bytes 7077888 | tf_op jit(solution)/shard_map/pallas_call | solution.py:79
  11.8 6.1 %all-to-all-start = ((bf16[16,96,768]{2,1,0:T(8,128)(2,1)}), bf16[16,96,768]{2,1,0:T(8,128)(2,1)S(1)}, u32[]{:S(2)}, u32[]{:S(2)}) async-start(bf16[16,96,768]{2,1,0:T(8,128)(2,1)} %bitcast.117), calls=%async_computation | async-start | bytes 4718592 | tf_op jit(solution)/shard_map/all_to_all | solution.py:414
  17.9 4.3 %shard_map.57 = bf16[768,768]{1,0:T(8,128)(2,1)} custom-call(bf16[12,192,768]{2,1,0:T(8,128)(2,1)} %amp_ref.10), custom_call_target="tpu_custom_call" | custom-call | bytes 7077888 | tf_op jit(solution)/shard_map/pallas_call | solution.py:79
  22.2 6.2 %shard_map.55 = (s32[62]{0:T(128)}, bf16[48,256,256]{2,1,0:T(8,128)(2,1)}) custom-call(s32[6]{0:T(128)} %cd_ref.1, s32[16]{0:T(128)} %ab_ref.1, bf16[768,2048]{1,0:T(8,128)(2,1)} %plus_ref, bf16[768,2048]{1,0:T(8,128)(2,1)} %minus_ref.1), custom_call_target="tpu_custom_call" | custom-call | bytes 12582912 | tf_op jit(solution)/shard_map/pallas_call | solution.py:196
  28.5 21.8 %all-to-all-done = bf16[16,96,768]{2,1,0:T(8,128)(2,1)S(1)} async-done(((bf16[16,96,768]{2,1,0:T(8,128)(2,1)}), bf16[16,96,768]{2,1,0:T(8,128)(2,1)S(1)}, u32[]{:S(2)}, u32[]{:S(2)}) %all-to-all-start) | async-done | bytes 2359328 | tf_op jit(solution)/shard_map/all_to_all | solution.py:414
  50.9 8.7 %shard_map.58 = bf16[8,2,1152,128]{3,2,1,0:T(8,128)(2,1)} custom-call(s32[2]{0:T(128)S(1)} %pad_add_fusion.me_ref, s32[62]{0:T(128)S(1)} %copy-done.2, bf16[12,192,768]{2,1,0:T(8,128)(2,1)} %amp_ref.10, bf16[1536,768]{1,0:T(8,128)(2,1)S(1)} %bitcast.112, bf16[48,256,256]{2,1,0:T(8,128)(2,1)} %get-tuple-element.63.weight_ref), custom_call_target="tpu_custom_call" | custom-call | bytes 16515072 | tf_op jit(solution)/shard_map/pallas_call | solution.py:324
  59.6 3.7 %all-to-all-start.1 = ((bf16[16,48,768]{2,1,0:T(8,128)(2,1)}), bf16[16,48,768]{2,1,0:T(8,128)(2,1)S(1)}, u32[]{:S(2)}, u32[]{:S(2)}) async-start(bf16[16,48,768]{2,1,0:T(8,128)(2,1)} %bitcast.118), calls=%async_computation.2 | async-start | bytes 2359296 | tf_op jit(solution)/shard_map/all_to_all | solution.py:414
  63.4 6.9 %shard_map.59 = (bf16[8,1,384,128]{3,2,1,0:T(8,128)(2,1)S(1)}, bf16[8,1,384,128]{3,2,1,0:T(8,128)(2,1)}) custom-call(s32[2]{0:T(128)S(1)} %pad_add_fusion.1.me_ref, s32[62]{0:T(128)S(1)} %copy-done.3, bf16[12,192,768]{2,1,0:T(8,128)(2,1)} %amp_ref.10, bf16[1536,768]{1,0:T(8,128)(2,1)S(1)} %bitcast.113, bf16[48,256,256]{2,1,0:T(8,128)(2,1)} %get-tuple-element.63.weight_ref), custom_call_target="tpu_custom_call" | custom-call | bytes 5505024 | tf_op jit(solution)/shard_map/pallas_call | solution.py:324
  71.2 1.2 collective-permute-start.2
  72.4 10.8 %all-to-all-done.1 = bf16[16,48,768]{2,1,0:T(8,128)(2,1)S(1)} async-done(((bf16[16,48,768]{2,1,0:T(8,128)(2,1)}), bf16[16,48,768]{2,1,0:T(8,128)(2,1)S(1)}, u32[]{:S(2)}, u32[]{:S(2)}) %all-to-all-start.1) | async-done | bytes 1179680 | tf_op jit(solution)/shard_map/all_to_all | solution.py:414
  83.2 7.3 %shard_map.60 = (bf16[8,1,384,128]{3,2,1,0:T(8,128)(2,1)S(1)}, bf16[8,1,384,128]{3,2,1,0:T(8,128)(2,1)S(1)}) custom-call(s32[2]{0:T(128)S(1)} %pad_add_fusion.1.me_ref, s32[62]{0:T(128)S(1)} %copy-done.3, bf16[12,192,768]{2,1,0:T(8,128)(2,1)} %amp_ref.10, bf16[768,768]{1,0:T(8,128)(2,1)S(1)} %bitcast.114, bf16[48,256,256]{2,1,0:T(8,128)(2,1)} %get-tuple-element.63.weight_ref), custom_call_target="tpu_custom_call" | custom-call | bytes 5505024 | tf_op jit(solution)/shard_map/pallas_call | solution.py:324
  90.5 1.5 collective-permute-start.3
  92.8 7.2 %shard_map.61 = bf16[8,2,384,128]{3,2,1,0:T(8,128)(2,1)S(1)} custom-call(s32[2]{0:T(128)S(1)} %pad_add_fusion.1.me_ref, s32[62]{0:T(128)S(1)} %copy-done.3, bf16[12,192,768]{2,1,0:T(8,128)(2,1)} %amp_ref.10, bf16[768,768]{1,0:T(8,128)(2,1)S(1)} %bitcast.115, bf16[48,256,256]{2,1,0:T(8,128)(2,1)} %get-tuple-element.63.weight_ref), custom_call_target="tpu_custom_call" | custom-call | bytes 5505024 | tf_op jit(solution)/shard_map/pallas_call | solution.py:324
  100.0 1.6 collective-permute-start
  101.6 4.3 %collective-permute-start.1 = (bf16[1,384,128]{2,1,0:T(8,128)(2,1)S(1)}, bf16[1,384,128]{2,1,0:T(8,128)(2,1)S(1)}, u32[]{:S(2)}, u32[]{:S(2)}) collective-permute-start(bf16[1,384,128]{2,1,0:T(8,128)(2,1)S(1)} %get-tuple-element.71), channel_id=1, source_target_pairs={{2,0},{4,2},{6,4},{8,6},{10,8},{12,10},{14,12},{0,14},{3,1},{5,3},... | collective-permute-start | bytes 294920 | tf_op jit(solution)/shard_map/ppermute | solution.py:428
  105.9 5.2 %collective-permute-done = bf16[1,384,128]{2,1,0:T(8,128)(2,1)S(1)} collective-permute-done((bf16[1,384,128]{2,1,0:T(8,128)(2,1)S(1)}, bf16[1,384,128]{2,1,0:T(8,128)(2,1)S(1)}, u32[]{:S(2)}, u32[]{:S(2)}) %collective-permute-start) | collective-permute-done | bytes 98336 | tf_op jit(solution)/shard_map/ppermute | solution.py:428
  111.1 1.8 %collective-permute-done.3 = bf16[8,1,384,128]{3,2,1,0:T(8,128)(2,1)S(1)} collective-permute-done((bf16[8,1,384,128]{3,2,1,0:T(8,128)(2,1)S(1)}, bf16[8,1,384,128]{3,2,1,0:T(8,128)(2,1)S(1)}, u32[]{:S(2)}, u32[]{:S(2)}) %collective-permute-start.3) | collective-permute-done | bytes 786464 | tf_op jit(solution)/shard_map/ppermute | solution.py:473
  113.9 1.8 %collective-permute-start.4 = (bf16[1,384,128]{2,1,0:T(8,128)(2,1)S(1)}, bf16[1,384,128]{2,1,0:T(8,128)(2,1)S(1)}, u32[]{:S(2)}, u32[]{:S(2)}) collective-permute-start(bf16[1,384,128]{2,1,0:T(8,128)(2,1)S(1)} %fusion.7), channel_id=1, source_target_pairs={{0,2},{2,4},{4,6},{6,8},{8,10},{10,12},{12,14},{14,0},{1,3},{3,5},... | collective-permute-start | bytes 294920 | tf_op jit(solution)/shard_map/ppermute | solution.py:428
  115.7 4.2 %collective-permute-start.5 = (bf16[1,384,128]{2,1,0:T(8,128)(2,1)S(1)}, bf16[1,384,128]{2,1,0:T(8,128)(2,1)S(1)}, u32[]{:S(2)}, u32[]{:S(2)}) collective-permute-start(bf16[1,384,128]{2,1,0:T(8,128)(2,1)S(1)} %fusion.8), channel_id=1, source_target_pairs={{2,0},{4,2},{6,4},{8,6},{10,8},{12,10},{14,12},{0,14},{3,1},{5,3},... | collective-permute-start | bytes 294920 | tf_op jit(solution)/shard_map/ppermute | solution.py:428
  119.9 1.3 slice_bitcast_fusion.12
  121.3 3.2 %collective-permute-start.11 = (bf16[2,384,128]{2,1,0:T(8,128)(2,1)S(1)}, bf16[2,384,128]{2,1,0:T(8,128)(2,1)S(1)}, u32[]{:S(2)}, u32[]{:S(2)}) collective-permute-start(bf16[2,384,128]{2,1,0:T(8,128)(2,1)S(1)} %get-tuple-element.93), channel_id=1, source_target_pairs={{2,0},{4,2},{6,4},{8,6},{10,8},{12,10},{14,12},{0,14},{3,1},{5,3},... | collective-permute-start | bytes 589832 | tf_op jit(solution)/shard_map/ppermute | solution.py:428
  124.8 3.2 %collective-permute-start.7 = (bf16[2,384,128]{2,1,0:T(8,128)(2,1)S(1)}, bf16[2,384,128]{2,1,0:T(8,128)(2,1)S(1)}, u32[]{:S(2)}, u32[]{:S(2)}) collective-permute-start(bf16[2,384,128]{2,1,0:T(8,128)(2,1)S(1)} %add_convert_fusion.4), channel_id=1, source_target_pairs={{2,0},{4,2},{6,4},{8,6},{10,8},{12,10},{14,12},{0,14},{3,1},{5,3},... | collective-permute-start | bytes 589832 | tf_op jit(solution)/shard_map/ppermute | solution.py:428
  128.0 2.2 %collective-permute-done.10 = bf16[2,384,128]{2,1,0:T(8,128)(2,1)S(1)} collective-permute-done((bf16[2,384,128]{2,1,0:T(8,128)(2,1)S(1)}, bf16[2,384,128]{2,1,0:T(8,128)(2,1)S(1)}, u32[]{:S(2)}, u32[]{:S(2)}) %collective-permute-start.10) | collective-permute-done | bytes 196640 | tf_op jit(solution)/shard_map/ppermute | solution.py:428
  130.4 3.3 %collective-permute-start.13 = (bf16[2,384,128]{2,1,0:T(8,128)(2,1)S(1)}, bf16[2,384,128]{2,1,0:T(8,128)(2,1)S(1)}, u32[]{:S(2)}, u32[]{:S(2)}) collective-permute-start(bf16[2,384,128]{2,1,0:T(8,128)(2,1)S(1)} %get-tuple-element.97), channel_id=1, source_target_pairs={{2,0},{4,2},{6,4},{8,6},{10,8},{12,10},{14,12},{0,14},{3,1},{5,3},... | collective-permute-start | bytes 589832 | tf_op jit(solution)/shard_map/ppermute | solution.py:428
  136.0 3.2 %collective-permute-start.9 = (bf16[2,384,128]{2,1,0:T(8,128)(2,1)}, bf16[2,384,128]{2,1,0:T(8,128)(2,1)S(1)}, u32[]{:S(2)}, u32[]{:S(2)}) collective-permute-start(bf16[2,384,128]{2,1,0:T(8,128)(2,1)} %add_convert_fusion.2), channel_id=1, source_target_pairs={{2,0},{4,2},{6,4},{8,6},{10,8},{12,10},{14,12},{0,14},{3,1},{5,3},... | collective-permute-start | bytes 589832 | tf_op jit(solution)/shard_map/ppermute | solution.py:428
  139.2 1.0 slice_bitcast_fusion
  141.1 3.0 %collective-permute-start.15 = (bf16[2,384,128]{2,1,0:T(8,128)(2,1)S(1)}, bf16[2,384,128]{2,1,0:T(8,128)(2,1)S(1)}, u32[]{:S(2)}, u32[]{:S(2)}) collective-permute-start(bf16[2,384,128]{2,1,0:T(8,128)(2,1)S(1)} %get-tuple-element.101), channel_id=1, source_target_pairs={{2,0},{4,2},{6,4},{8,6},{10,8},{12,10},{14,12},{0,14},{3,1},{5,3},... | collective-permute-start | bytes 589832 | tf_op jit(solution)/shard_map/ppermute | solution.py:428
  144.7 3.0 %collective-permute-done.14 = bf16[2,384,128]{2,1,0:T(8,128)(2,1)S(1)} collective-permute-done((bf16[2,384,128]{2,1,0:T(8,128)(2,1)S(1)}, bf16[2,384,128]{2,1,0:T(8,128)(2,1)S(1)}, u32[]{:S(2)}, u32[]{:S(2)}) %collective-permute-start.14) | collective-permute-done | bytes 196640 | tf_op jit(solution)/shard_map/ppermute | solution.py:428
  148.0 1.7 %collective-permute-start.19 = (bf16[384,128]{1,0:T(8,128)(2,1)S(1)}, bf16[384,128]{1,0:T(8,128)(2,1)S(1)}, u32[]{:S(2)}, u32[]{:S(2)}) collective-permute-start(bf16[384,128]{1,0:T(8,128)(2,1)S(1)} %fusion.9), channel_id=1, source_target_pairs={{0,1},{1,0},{2,3},{3,2},{4,5},{5,4},{6,7},{7,6},{8,9},{9,8},{10,11... | collective-permute-start | bytes 294920 | tf_op jit(solution)/shard_map/ppermute | solution.py:495
  150.6 2.3 %collective-permute-start.18 = (bf16[2,384,128]{2,1,0:T(8,128)(2,1)S(1)}, bf16[2,384,128]{2,1,0:T(8,128)(2,1)S(1)}, u32[]{:S(2)}, u32[]{:S(2)}) collective-permute-start(bf16[2,384,128]{2,1,0:T(8,128)(2,1)S(1)} %get-tuple-element.108), channel_id=1, source_target_pairs={{2,0},{4,2},{6,4},{8,6},{10,8},{12,10},{14,12},{0,14},{3,1},{5,3},... | collective-permute-start | bytes 589832 | tf_op jit(solution)/shard_map/ppermute | solution.py:428
  153.0 1.9 %shard_map.62.done_ref = bf16[128,2304]{1,0:T(8,128)(2,1)} custom-call(bf16[1,2,1152,128]{3,2,1,0:T(8,128)(2,1)} %reduce-scatter.2.cloned.1.call-done.near, bf16[1152,128]{1,0:T(8,128)(2,1)} %copy-done.7), custom_call_target="tpu_custom_call" | custom-call | tf_op jit(solution)/shard_map/pallas_call | solution.py:361
  155.0 1.7 %collective-permute-done.17.up_ref = bf16[2,384,128]{2,1,0:T(8,128)(2,1)S(1)} collective-permute-done((bf16[2,384,128]{2,1,0:T(8,128)(2,1)S(1)}, bf16[2,384,128]{2,1,0:T(8,128)(2,1)S(1)}, u32[]{:S(2)}, u32[]{:S(2)}) %collective-permute-start.17) | collective-permute-done | bytes 196640 | tf_op jit(solution)/shard_map/ppermute | solution.py:428
  (62 shorter events, 9.9 us)
Async XLA Ops:
  11.8 38.6 %all-to-all-start = ((bf16[16,96,768]{2,1,0:T(8,128)(2,1)}), bf16[16,96,768]{2,1,0:T(8,128)(2,1)S(1)}, u32[]{:S(2)}, u32[]{:S(2)}) async-start(bf16[16,96,768]{2,1,0:T(8,128)(2,1)} %bitcast.117), calls=%async_computation | async-start | bytes 4718592 | tf_op jit(solution)/shard_map/all_to_all | solution.py:414
  17.9 121.3 %reduce-scatter.2.cloned.1.call-start = ((), (), s32[]{:S(2)}) async-start(), calls=%async_computation.3 | async-start | bytes 5308416 | tf_op jit(solution)/shard_map/reduce_scatter | solution.py:417
  50.3 0.6 copy-start.2
  59.6 3.8 %copy-start.3 = (s32[62]{0:T(128)S(1)}, s32[62]{0:T(128)}, u32[]{:S(2)}) copy-start(s32[62]{0:T(128)} %get-tuple-element.59.lists) | copy-start | bytes 748
  59.6 23.6 %all-to-all-start.1 = ((bf16[16,48,768]{2,1,0:T(8,128)(2,1)}), bf16[16,48,768]{2,1,0:T(8,128)(2,1)S(1)}, u32[]{:S(2)}, u32[]{:S(2)}) async-start(bf16[16,48,768]{2,1,0:T(8,128)(2,1)} %bitcast.118), calls=%async_computation.2 | async-start | bytes 2359296 | tf_op jit(solution)/shard_map/all_to_all | solution.py:414
  70.3 0.9 copy-start
  71.2 39.9 %collective-permute-start.2 = (bf16[8,1,384,128]{3,2,1,0:T(8,128)(2,1)}, bf16[8,1,384,128]{3,2,1,0:T(8,128)(2,1)}, u32[]{:S(2)}, u32[]{:S(2)}) collective-permute-start(bf16[8,1,384,128]{3,2,1,0:T(8,128)(2,1)} %get-tuple-element.74), channel_id=1, source_target_pairs={{0,1},{1,0},{2,3},{3,2},{4,5},{5,4},{6,7},{7,6},{8,9},{9,8},{10,11... | collective-permute-start | bytes 2359304 | tf_op jit(solution)/shard_map/ppermute | solution.py:470
  83.2 8.8 %copy-start.1 = (bf16[8,1,384,128]{3,2,1,0:T(8,128)(2,1)S(1)}, bf16[8,1,384,128]{3,2,1,0:T(8,128)(2,1)}, u32[]{:S(2)}) copy-start(bf16[8,1,384,128]{3,2,1,0:T(8,128)(2,1)} %copy-done) | copy-start | bytes 2359300
  90.5 22.4 %collective-permute-start.3 = (bf16[8,1,384,128]{3,2,1,0:T(8,128)(2,1)S(1)}, bf16[8,1,384,128]{3,2,1,0:T(8,128)(2,1)S(1)}, u32[]{:S(2)}, u32[]{:S(2)}) collective-permute-start(bf16[8,1,384,128]{3,2,1,0:T(8,128)(2,1)S(1)} %get-tuple-element.75), channel_id=1, source_target_pairs={{0,1},{1,0},{2,3},{3,2},{4,5},{5,4},{6,7},{7,6},{8,9},{9,8},{10,11... | collective-permute-start | bytes 2359304 | tf_op jit(solution)/shard_map/ppermute | solution.py:473
  100.0 11.1 %collective-permute-start = (bf16[1,384,128]{2,1,0:T(8,128)(2,1)S(1)}, bf16[1,384,128]{2,1,0:T(8,128)(2,1)S(1)}, u32[]{:S(2)}, u32[]{:S(2)}) collective-permute-start(bf16[1,384,128]{2,1,0:T(8,128)(2,1)S(1)} %get-tuple-element.70), channel_id=1, source_target_pairs={{0,2},{2,4},{4,6},{6,8},{8,10},{10,12},{12,14},{14,0},{1,3},{3,5},... | collective-permute-start | bytes 294920 | tf_op jit(solution)/shard_map/ppermute | solution.py:428
  101.6 9.5 %collective-permute-start.1 = (bf16[1,384,128]{2,1,0:T(8,128)(2,1)S(1)}, bf16[1,384,128]{2,1,0:T(8,128)(2,1)S(1)}, u32[]{:S(2)}, u32[]{:S(2)}) collective-permute-start(bf16[1,384,128]{2,1,0:T(8,128)(2,1)S(1)} %get-tuple-element.71), channel_id=1, source_target_pairs={{2,0},{4,2},{6,4},{8,6},{10,8},{12,10},{14,12},{0,14},{3,1},{5,3},... | collective-permute-start | bytes 294920 | tf_op jit(solution)/shard_map/ppermute | solution.py:428
  113.9 10.7 %collective-permute-start.4 = (bf16[1,384,128]{2,1,0:T(8,128)(2,1)S(1)}, bf16[1,384,128]{2,1,0:T(8,128)(2,1)S(1)}, u32[]{:S(2)}, u32[]{:S(2)}) collective-permute-start(bf16[1,384,128]{2,1,0:T(8,128)(2,1)S(1)} %fusion.7), channel_id=1, source_target_pairs={{0,2},{2,4},{4,6},{6,8},{8,10},{10,12},{12,14},{14,0},{1,3},{3,5},... | collective-permute-start | bytes 294920 | tf_op jit(solution)/shard_map/ppermute | solution.py:428
  115.7 8.9 %collective-permute-start.5 = (bf16[1,384,128]{2,1,0:T(8,128)(2,1)S(1)}, bf16[1,384,128]{2,1,0:T(8,128)(2,1)S(1)}, u32[]{:S(2)}, u32[]{:S(2)}) collective-permute-start(bf16[1,384,128]{2,1,0:T(8,128)(2,1)S(1)} %fusion.8), channel_id=1, source_target_pairs={{2,0},{4,2},{6,4},{8,6},{10,8},{12,10},{14,12},{0,14},{3,1},{5,3},... | collective-permute-start | bytes 294920 | tf_op jit(solution)/shard_map/ppermute | solution.py:428
  121.2 9.0 %collective-permute-start.10 = (bf16[2,384,128]{2,1,0:T(8,128)(2,1)S(1)}, bf16[2,384,128]{2,1,0:T(8,128)(2,1)S(1)}, u32[]{:S(2)}, u32[]{:S(2)}) collective-permute-start(bf16[2,384,128]{2,1,0:T(8,128)(2,1)S(1)} %get-tuple-element.92), channel_id=1, source_target_pairs={{0,2},{2,4},{4,6},{6,8},{8,10},{10,12},{12,14},{14,0},{1,3},{3,5},... | collective-permute-start | bytes 589832 | tf_op jit(solution)/shard_map/ppermute | solution.py:428
  121.3 8.9 %collective-permute-start.11 = (bf16[2,384,128]{2,1,0:T(8,128)(2,1)S(1)}, bf16[2,384,128]{2,1,0:T(8,128)(2,1)S(1)}, u32[]{:S(2)}, u32[]{:S(2)}) collective-permute-start(bf16[2,384,128]{2,1,0:T(8,128)(2,1)S(1)} %get-tuple-element.93), channel_id=1, source_target_pairs={{2,0},{4,2},{6,4},{8,6},{10,8},{12,10},{14,12},{0,14},{3,1},{5,3},... | collective-permute-start | bytes 589832 | tf_op jit(solution)/shard_map/ppermute | solution.py:428
  124.7 9.7 %collective-permute-start.6 = (bf16[2,384,128]{2,1,0:T(8,128)(2,1)S(1)}, bf16[2,384,128]{2,1,0:T(8,128)(2,1)S(1)}, u32[]{:S(2)}, u32[]{:S(2)}) collective-permute-start(bf16[2,384,128]{2,1,0:T(8,128)(2,1)S(1)} %add_convert_fusion.5), channel_id=1, source_target_pairs={{0,2},{2,4},{4,6},{6,8},{8,10},{10,12},{12,14},{14,0},{1,3},{3,5},... | collective-permute-start | bytes 589832 | tf_op jit(solution)/shard_map/ppermute | solution.py:428
  124.8 9.6 %collective-permute-start.7 = (bf16[2,384,128]{2,1,0:T(8,128)(2,1)S(1)}, bf16[2,384,128]{2,1,0:T(8,128)(2,1)S(1)}, u32[]{:S(2)}, u32[]{:S(2)}) collective-permute-start(bf16[2,384,128]{2,1,0:T(8,128)(2,1)S(1)} %add_convert_fusion.4), channel_id=1, source_target_pairs={{2,0},{4,2},{6,4},{8,6},{10,8},{12,10},{14,12},{0,14},{3,1},{5,3},... | collective-permute-start | bytes 589832 | tf_op jit(solution)/shard_map/ppermute | solution.py:428
  130.3 8.9 %collective-permute-start.12 = (bf16[2,384,128]{2,1,0:T(8,128)(2,1)S(1)}, bf16[2,384,128]{2,1,0:T(8,128)(2,1)S(1)}, u32[]{:S(2)}, u32[]{:S(2)}) collective-permute-start(bf16[2,384,128]{2,1,0:T(8,128)(2,1)S(1)} %get-tuple-element.96), channel_id=1, source_target_pairs={{0,2},{2,4},{4,6},{6,8},{8,10},{10,12},{12,14},{14,0},{1,3},{3,5},... | collective-permute-start | bytes 589832 | tf_op jit(solution)/shard_map/ppermute | solution.py:428
  130.4 8.8 %collective-permute-start.13 = (bf16[2,384,128]{2,1,0:T(8,128)(2,1)S(1)}, bf16[2,384,128]{2,1,0:T(8,128)(2,1)S(1)}, u32[]{:S(2)}, u32[]{:S(2)}) collective-permute-start(bf16[2,384,128]{2,1,0:T(8,128)(2,1)S(1)} %get-tuple-element.97), channel_id=1, source_target_pairs={{2,0},{4,2},{6,4},{8,6},{10,8},{12,10},{14,12},{0,14},{3,1},{5,3},... | collective-permute-start | bytes 589832 | tf_op jit(solution)/shard_map/ppermute | solution.py:428
  134.4 9.7 %copy-start.6 = (bf16[1,384,128]{2,1,0:T(8,128)(2,1)S(1)}, bf16[1,384,128]{2,1,0:T(8,128)(2,1)}, u32[]{:S(2)}) copy-start(bf16[1,384,128]{2,1,0:T(8,128)(2,1)} %get-tuple-element.137) | copy-start | bytes 294916
  135.2 12.6 %copy-start.4 = (bf16[1,384,128]{2,1,0:T(8,128)(2,1)S(1)}, bf16[1,384,128]{2,1,0:T(8,128)(2,1)}, u32[]{:S(2)}) copy-start(bf16[1,384,128]{2,1,0:T(8,128)(2,1)} %get-tuple-element.135) | copy-start | bytes 294916
  135.2 12.6 %copy-start.5 = (bf16[1,384,128]{2,1,0:T(8,128)(2,1)S(1)}, bf16[1,384,128]{2,1,0:T(8,128)(2,1)}, u32[]{:S(2)}) copy-start(bf16[1,384,128]{2,1,0:T(8,128)(2,1)} %get-tuple-element.136) | copy-start | bytes 294916
  135.9 8.7 %collective-permute-start.8 = (bf16[2,384,128]{2,1,0:T(8,128)(2,1)}, bf16[2,384,128]{2,1,0:T(8,128)(2,1)S(1)}, u32[]{:S(2)}, u32[]{:S(2)}) collective-permute-start(bf16[2,384,128]{2,1,0:T(8,128)(2,1)} %add_convert_fusion.3), channel_id=1, source_target_pairs={{0,2},{2,4},{4,6},{6,8},{8,10},{10,12},{12,14},{14,0},{1,3},{3,5},... | collective-permute-start | bytes 589832 | tf_op jit(solution)/shard_map/ppermute | solution.py:428
  136.0 8.7 %collective-permute-start.9 = (bf16[2,384,128]{2,1,0:T(8,128)(2,1)}, bf16[2,384,128]{2,1,0:T(8,128)(2,1)S(1)}, u32[]{:S(2)}, u32[]{:S(2)}) collective-permute-start(bf16[2,384,128]{2,1,0:T(8,128)(2,1)} %add_convert_fusion.2), channel_id=1, source_target_pairs={{2,0},{4,2},{6,4},{8,6},{10,8},{12,10},{14,12},{0,14},{3,1},{5,3},... | collective-permute-start | bytes 589832 | tf_op jit(solution)/shard_map/ppermute | solution.py:428
  140.2 7.5 %collective-permute-start.16 = (bf16[1152,128]{1,0:T(8,128)(2,1)S(1)}, bf16[1152,128]{1,0:T(8,128)(2,1)S(1)}, u32[]{:S(2)}, u32[]{:S(2)}) collective-permute-start(bf16[1152,128]{1,0:T(8,128)(2,1)S(1)} %slice_bitcast_fusion), channel_id=1, source_target_pairs={{0,1},{1,0},{2,3},{3,2},{4,5},{5,4},{6,7},{7,6},{8,9},{9,8},{10,11... | collective-permute-start | bytes 884744 | tf_op jit(solution)/shard_map/ppermute | solution.py:489
  140.8 7.0 %collective-permute-start.14 = (bf16[2,384,128]{2,1,0:T(8,128)(2,1)S(1)}, bf16[2,384,128]{2,1,0:T(8,128)(2,1)S(1)}, u32[]{:S(2)}, u32[]{:S(2)}) collective-permute-start(bf16[2,384,128]{2,1,0:T(8,128)(2,1)S(1)} %get-tuple-element.100), channel_id=1, source_target_pairs={{0,2},{2,4},{4,6},{6,8},{8,10},{10,12},{12,14},{14,0},{1,3},{3,5},... | collective-permute-start | bytes 589832 | tf_op jit(solution)/shard_map/ppermute | solution.py:428
  141.1 6.6 %collective-permute-start.15 = (bf16[2,384,128]{2,1,0:T(8,128)(2,1)S(1)}, bf16[2,384,128]{2,1,0:T(8,128)(2,1)S(1)}, u32[]{:S(2)}, u32[]{:S(2)}) collective-permute-start(bf16[2,384,128]{2,1,0:T(8,128)(2,1)S(1)} %get-tuple-element.101), channel_id=1, source_target_pairs={{2,0},{4,2},{6,4},{8,6},{10,8},{12,10},{14,12},{0,14},{3,1},{5,3},... | collective-permute-start | bytes 589832 | tf_op jit(solution)/shard_map/ppermute | solution.py:428
  147.7 5.3 %copy-start.7 = (bf16[1152,128]{1,0:T(8,128)(2,1)}, bf16[1152,128]{1,0:T(8,128)(2,1)S(1)}, u32[]{:S(2)}) copy-start(bf16[1152,128]{1,0:T(8,128)(2,1)S(1)} %collective-permute-done.16.far) | copy-start | bytes 884740
  148.0 8.6 %collective-permute-start.19 = (bf16[384,128]{1,0:T(8,128)(2,1)S(1)}, bf16[384,128]{1,0:T(8,128)(2,1)S(1)}, u32[]{:S(2)}, u32[]{:S(2)}) collective-permute-start(bf16[384,128]{1,0:T(8,128)(2,1)S(1)} %fusion.9), channel_id=1, source_target_pairs={{0,1},{1,0},{2,3},{3,2},{4,5},{5,4},{6,7},{7,6},{8,9},{9,8},{10,11... | collective-permute-start | bytes 294920 | tf_op jit(solution)/shard_map/ppermute | solution.py:495
  149.7 6.9 %collective-permute-start.17 = (bf16[2,384,128]{2,1,0:T(8,128)(2,1)S(1)}, bf16[2,384,128]{2,1,0:T(8,128)(2,1)S(1)}, u32[]{:S(2)}, u32[]{:S(2)}) collective-permute-start(bf16[2,384,128]{2,1,0:T(8,128)(2,1)S(1)} %get-tuple-element.107), channel_id=1, source_target_pairs={{0,2},{2,4},{4,6},{6,8},{8,10},{10,12},{12,14},{14,0},{1,3},{3,5},... | collective-permute-start | bytes 589832 | tf_op jit(solution)/shard_map/ppermute | solution.py:428
  150.6 6.0 %collective-permute-start.18 = (bf16[2,384,128]{2,1,0:T(8,128)(2,1)S(1)}, bf16[2,384,128]{2,1,0:T(8,128)(2,1)S(1)}, u32[]{:S(2)}, u32[]{:S(2)}) collective-permute-start(bf16[2,384,128]{2,1,0:T(8,128)(2,1)S(1)} %get-tuple-element.108), channel_id=1, source_target_pairs={{2,0},{4,2},{6,4},{8,6},{10,8},{12,10},{14,12},{0,14},{3,1},{5,3},... | collective-permute-start | bytes 589832 | tf_op jit(solution)/shard_map/ppermute | solution.py:428
Sparse Core Ops, SparseCore 0:
  59.8 62.1 reduce-scatter.1

commit v10 on v9

--- a/solution.py
+++ b/solution.py
@@ -469,10 +469,10 @@
     near0, far0 = product(turned, received0, 0, FIRST - UNIT, UNIT, 0)
     far0 = swap(far0)
     received1, _ = lax.optimization_barrier((received1, near0))
+    (terms1,) = product(turned, received1, FIRST, UNIT, rest - UNIT, N_X)
+    received1, _ = lax.optimization_barrier((received1, terms1))
     near1, far1 = product(turned, received1, FIRST, 0, UNIT, 0)
     far1 = swap(far1)
-    received1, _ = lax.optimization_barrier((received1, near1))
-    (terms1,) = product(turned, received1, FIRST, UNIT, rest - UNIT, N_X)
 
     def late(k):
         return (terms1[k],)
@@ -480,17 +480,16 @@
     def early(k):
         return [jnp.concatenate(pair, 0) for pair in ((near0[k], near1[k]), (far0[k], far1[k]))]
 
-    late_ring = set_out(late)
+    late_ring = go_on(late, 1, *set_out(late))
     late_ring, far0, far1 = lax.optimization_barrier((late_ring, far0, far1))
     early_ring = set_out(early)
-    for step in range(1, half):
+    for step in range(2, half):
         late_ring = go_on(late, step, *late_ring)
         if step == half - 1:
             last0 = swap(sum0[0, 1])
-            early_ring, late_ring, last0 = lax.optimization_barrier(
-                (early_ring, late_ring, last0)
-            )
-        early_ring = go_on(early, step, *early_ring)
+            early_ring, last0 = lax.optimization_barrier((early_ring, last0))
+        early_ring = go_on(early, step - 1, *early_ring)
+    early_ring = go_on(early, half - 1, *early_ring)
     late_sum = add(terms1[0], *late_ring)
     far_late = swap(late_sum[1].astype(jnp.bfloat16))
     done = finish_first(sum0, last0)

time: 166 us -> 174 us (1.048)
  waiting for transfers between devices: 47.8 us -> 60.5 us
  starting transfers between devices: 46.4 us -> 43 us
  other arithmetic: 3.3 us -> 6.12 us
  Pallas kernels: 48.5 us -> 46.2 us
    ppermute x16, waiting for transfers between devices: 13.4 us -> 24 us  [send(): return lax.optimization_barrier((up(pair[0]), down(pair[1])))]
    ppermute x1, waiting for transfers between devices: 0.01 us -> 2.74 us  [on_device(): last0 = swap(sum0[0, 1])]
    pallas_call x4, Pallas kernels: 30.1 us -> 27.9 us  [ladder(): pl.pallas_call(functools.partial(ladder_kernel, begin, first), in_specs=[...]
    ppermute x16, starting transfers between devices: 31.6 us -> 29.7 us  [send(): return lax.optimization_barrier((up(pair[0]), down(pair[1])))]
    convert_element_type x10, other arithmetic: 3.04 us -> 4.84 us  [send(): p.astype(jnp.bfloat16)]
    ppermute x1, waiting for transfers between devices: 1.77 us -> 0.01 us  [on_device(): far1 = swap(far1)]
  transfers between devices with their start and end apart: 23 -> 23, of which waited for: 9 -> 13; matrix products, arithmetic and copies ran while one was open for 4% -> 3% of each run, Pallas kernels for 21% -> 18%
where the time goes in v10:
time: 174 us; the launch traced here: 173 us
  waiting for transfers between devices  60.5 us (35%)
  Pallas kernels  46.2 us (27%)
  starting transfers between devices  43 us (25%)
  between operations  13.7 us (8%)
  other arithmetic  6.12 us (4%)
  local copies, waits for them, and re-layouts  3.42 us (2%)
    all_to_all x2, waiting for transfers between devices, exchange(): lax.all_to_all(packed, 'row', split_axis=0, concat_axis=0, tiled=True)  33.6 us
    ppermute x16, starting transfers between devices, send(): return lax.optimization_barrier((up(pair[0]), down(pair[1])))  29.7 us
    pallas_call x4, Pallas kernels, ladder(): pl.pallas_call(functools.partial(ladder_kernel, begin, first), in_specs=[...  27.9 us
    ppermute x16, waiting for transfers between devices, send(): return lax.optimization_barrier((up(pair[0]), down(pair[1])))  24 us
    all_to_all x2, starting transfers between devices, exchange(): lax.all_to_all(packed, 'row', split_axis=0, concat_axis=0, tiled=True)  9.84 us
    pallas_call x2, Pallas kernels, pack(): pl.pallas_call(functools.partial(pack_kernel, first, n_i), in_specs=[hbm]...  9.47 us
    pallas_call x1, Pallas kernels, match(): pl.pallas_call(match_kernel, in_specs=[smem, smem, hbm, hbm], out_specs=[...  5.93 us
    convert_element_type x10, other arithmetic, send(): p.astype(jnp.bfloat16)  4.84 us
  transfers between devices with their start and end apart: 23, of which 13 were waited for; matrix products, arithmetic and copies ran while one was open for 3% of the time, Pallas kernels for 18%

profile of v10, /device:TPU:2, one launch (start us, length us, event | category | flops | bytes accessed | tf_op | source)
XLA Modules:
  0.0 172.8 jit_solution(6892430166674551747)
XLA Ops:
  6.5 5.2 %shard_map.56 = bf16[1536,768]{1,0:T(8,128)(2,1)} custom-call(bf16[12,192,768]{2,1,0:T(8,128)(2,1)} %amp_ref.10), custom_call_target="tpu_custom_call" | custom-call | bytes 7077888 | tf_op jit(solution)/shard_map/pallas_call | solution.py:79
  11.8 6.1 %all-to-all-start = ((bf16[16,96,768]{2,1,0:T(8,128)(2,1)}), bf16[16,96,768]{2,1,0:T(8,128)(2,1)S(1)}, u32[]{:S(2)}, u32[]{:S(2)}) async-start(bf16[16,96,768]{2,1,0:T(8,128)(2,1)} %bitcast.117), calls=%async_computation | async-start | bytes 4718592 | tf_op jit(solution)/shard_map/all_to_all | solution.py:414
  17.9 4.3 %shard_map.57 = bf16[768,768]{1,0:T(8,128)(2,1)} custom-call(bf16[12,192,768]{2,1,0:T(8,128)(2,1)} %amp_ref.10), custom_call_target="tpu_custom_call" | custom-call | bytes 7077888 | tf_op jit(solution)/shard_map/pallas_call | solution.py:79
  22.2 5.9 %shard_map.55 = (s32[62]{0:T(128)}, bf16[48,256,256]{2,1,0:T(8,128)(2,1)}) custom-call(s32[6]{0:T(128)} %cd_ref.1, s32[16]{0:T(128)} %ab_ref.1, bf16[768,2048]{1,0:T(8,128)(2,1)} %plus_ref, bf16[768,2048]{1,0:T(8,128)(2,1)} %minus_ref.1), custom_call_target="tpu_custom_call" | custom-call | bytes 12582912 | tf_op jit(solution)/shard_map/pallas_call | solution.py:196
  28.2 22.1 %all-to-all-done = bf16[16,96,768]{2,1,0:T(8,128)(2,1)S(1)} async-done(((bf16[16,96,768]{2,1,0:T(8,128)(2,1)}), bf16[16,96,768]{2,1,0:T(8,128)(2,1)S(1)}, u32[]{:S(2)}, u32[]{:S(2)}) %all-to-all-start) | async-done | bytes 2359328 | tf_op jit(solution)/shard_map/all_to_all | solution.py:414
  50.9 8.3 %shard_map.58 = bf16[8,2,1152,128]{3,2,1,0:T(8,128)(2,1)} custom-call(s32[2]{0:T(128)S(1)} %pad_add_fusion.me_ref, s32[62]{0:T(128)S(1)} %copy-done.2, bf16[12,192,768]{2,1,0:T(8,128)(2,1)} %amp_ref.10, bf16[1536,768]{1,0:T(8,128)(2,1)S(1)} %bitcast.112, bf16[48,256,256]{2,1,0:T(8,128)(2,1)} %get-tuple-element.61.weight_ref), custom_call_target="tpu_custom_call" | custom-call | bytes 16515072 | tf_op jit(solution)/shard_map/pallas_call | solution.py:324
  59.3 3.7 %all-to-all-start.1 = ((bf16[16,48,768]{2,1,0:T(8,128)(2,1)}), bf16[16,48,768]{2,1,0:T(8,128)(2,1)S(1)}, u32[]{:S(2)}, u32[]{:S(2)}) async-start(bf16[16,48,768]{2,1,0:T(8,128)(2,1)} %bitcast.118), calls=%async_computation.2 | async-start | bytes 2359296 | tf_op jit(solution)/shard_map/all_to_all | solution.py:414
  63.1 5.9 %shard_map.59 = (bf16[8,1,384,128]{3,2,1,0:T(8,128)(2,1)S(1)}, bf16[8,1,384,128]{3,2,1,0:T(8,128)(2,1)}) custom-call(s32[2]{0:T(128)S(1)} %pad_add_fusion.1.me_ref, s32[62]{0:T(128)S(1)} %copy-done.3, bf16[12,192,768]{2,1,0:T(8,128)(2,1)} %amp_ref.10, bf16[1536,768]{1,0:T(8,128)(2,1)S(1)} %bitcast.113, bf16[48,256,256]{2,1,0:T(8,128)(2,1)} %get-tuple-element.61.weight_ref), custom_call_target="tpu_custom_call" | custom-call | bytes 5505024 | tf_op jit(solution)/shard_map/pallas_call | solution.py:324
  69.9 1.4 collective-permute-start.4
  71.3 11.6 %all-to-all-done.1 = bf16[16,48,768]{2,1,0:T(8,128)(2,1)S(1)} async-done(((bf16[16,48,768]{2,1,0:T(8,128)(2,1)}), bf16[16,48,768]{2,1,0:T(8,128)(2,1)S(1)}, u32[]{:S(2)}, u32[]{:S(2)}) %all-to-all-start.1) | async-done | bytes 1179680 | tf_op jit(solution)/shard_map/all_to_all | solution.py:414
  82.9 6.8 %shard_map.60 = bf16[8,2,384,128]{3,2,1,0:T(8,128)(2,1)S(1)} custom-call(s32[2]{0:T(128)S(1)} %pad_add_fusion.1.me_ref, s32[62]{0:T(128)S(1)} %copy-done.3, bf16[12,192,768]{2,1,0:T(8,128)(2,1)} %amp_ref.10, bf16[768,768]{1,0:T(8,128)(2,1)S(1)} %bitcast.114, bf16[48,256,256]{2,1,0:T(8,128)(2,1)} %get-tuple-element.61.weight_ref), custom_call_target="tpu_custom_call" | custom-call | bytes 5505024 | tf_op jit(solution)/shard_map/pallas_call | solution.py:324
  89.7 6.9 %shard_map.61 = (bf16[8,1,384,128]{3,2,1,0:T(8,128)(2,1)S(1)}, bf16[8,1,384,128]{3,2,1,0:T(8,128)(2,1)S(1)}) custom-call(s32[2]{0:T(128)S(1)} %pad_add_fusion.1.me_ref, s32[62]{0:T(128)S(1)} %copy-done.3, bf16[12,192,768]{2,1,0:T(8,128)(2,1)} %amp_ref.10, bf16[768,768]{1,0:T(8,128)(2,1)S(1)} %bitcast.115, bf16[48,256,256]{2,1,0:T(8,128)(2,1)} %get-tuple-element.61.weight_ref), custom_call_target="tpu_custom_call" | custom-call | bytes 5505024 | tf_op jit(solution)/shard_map/pallas_call | solution.py:324
  97.1 2.0 %collective-permute-start = (bf16[1,384,128]{2,1,0:T(8,128)(2,1)S(1)}, bf16[1,384,128]{2,1,0:T(8,128)(2,1)S(1)}, u32[]{:S(2)}, u32[]{:S(2)}) collective-permute-start(bf16[1,384,128]{2,1,0:T(8,128)(2,1)S(1)} %get-tuple-element.66), channel_id=1, source_target_pairs={{0,2},{2,4},{4,6},{6,8},{8,10},{10,12},{12,14},{14,0},{1,3},{3,5},... | collective-permute-start | bytes 294920 | tf_op jit(solution)/shard_map/ppermute | solution.py:428
  99.1 4.7 %collective-permute-start.1 = (bf16[1,384,128]{2,1,0:T(8,128)(2,1)S(1)}, bf16[1,384,128]{2,1,0:T(8,128)(2,1)S(1)}, u32[]{:S(2)}, u32[]{:S(2)}) collective-permute-start(bf16[1,384,128]{2,1,0:T(8,128)(2,1)S(1)} %get-tuple-element.67), channel_id=1, source_target_pairs={{2,0},{4,2},{6,4},{8,6},{10,8},{12,10},{14,12},{0,14},{3,1},{5,3},... | collective-permute-start | bytes 294920 | tf_op jit(solution)/shard_map/ppermute | solution.py:428
  103.9 5.2 %collective-permute-done = bf16[1,384,128]{2,1,0:T(8,128)(2,1)S(1)} collective-permute-done((bf16[1,384,128]{2,1,0:T(8,128)(2,1)S(1)}, bf16[1,384,128]{2,1,0:T(8,128)(2,1)S(1)}, u32[]{:S(2)}, u32[]{:S(2)}) %collective-permute-start) | collective-permute-done | bytes 98336 | tf_op jit(solution)/shard_map/ppermute | solution.py:428
  109.2 3.2 %collective-permute-start.3 = (bf16[2,384,128]{2,1,0:T(8,128)(2,1)S(1)}, bf16[2,384,128]{2,1,0:T(8,128)(2,1)S(1)}, u32[]{:S(2)}, u32[]{:S(2)}) collective-permute-start(bf16[2,384,128]{2,1,0:T(8,128)(2,1)S(1)} %get-tuple-element.71), channel_id=1, source_target_pairs={{2,0},{4,2},{6,4},{8,6},{10,8},{12,10},{14,12},{0,14},{3,1},{5,3},... | collective-permute-start | bytes 589832 | tf_op jit(solution)/shard_map/ppermute | solution.py:428
  112.5 9.2 %collective-permute-done.2 = bf16[2,384,128]{2,1,0:T(8,128)(2,1)S(1)} collective-permute-done((bf16[2,384,128]{2,1,0:T(8,128)(2,1)S(1)}, bf16[2,384,128]{2,1,0:T(8,128)(2,1)S(1)}, u32[]{:S(2)}, u32[]{:S(2)}) %collective-permute-start.2) | collective-permute-done | bytes 196640 | tf_op jit(solution)/shard_map/ppermute | solution.py:428
  121.8 2.6 %collective-permute-start.6 = (bf16[1,384,128]{2,1,0:T(8,128)(2,1)S(1)}, bf16[1,384,128]{2,1,0:T(8,128)(2,1)S(1)}, u32[]{:S(2)}, u32[]{:S(2)}) collective-permute-start(bf16[1,384,128]{2,1,0:T(8,128)(2,1)S(1)} %fusion.7), channel_id=1, source_target_pairs={{0,2},{2,4},{4,6},{6,8},{8,10},{10,12},{12,14},{14,0},{1,3},{3,5},... | collective-permute-start | bytes 294920 | tf_op jit(solution)/shard_map/ppermute | solution.py:428
  126.0 1.4 collective-permute-start.15
  127.4 1.9 %collective-permute-start.16 = (bf16[2,384,128]{2,1,0:T(8,128)(2,1)S(1)}, bf16[2,384,128]{2,1,0:T(8,128)(2,1)S(1)}, u32[]{:S(2)}, u32[]{:S(2)}) collective-permute-start(bf16[2,384,128]{2,1,0:T(8,128)(2,1)S(1)} %get-tuple-element.102), channel_id=1, source_target_pairs={{2,0},{4,2},{6,4},{8,6},{10,8},{12,10},{14,12},{0,14},{3,1},{5,3},... | collective-permute-start | bytes 589832 | tf_op jit(solution)/shard_map/ppermute | solution.py:428
  131.0 1.6 collective-permute-start.8
  132.7 1.6 collective-permute-start.9
  136.0 1.2 collective-permute-start.17
  137.2 2.0 %collective-permute-start.18 = (bf16[2,384,128]{2,1,0:T(8,128)(2,1)}, bf16[2,384,128]{2,1,0:T(8,128)(2,1)}, u32[]{:S(2)}, u32[]{:S(2)}) collective-permute-start(bf16[2,384,128]{2,1,0:T(8,128)(2,1)} %get-tuple-element.106), channel_id=1, source_target_pairs={{2,0},{4,2},{6,4},{8,6},{10,8},{12,10},{14,12},{0,14},{3,1},{5,3},... | collective-permute-start | bytes 589832 | tf_op jit(solution)/shard_map/ppermute | solution.py:428
  141.0 2.2 %collective-permute-done.17 = bf16[2,384,128]{2,1,0:T(8,128)(2,1)} collective-permute-done((bf16[2,384,128]{2,1,0:T(8,128)(2,1)}, bf16[2,384,128]{2,1,0:T(8,128)(2,1)}, u32[]{:S(2)}, u32[]{:S(2)}) %collective-permute-start.17) | collective-permute-done | bytes 196640 | tf_op jit(solution)/shard_map/ppermute | solution.py:428
  144.3 2.7 %collective-permute-done.10.far = bf16[1152,128]{1,0:T(8,128)(2,1)S(1)} collective-permute-done((bf16[1152,128]{1,0:T(8,128)(2,1)S(1)}, bf16[1152,128]{1,0:T(8,128)(2,1)S(1)}, u32[]{:S(2)}, u32[]{:S(2)}) %collective-permute-start.10) | collective-permute-done | bytes 294944 | tf_op jit(solution)/shard_map/ppermute | solution.py:489
  149.4 3.1 %collective-permute-start.12 = (bf16[2,384,128]{2,1,0:T(8,128)(2,1)S(1)}, bf16[2,384,128]{2,1,0:T(8,128)(2,1)S(1)}, u32[]{:S(2)}, u32[]{:S(2)}) collective-permute-start(bf16[2,384,128]{2,1,0:T(8,128)(2,1)S(1)} %add_convert_fusion.2), channel_id=1, source_target_pairs={{2,0},{4,2},{6,4},{8,6},{10,8},{12,10},{14,12},{0,14},{3,1},{5,3},... | collective-permute-start | bytes 589832 | tf_op jit(solution)/shard_map/ppermute | solution.py:428
  153.2 3.2 %collective-permute-done.11 = bf16[2,384,128]{2,1,0:T(8,128)(2,1)S(1)} collective-permute-done((bf16[2,384,128]{2,1,0:T(8,128)(2,1)S(1)}, bf16[2,384,128]{2,1,0:T(8,128)(2,1)S(1)}, u32[]{:S(2)}, u32[]{:S(2)}) %collective-permute-start.11) | collective-permute-done | bytes 196640 | tf_op jit(solution)/shard_map/ppermute | solution.py:428
  157.4 2.0 %collective-permute-start.13 = (bf16[2,384,128]{2,1,0:T(8,128)(2,1)S(1)}, bf16[2,384,128]{2,1,0:T(8,128)(2,1)S(1)}, u32[]{:S(2)}, u32[]{:S(2)}) collective-permute-start(bf16[2,384,128]{2,1,0:T(8,128)(2,1)S(1)} %get-tuple-element.95), channel_id=1, source_target_pairs={{0,2},{2,4},{4,6},{6,8},{8,10},{10,12},{12,14},{14,0},{1,3},{3,5},... | collective-permute-start | bytes 589832 | tf_op jit(solution)/shard_map/ppermute | solution.py:428
  159.4 1.4 collective-permute-start.14
  160.8 1.9 %shard_map.62.done_ref = bf16[128,2304]{1,0:T(8,128)(2,1)} custom-call(bf16[1,2,1152,128]{3,2,1,0:T(8,128)(2,1)} %reduce-scatter.2.cloned.1.call-done.near, bf16[1152,128]{1,0:T(8,128)(2,1)} %copy-done.7), custom_call_target="tpu_custom_call" | custom-call | tf_op jit(solution)/shard_map/pallas_call | solution.py:361
  162.7 1.7 collective-permute-done.13.up_ref
  (62 shorter events, 16.1 us)
Async XLA Ops:
  11.8 38.6 %all-to-all-start = ((bf16[16,96,768]{2,1,0:T(8,128)(2,1)}), bf16[16,96,768]{2,1,0:T(8,128)(2,1)S(1)}, u32[]{:S(2)}, u32[]{:S(2)}) async-start(bf16[16,96,768]{2,1,0:T(8,128)(2,1)} %bitcast.117), calls=%async_computation | async-start | bytes 4718592 | tf_op jit(solution)/shard_map/all_to_all | solution.py:414
  17.9 121.3 %reduce-scatter.2.cloned.1.call-start = ((), (), s32[]{:S(2)}) async-start(), calls=%async_computation.3 | async-start | bytes 5308416 | tf_op jit(solution)/shard_map/reduce_scatter | solution.py:417
  50.3 0.6 copy-start.2
  59.3 3.8 %copy-start.3 = (s32[62]{0:T(128)S(1)}, s32[62]{0:T(128)}, u32[]{:S(2)}) copy-start(s32[62]{0:T(128)} %get-tuple-element.57.lists) | copy-start | bytes 748
  59.3 23.6 %all-to-all-start.1 = ((bf16[16,48,768]{2,1,0:T(8,128)(2,1)}), bf16[16,48,768]{2,1,0:T(8,128)(2,1)S(1)}, u32[]{:S(2)}, u32[]{:S(2)}) async-start(bf16[16,48,768]{2,1,0:T(8,128)(2,1)} %bitcast.118), calls=%async_computation.2 | async-start | bytes 2359296 | tf_op jit(solution)/shard_map/all_to_all | solution.py:414
  69.0 0.9 copy-start
  69.9 51.8 %collective-permute-start.4 = (bf16[8,1,384,128]{3,2,1,0:T(8,128)(2,1)}, bf16[8,1,384,128]{3,2,1,0:T(8,128)(2,1)S(1)}, u32[]{:S(2)}, u32[]{:S(2)}) collective-permute-start(bf16[8,1,384,128]{3,2,1,0:T(8,128)(2,1)} %get-tuple-element.74), channel_id=1, source_target_pairs={{0,1},{1,0},{2,3},{3,2},{4,5},{5,4},{6,7},{7,6},{8,9},{9,8},{10,11... | collective-permute-start | bytes 2359304 | tf_op jit(solution)/shard_map/ppermute | solution.py:470
  89.7 14.2 %copy-start.1 = (bf16[8,1,384,128]{3,2,1,0:T(8,128)(2,1)S(1)}, bf16[8,1,384,128]{3,2,1,0:T(8,128)(2,1)}, u32[]{:S(2)}) copy-start(bf16[8,1,384,128]{3,2,1,0:T(8,128)(2,1)} %copy-done) | copy-start | bytes 2359300
  96.6 25.2 %collective-permute-start.5 = (bf16[8,1,384,128]{3,2,1,0:T(8,128)(2,1)S(1)}, bf16[8,1,384,128]{3,2,1,0:T(8,128)(2,1)S(1)}, u32[]{:S(2)}, u32[]{:S(2)}) collective-permute-start(bf16[8,1,384,128]{3,2,1,0:T(8,128)(2,1)S(1)} %get-tuple-element.76), channel_id=1, source_target_pairs={{0,1},{1,0},{2,3},{3,2},{4,5},{5,4},{6,7},{7,6},{8,9},{9,8},{10,11... | collective-permute-start | bytes 2359304 | tf_op jit(solution)/shard_map/ppermute | solution.py:475
  97.1 11.9 %collective-permute-start = (bf16[1,384,128]{2,1,0:T(8,128)(2,1)S(1)}, bf16[1,384,128]{2,1,0:T(8,128)(2,1)S(1)}, u32[]{:S(2)}, u32[]{:S(2)}) collective-permute-start(bf16[1,384,128]{2,1,0:T(8,128)(2,1)S(1)} %get-tuple-element.66), channel_id=1, source_target_pairs={{0,2},{2,4},{4,6},{6,8},{8,10},{10,12},{12,14},{14,0},{1,3},{3,5},... | collective-permute-start | bytes 294920 | tf_op jit(solution)/shard_map/ppermute | solution.py:428
  99.1 9.9 %collective-permute-start.1 = (bf16[1,384,128]{2,1,0:T(8,128)(2,1)S(1)}, bf16[1,384,128]{2,1,0:T(8,128)(2,1)S(1)}, u32[]{:S(2)}, u32[]{:S(2)}) collective-permute-start(bf16[1,384,128]{2,1,0:T(8,128)(2,1)S(1)} %get-tuple-element.67), channel_id=1, source_target_pairs={{2,0},{4,2},{6,4},{8,6},{10,8},{12,10},{14,12},{0,14},{3,1},{5,3},... | collective-permute-start | bytes 294920 | tf_op jit(solution)/shard_map/ppermute | solution.py:428
  109.1 12.6 %collective-permute-start.2 = (bf16[2,384,128]{2,1,0:T(8,128)(2,1)S(1)}, bf16[2,384,128]{2,1,0:T(8,128)(2,1)S(1)}, u32[]{:S(2)}, u32[]{:S(2)}) collective-permute-start(bf16[2,384,128]{2,1,0:T(8,128)(2,1)S(1)} %get-tuple-element.70), channel_id=1, source_target_pairs={{0,2},{2,4},{4,6},{6,8},{8,10},{10,12},{12,14},{14,0},{1,3},{3,5},... | collective-permute-start | bytes 589832 | tf_op jit(solution)/shard_map/ppermute | solution.py:428
  109.2 12.5 %collective-permute-start.3 = (bf16[2,384,128]{2,1,0:T(8,128)(2,1)S(1)}, bf16[2,384,128]{2,1,0:T(8,128)(2,1)S(1)}, u32[]{:S(2)}, u32[]{:S(2)}) collective-permute-start(bf16[2,384,128]{2,1,0:T(8,128)(2,1)S(1)} %get-tuple-element.71), channel_id=1, source_target_pairs={{2,0},{4,2},{6,4},{8,6},{10,8},{12,10},{14,12},{0,14},{3,1},{5,3},... | collective-permute-start | bytes 589832 | tf_op jit(solution)/shard_map/ppermute | solution.py:428
  121.8 7.5 %collective-permute-start.6 = (bf16[1,384,128]{2,1,0:T(8,128)(2,1)S(1)}, bf16[1,384,128]{2,1,0:T(8,128)(2,1)S(1)}, u32[]{:S(2)}, u32[]{:S(2)}) collective-permute-start(bf16[1,384,128]{2,1,0:T(8,128)(2,1)S(1)} %fusion.7), channel_id=1, source_target_pairs={{0,2},{2,4},{4,6},{6,8},{8,10},{10,12},{12,14},{14,0},{1,3},{3,5},... | collective-permute-start | bytes 294920 | tf_op jit(solution)/shard_map/ppermute | solution.py:428
  124.4 5.1 %collective-permute-start.7 = (bf16[1,384,128]{2,1,0:T(8,128)(2,1)S(1)}, bf16[1,384,128]{2,1,0:T(8,128)(2,1)S(1)}, u32[]{:S(2)}, u32[]{:S(2)}) collective-permute-start(bf16[1,384,128]{2,1,0:T(8,128)(2,1)S(1)} %fusion.8), channel_id=1, source_target_pairs={{2,0},{4,2},{6,4},{8,6},{10,8},{12,10},{14,12},{0,14},{3,1},{5,3},... | collective-permute-start | bytes 294920 | tf_op jit(solution)/shard_map/ppermute | solution.py:428
  126.0 8.7 %collective-permute-start.15 = (bf16[2,384,128]{2,1,0:T(8,128)(2,1)S(1)}, bf16[2,384,128]{2,1,0:T(8,128)(2,1)S(1)}, u32[]{:S(2)}, u32[]{:S(2)}) collective-permute-start(bf16[2,384,128]{2,1,0:T(8,128)(2,1)S(1)} %get-tuple-element.101), channel_id=1, source_target_pairs={{0,2},{2,4},{4,6},{6,8},{8,10},{10,12},{12,14},{14,0},{1,3},{3,5},... | collective-permute-start | bytes 589832 | tf_op jit(solution)/shard_map/ppermute | solution.py:428
  127.4 7.7 %collective-permute-start.16 = (bf16[2,384,128]{2,1,0:T(8,128)(2,1)S(1)}, bf16[2,384,128]{2,1,0:T(8,128)(2,1)S(1)}, u32[]{:S(2)}, u32[]{:S(2)}) collective-permute-start(bf16[2,384,128]{2,1,0:T(8,128)(2,1)S(1)} %get-tuple-element.102), channel_id=1, source_target_pairs={{2,0},{4,2},{6,4},{8,6},{10,8},{12,10},{14,12},{0,14},{3,1},{5,3},... | collective-permute-start | bytes 589832 | tf_op jit(solution)/shard_map/ppermute | solution.py:428
  129.5 11.4 %copy-start.6 = (bf16[1,384,128]{2,1,0:T(8,128)(2,1)S(1)}, bf16[1,384,128]{2,1,0:T(8,128)(2,1)}, u32[]{:S(2)}) copy-start(bf16[1,384,128]{2,1,0:T(8,128)(2,1)} %get-tuple-element.121) | copy-start | bytes 294916
  131.0 16.0 %copy-start.5 = (bf16[1,384,128]{2,1,0:T(8,128)(2,1)S(1)}, bf16[1,384,128]{2,1,0:T(8,128)(2,1)}, u32[]{:S(2)}) copy-start(bf16[1,384,128]{2,1,0:T(8,128)(2,1)} %get-tuple-element.119) | copy-start | bytes 294916
  131.0 10.0 %collective-permute-start.8 = (bf16[2,384,128]{2,1,0:T(8,128)(2,1)}, bf16[2,384,128]{2,1,0:T(8,128)(2,1)}, u32[]{:S(2)}, u32[]{:S(2)}) collective-permute-start(bf16[2,384,128]{2,1,0:T(8,128)(2,1)} %add_convert_fusion.5), channel_id=1, source_target_pairs={{0,2},{2,4},{4,6},{6,8},{8,10},{10,12},{12,14},{14,0},{1,3},{3,5},... | collective-permute-start | bytes 589832 | tf_op jit(solution)/shard_map/ppermute | solution.py:428
  132.7 8.3 %collective-permute-start.9 = (bf16[2,384,128]{2,1,0:T(8,128)(2,1)}, bf16[2,384,128]{2,1,0:T(8,128)(2,1)}, u32[]{:S(2)}, u32[]{:S(2)}) collective-permute-start(bf16[2,384,128]{2,1,0:T(8,128)(2,1)} %add_convert_fusion.4), channel_id=1, source_target_pairs={{2,0},{4,2},{6,4},{8,6},{10,8},{12,10},{14,12},{0,14},{3,1},{5,3},... | collective-permute-start | bytes 589832 | tf_op jit(solution)/shard_map/ppermute | solution.py:428
  136.0 12.2 %copy-start.4 = (bf16[1,384,128]{2,1,0:T(8,128)(2,1)S(1)}, bf16[1,384,128]{2,1,0:T(8,128)(2,1)}, u32[]{:S(2)}) copy-start(bf16[1,384,128]{2,1,0:T(8,128)(2,1)} %get-tuple-element.120) | copy-start | bytes 294916
  136.0 7.2 %collective-permute-start.17 = (bf16[2,384,128]{2,1,0:T(8,128)(2,1)}, bf16[2,384,128]{2,1,0:T(8,128)(2,1)}, u32[]{:S(2)}, u32[]{:S(2)}) collective-permute-start(bf16[2,384,128]{2,1,0:T(8,128)(2,1)} %get-tuple-element.105), channel_id=1, source_target_pairs={{0,2},{2,4},{4,6},{6,8},{8,10},{10,12},{12,14},{14,0},{1,3},{3,5},... | collective-permute-start | bytes 589832 | tf_op jit(solution)/shard_map/ppermute | solution.py:428
  137.2 6.0 %collective-permute-start.18 = (bf16[2,384,128]{2,1,0:T(8,128)(2,1)}, bf16[2,384,128]{2,1,0:T(8,128)(2,1)}, u32[]{:S(2)}, u32[]{:S(2)}) collective-permute-start(bf16[2,384,128]{2,1,0:T(8,128)(2,1)} %get-tuple-element.106), channel_id=1, source_target_pairs={{2,0},{4,2},{6,4},{8,6},{10,8},{12,10},{14,12},{0,14},{3,1},{5,3},... | collective-permute-start | bytes 589832 | tf_op jit(solution)/shard_map/ppermute | solution.py:428
  140.2 6.8 %collective-permute-start.10 = (bf16[1152,128]{1,0:T(8,128)(2,1)S(1)}, bf16[1152,128]{1,0:T(8,128)(2,1)S(1)}, u32[]{:S(2)}, u32[]{:S(2)}) collective-permute-start(bf16[1152,128]{1,0:T(8,128)(2,1)S(1)} %slice_bitcast_fusion), channel_id=1, source_target_pairs={{0,1},{1,0},{2,3},{3,2},{4,5},{5,4},{6,7},{7,6},{8,9},{9,8},{10,11... | collective-permute-start | bytes 884744 | tf_op jit(solution)/shard_map/ppermute | solution.py:489
  147.0 10.4 %copy-start.7 = (bf16[1152,128]{1,0:T(8,128)(2,1)}, bf16[1152,128]{1,0:T(8,128)(2,1)S(1)}, u32[]{:S(2)}) copy-start(bf16[1152,128]{1,0:T(8,128)(2,1)S(1)} %collective-permute-done.10.far) | copy-start | bytes 884740
  149.2 7.3 %collective-permute-start.11 = (bf16[2,384,128]{2,1,0:T(8,128)(2,1)S(1)}, bf16[2,384,128]{2,1,0:T(8,128)(2,1)S(1)}, u32[]{:S(2)}, u32[]{:S(2)}) collective-permute-start(bf16[2,384,128]{2,1,0:T(8,128)(2,1)S(1)} %add_convert_fusion.3), channel_id=1, source_target_pairs={{0,2},{2,4},{4,6},{6,8},{8,10},{10,12},{12,14},{14,0},{1,3},{3,5},... | collective-permute-start | bytes 589832 | tf_op jit(solution)/shard_map/ppermute | solution.py:428
  149.4 7.9 %collective-permute-start.12 = (bf16[2,384,128]{2,1,0:T(8,128)(2,1)S(1)}, bf16[2,384,128]{2,1,0:T(8,128)(2,1)S(1)}, u32[]{:S(2)}, u32[]{:S(2)}) collective-permute-start(bf16[2,384,128]{2,1,0:T(8,128)(2,1)S(1)} %add_convert_fusion.2), channel_id=1, source_target_pairs={{2,0},{4,2},{6,4},{8,6},{10,8},{12,10},{14,12},{0,14},{3,1},{5,3},... | collective-permute-start | bytes 589832 | tf_op jit(solution)/shard_map/ppermute | solution.py:428
  152.5 12.5 %collective-permute-start.19 = (bf16[384,128]{1,0:T(8,128)(2,1)S(1)}, bf16[384,128]{1,0:T(8,128)(2,1)S(1)}, u32[]{:S(2)}, u32[]{:S(2)}) collective-permute-start(bf16[384,128]{1,0:T(8,128)(2,1)S(1)} %fusion.9), channel_id=1, source_target_pairs={{0,1},{1,0},{2,3},{3,2},{4,5},{5,4},{6,7},{7,6},{8,9},{9,8},{10,11... | collective-permute-start | bytes 294920 | tf_op jit(solution)/shard_map/ppermute | solution.py:494
  157.4 7.0 %collective-permute-start.13 = (bf16[2,384,128]{2,1,0:T(8,128)(2,1)S(1)}, bf16[2,384,128]{2,1,0:T(8,128)(2,1)S(1)}, u32[]{:S(2)}, u32[]{:S(2)}) collective-permute-start(bf16[2,384,128]{2,1,0:T(8,128)(2,1)S(1)} %get-tuple-element.95), channel_id=1, source_target_pairs={{0,2},{2,4},{4,6},{6,8},{8,10},{10,12},{12,14},{14,0},{1,3},{3,5},... | collective-permute-start | bytes 589832 | tf_op jit(solution)/shard_map/ppermute | solution.py:428
  159.4 5.7 %collective-permute-start.14 = (bf16[2,384,128]{2,1,0:T(8,128)(2,1)S(1)}, bf16[2,384,128]{2,1,0:T(8,128)(2,1)S(1)}, u32[]{:S(2)}, u32[]{:S(2)}) collective-permute-start(bf16[2,384,128]{2,1,0:T(8,128)(2,1)S(1)} %get-tuple-element.96), channel_id=1, source_target_pairs={{2,0},{4,2},{6,4},{8,6},{10,8},{12,10},{14,12},{0,14},{3,1},{5,3},... | collective-permute-start | bytes 589832 | tf_op jit(solution)/shard_map/ppermute | solution.py:428
Sparse Core Ops, SparseCore 0:
  59.4 66.9 reduce-scatter.1

commit v11 on v8

--- a/solution.py
+++ b/solution.py
@@ -364,7 +364,7 @@
         in_specs=[slots(near, 1, 0), pl.BlockSpec(far.shape, lambda g: (0, 0))],
         out_specs=pl.BlockSpec((TILE, rows), lambda g: (0, 0)),
         out_shape=jax.ShapeDtypeStruct((TILE, 2 * rows), jnp.bfloat16),
-        compiler_params=params(57),
+        compiler_params=params(16),
     )(near, far)
 
 
@@ -486,9 +486,10 @@
     for step in range(1, half):
         late_ring = go_on(late, step, *late_ring)
         early_ring = go_on(early, step, *early_ring)
+    late_ring, last0 = lax.optimization_barrier((late_ring, swap(sum0[0, 1])))
     late_sum = add(terms1[0], *late_ring)
     far_late = swap(late_sum[1].astype(jnp.bfloat16))
-    done = finish_first(sum0, swap(sum0[0, 1]))
+    done = finish_first(sum0, last0)
     return finish_last(
         done, add(*early(0)).reshape(-1, TILE), *early_ring, late_sum[0], far_late
     )

time: 166 us -> 168 us (1.012)
  starting transfers between devices: 49.3 us -> 45.5 us
  Pallas kernels: 47.3 us -> 50.2 us
    ppermute x1, waiting for transfers between devices: 4.56 us -> 0.01 us  [on_device(): late_ring, last0 = lax.optimization_barrier((late_ring, swap(sum0[0, 1])))]
    pallas_call x4, Pallas kernels: 28.9 us -> 32.4 us  [ladder(): pl.pallas_call(functools.partial(ladder_kernel, begin, first), in_specs=[...]
    ppermute x16, waiting for transfers between devices: 11.6 us -> 14.3 us  [send(): return lax.optimization_barrier((up(pair[0]), down(pair[1])))]
    ppermute x1, starting transfers between devices: 2.88 us -> 0.7 us  [on_device(): far0 = swap(far0)]
    ppermute x1, waiting for transfers between devices: 0.01 us -> 1.85 us  [on_device(): far_late = swap(late_sum[1].astype(jnp.bfloat16))]
  transfers between devices with their start and end apart: 23 -> 23, of which waited for: 12 -> 11; matrix products, arithmetic and copies ran while one was open for 1% -> 3% of each run, Pallas kernels for 20% -> 21%
where the time goes in v11:
time: 168 us; the launch traced here: 166 us
  Pallas kernels  50.2 us (30%)
  waiting for transfers between devices  50.1 us (30%)
  starting transfers between devices  45.5 us (27%)
  between operations  13.7 us (8%)
  local copies, waits for them, and re-layouts  4.64 us (3%)
  other arithmetic  1.94 us (1%)
    pallas_call x4, Pallas kernels, ladder(): pl.pallas_call(functools.partial(ladder_kernel, begin, first), in_specs=[...  32.4 us
    all_to_all x2, waiting for transfers between devices, exchange(): lax.all_to_all(packed, 'row', split_axis=0, concat_axis=0, tiled=True)  32.4 us
    ppermute x16, starting transfers between devices, send(): return lax.optimization_barrier((up(pair[0]), down(pair[1])))  30.7 us
    ppermute x16, waiting for transfers between devices, send(): return lax.optimization_barrier((up(pair[0]), down(pair[1])))  14.3 us
    all_to_all x2, starting transfers between devices, exchange(): lax.all_to_all(packed, 'row', split_axis=0, concat_axis=0, tiled=True)  9.84 us
    pallas_call x2, Pallas kernels, pack(): pl.pallas_call(functools.partial(pack_kernel, first, n_i), in_specs=[hbm]...  9.46 us
    pallas_call x1, Pallas kernels, match(): pl.pallas_call(match_kernel, in_specs=[smem, smem, hbm, hbm], out_specs=[...  6.52 us
  transfers between devices with their start and end apart: 23, of which 11 were waited for; matrix products, arithmetic and copies ran while one was open for 3% of the time, Pallas kernels for 21%

profile of v11, /device:TPU:2, one launch (start us, length us, event | category | flops | bytes accessed | tf_op | source)
XLA Modules:
  0.0 166.1 jit_solution(4658947847452422336)
XLA Ops:
  6.5 5.2 %shard_map.56 = bf16[1536,768]{1,0:T(8,128)(2,1)} custom-call(bf16[12,192,768]{2,1,0:T(8,128)(2,1)} %amp_ref.10), custom_call_target="tpu_custom_call" | custom-call | bytes 7077888 | tf_op jit(solution)/shard_map/pallas_call | solution.py:79
  11.7 6.1 %all-to-all-start = ((bf16[16,96,768]{2,1,0:T(8,128)(2,1)}), bf16[16,96,768]{2,1,0:T(8,128)(2,1)S(1)}, u32[]{:S(2)}, u32[]{:S(2)}) async-start(bf16[16,96,768]{2,1,0:T(8,128)(2,1)} %bitcast.117), calls=%async_computation | async-start | bytes 4718592 | tf_op jit(solution)/shard_map/all_to_all | solution.py:414
  17.9 4.3 %shard_map.57 = bf16[768,768]{1,0:T(8,128)(2,1)} custom-call(bf16[12,192,768]{2,1,0:T(8,128)(2,1)} %amp_ref.10), custom_call_target="tpu_custom_call" | custom-call | bytes 7077888 | tf_op jit(solution)/shard_map/pallas_call | solution.py:79
  22.2 6.5 %shard_map.55 = (s32[62]{0:T(128)}, bf16[48,256,256]{2,1,0:T(8,128)(2,1)}) custom-call(s32[6]{0:T(128)} %cd_ref.1, s32[16]{0:T(128)} %ab_ref.1, bf16[768,2048]{1,0:T(8,128)(2,1)} %plus_ref, bf16[768,2048]{1,0:T(8,128)(2,1)} %minus_ref.1), custom_call_target="tpu_custom_call" | custom-call | bytes 12582912 | tf_op jit(solution)/shard_map/pallas_call | solution.py:196
  28.8 21.5 %all-to-all-done = bf16[16,96,768]{2,1,0:T(8,128)(2,1)S(1)} async-done(((bf16[16,96,768]{2,1,0:T(8,128)(2,1)}), bf16[16,96,768]{2,1,0:T(8,128)(2,1)S(1)}, u32[]{:S(2)}, u32[]{:S(2)}) %all-to-all-start) | async-done | bytes 2359328 | tf_op jit(solution)/shard_map/all_to_all | solution.py:414
  51.0 9.5 %shard_map.58 = bf16[8,2,1152,128]{3,2,1,0:T(8,128)(2,1)} custom-call(s32[2]{0:T(128)S(1)} %pad_add_fusion.me_ref, s32[62]{0:T(128)S(1)} %copy-done.3, bf16[12,192,768]{2,1,0:T(8,128)(2,1)} %amp_ref.10, bf16[1536,768]{1,0:T(8,128)(2,1)S(1)} %bitcast.112, bf16[48,256,256]{2,1,0:T(8,128)(2,1)} %get-tuple-element.61.weight_ref), custom_call_target="tpu_custom_call" | custom-call | bytes 16515072 | tf_op jit(solution)/shard_map/pallas_call | solution.py:324
  60.5 3.7 %all-to-all-start.1 = ((bf16[16,48,768]{2,1,0:T(8,128)(2,1)}), bf16[16,48,768]{2,1,0:T(8,128)(2,1)S(1)}, u32[]{:S(2)}, u32[]{:S(2)}) async-start(bf16[16,48,768]{2,1,0:T(8,128)(2,1)} %bitcast.118), calls=%async_computation.2 | async-start | bytes 2359296 | tf_op jit(solution)/shard_map/all_to_all | solution.py:414
  64.3 7.3 %shard_map.59 = (bf16[8,1,384,128]{3,2,1,0:T(8,128)(2,1)S(1)}, bf16[8,1,384,128]{3,2,1,0:T(8,128)(2,1)}) custom-call(s32[2]{0:T(128)S(1)} %pad_add_fusion.1.me_ref, s32[62]{0:T(128)S(1)} %copy-done.4, bf16[12,192,768]{2,1,0:T(8,128)(2,1)} %amp_ref.10, bf16[1536,768]{1,0:T(8,128)(2,1)S(1)} %bitcast.113, bf16[48,256,256]{2,1,0:T(8,128)(2,1)} %get-tuple-element.61.weight_ref), custom_call_target="tpu_custom_call" | custom-call | bytes 5505024 | tf_op jit(solution)/shard_map/pallas_call | solution.py:324
  73.2 10.9 %all-to-all-done.1 = bf16[16,48,768]{2,1,0:T(8,128)(2,1)S(1)} async-done(((bf16[16,48,768]{2,1,0:T(8,128)(2,1)}), bf16[16,48,768]{2,1,0:T(8,128)(2,1)S(1)}, u32[]{:S(2)}, u32[]{:S(2)}) %all-to-all-start.1) | async-done | bytes 1179680 | tf_op jit(solution)/shard_map/all_to_all | solution.py:414
  84.1 7.8 %shard_map.60 = (bf16[8,1,384,128]{3,2,1,0:T(8,128)(2,1)S(1)}, bf16[8,1,384,128]{3,2,1,0:T(8,128)(2,1)S(1)}) custom-call(s32[2]{0:T(128)S(1)} %pad_add_fusion.1.me_ref, s32[62]{0:T(128)S(1)} %copy-done.4, bf16[12,192,768]{2,1,0:T(8,128)(2,1)} %amp_ref.10, bf16[768,768]{1,0:T(8,128)(2,1)S(1)} %bitcast.114, bf16[48,256,256]{2,1,0:T(8,128)(2,1)} %get-tuple-element.61.weight_ref), custom_call_target="tpu_custom_call" | custom-call | bytes 5505024 | tf_op jit(solution)/shard_map/pallas_call | solution.py:324
  91.9 1.3 collective-permute-start.3
  94.0 7.8 %shard_map.61 = bf16[8,2,384,128]{3,2,1,0:T(8,128)(2,1)S(1)} custom-call(s32[2]{0:T(128)S(1)} %pad_add_fusion.1.me_ref, s32[62]{0:T(128)S(1)} %copy-done.4, bf16[12,192,768]{2,1,0:T(8,128)(2,1)} %amp_ref.10, bf16[768,768]{1,0:T(8,128)(2,1)S(1)} %bitcast.115, bf16[48,256,256]{2,1,0:T(8,128)(2,1)} %get-tuple-element.61.weight_ref), custom_call_target="tpu_custom_call" | custom-call | bytes 5505024 | tf_op jit(solution)/shard_map/pallas_call | solution.py:324
  102.6 4.3 %collective-permute-start.1 = (bf16[1,384,128]{2,1,0:T(8,128)(2,1)S(1)}, bf16[1,384,128]{2,1,0:T(8,128)(2,1)S(1)}, u32[]{:S(2)}, u32[]{:S(2)}) collective-permute-start(bf16[1,384,128]{2,1,0:T(8,128)(2,1)S(1)} %get-tuple-element.69), channel_id=1, source_target_pairs={{2,0},{4,2},{6,4},{8,6},{10,8},{12,10},{14,12},{0,14},{3,1},{5,3},... | collective-permute-start | bytes 294920 | tf_op jit(solution)/shard_map/ppermute | solution.py:428
  107.0 5.2 %collective-permute-done = bf16[1,384,128]{2,1,0:T(8,128)(2,1)S(1)} collective-permute-done((bf16[1,384,128]{2,1,0:T(8,128)(2,1)S(1)}, bf16[1,384,128]{2,1,0:T(8,128)(2,1)S(1)}, u32[]{:S(2)}, u32[]{:S(2)}) %collective-permute-start) | collective-permute-done | bytes 98336 | tf_op jit(solution)/shard_map/ppermute | solution.py:428
  112.2 1.5 collective-permute-done.3
  114.6 1.9 %collective-permute-start.11 = (bf16[1,384,128]{2,1,0:T(8,128)(2,1)S(1)}, bf16[1,384,128]{2,1,0:T(8,128)(2,1)S(1)}, u32[]{:S(2)}, u32[]{:S(2)}) collective-permute-start(bf16[1,384,128]{2,1,0:T(8,128)(2,1)S(1)} %get-tuple-element.91), channel_id=1, source_target_pairs={{0,2},{2,4},{4,6},{6,8},{8,10},{10,12},{12,14},{14,0},{1,3},{3,5},... | collective-permute-start | bytes 294920 | tf_op jit(solution)/shard_map/ppermute | solution.py:428
  116.5 3.5 %collective-permute-start.12 = (bf16[1,384,128]{2,1,0:T(8,128)(2,1)S(1)}, bf16[1,384,128]{2,1,0:T(8,128)(2,1)S(1)}, u32[]{:S(2)}, u32[]{:S(2)}) collective-permute-start(bf16[1,384,128]{2,1,0:T(8,128)(2,1)S(1)} %get-tuple-element.92), channel_id=1, source_target_pairs={{2,0},{4,2},{6,4},{8,6},{10,8},{12,10},{14,12},{0,14},{3,1},{5,3},... | collective-permute-start | bytes 294920 | tf_op jit(solution)/shard_map/ppermute | solution.py:428
  120.1 1.3 slice_bitcast_fusion.11
  121.5 3.2 %collective-permute-start.5 = (bf16[2,384,128]{2,1,0:T(8,128)(2,1)S(1)}, bf16[2,384,128]{2,1,0:T(8,128)(2,1)S(1)}, u32[]{:S(2)}, u32[]{:S(2)}) collective-permute-start(bf16[2,384,128]{2,1,0:T(8,128)(2,1)S(1)} %get-tuple-element.77), channel_id=1, source_target_pairs={{2,0},{4,2},{6,4},{8,6},{10,8},{12,10},{14,12},{0,14},{3,1},{5,3},... | collective-permute-start | bytes 589832 | tf_op jit(solution)/shard_map/ppermute | solution.py:428
  125.0 3.2 %collective-permute-start.14 = (bf16[2,384,128]{2,1,0:T(8,128)(2,1)S(1)}, bf16[2,384,128]{2,1,0:T(8,128)(2,1)S(1)}, u32[]{:S(2)}, u32[]{:S(2)}) collective-permute-start(bf16[2,384,128]{2,1,0:T(8,128)(2,1)S(1)} %add_convert_fusion.4), channel_id=1, source_target_pairs={{2,0},{4,2},{6,4},{8,6},{10,8},{12,10},{14,12},{0,14},{3,1},{5,3},... | collective-permute-start | bytes 589832 | tf_op jit(solution)/shard_map/ppermute | solution.py:428
  128.2 2.2 %collective-permute-done.4 = bf16[2,384,128]{2,1,0:T(8,128)(2,1)S(1)} collective-permute-done((bf16[2,384,128]{2,1,0:T(8,128)(2,1)S(1)}, bf16[2,384,128]{2,1,0:T(8,128)(2,1)S(1)}, u32[]{:S(2)}, u32[]{:S(2)}) %collective-permute-start.4) | collective-permute-done | bytes 196640 | tf_op jit(solution)/shard_map/ppermute | solution.py:428
  130.6 3.3 %collective-permute-start.7 = (bf16[2,384,128]{2,1,0:T(8,128)(2,1)S(1)}, bf16[2,384,128]{2,1,0:T(8,128)(2,1)S(1)}, u32[]{:S(2)}, u32[]{:S(2)}) collective-permute-start(bf16[2,384,128]{2,1,0:T(8,128)(2,1)S(1)} %get-tuple-element.81), channel_id=1, source_target_pairs={{2,0},{4,2},{6,4},{8,6},{10,8},{12,10},{14,12},{0,14},{3,1},{5,3},... | collective-permute-start | bytes 589832 | tf_op jit(solution)/shard_map/ppermute | solution.py:428
  134.9 3.2 %collective-permute-start.16 = (bf16[2,384,128]{2,1,0:T(8,128)(2,1)S(1)}, bf16[2,384,128]{2,1,0:T(8,128)(2,1)S(1)}, u32[]{:S(2)}, u32[]{:S(2)}) collective-permute-start(bf16[2,384,128]{2,1,0:T(8,128)(2,1)S(1)} %add_convert_fusion.2), channel_id=1, source_target_pairs={{2,0},{4,2},{6,4},{8,6},{10,8},{12,10},{14,12},{0,14},{3,1},{5,3},... | collective-permute-start | bytes 589832 | tf_op jit(solution)/shard_map/ppermute | solution.py:428
  138.9 2.5 %collective-permute-start.8 = (bf16[2,384,128]{2,1,0:T(8,128)(2,1)S(1)}, bf16[2,384,128]{2,1,0:T(8,128)(2,1)S(1)}, u32[]{:S(2)}, u32[]{:S(2)}) collective-permute-start(bf16[2,384,128]{2,1,0:T(8,128)(2,1)S(1)} %get-tuple-element.84), channel_id=1, source_target_pairs={{0,2},{2,4},{4,6},{6,8},{8,10},{10,12},{12,14},{14,0},{1,3},{3,5},... | collective-permute-start | bytes 589832 | tf_op jit(solution)/shard_map/ppermute | solution.py:428
  142.5 1.4 collective-permute-done.15
  144.0 1.0 slice_bitcast_fusion
  145.0 1.0 collective-permute-start.10
  146.1 1.8 %collective-permute-start.17 = (bf16[2,384,128]{2,1,0:T(8,128)(2,1)S(1)}, bf16[2,384,128]{2,1,0:T(8,128)(2,1)S(1)}, u32[]{:S(2)}, u32[]{:S(2)}) collective-permute-start(bf16[2,384,128]{2,1,0:T(8,128)(2,1)S(1)} %add_convert_fusion.1), channel_id=1, source_target_pairs={{0,2},{2,4},{4,6},{6,8},{8,10},{10,12},{12,14},{14,0},{1,3},{3,5},... | collective-permute-start | bytes 589832 | tf_op jit(solution)/shard_map/ppermute | solution.py:428
  147.8 1.6 collective-permute-start.18
  149.5 3.6 %collective-permute-done.17.up_ref = bf16[2,384,128]{2,1,0:T(8,128)(2,1)S(1)} collective-permute-done((bf16[2,384,128]{2,1,0:T(8,128)(2,1)S(1)}, bf16[2,384,128]{2,1,0:T(8,128)(2,1)S(1)}, u32[]{:S(2)}, u32[]{:S(2)}) %collective-permute-start.17) | collective-permute-done | bytes 196640 | tf_op jit(solution)/shard_map/ppermute | solution.py:428
  153.6 1.9 %collective-permute-start.19 = (bf16[384,128]{1,0:T(8,128)(2,1)S(1)}, bf16[384,128]{1,0:T(8,128)(2,1)S(1)}, u32[]{:S(2)}, u32[]{:S(2)}) collective-permute-start(bf16[384,128]{1,0:T(8,128)(2,1)S(1)} %fusion.9), channel_id=1, source_target_pairs={{0,1},{1,0},{2,3},{3,2},{4,5},{5,4},{6,7},{7,6},{8,9},{9,8},{10,11... | collective-permute-start | bytes 294920 | tf_op jit(solution)/shard_map/ppermute | solution.py:491
  156.5 1.8 %collective-permute-done.19.far_ref = bf16[384,128]{1,0:T(8,128)(2,1)S(1)} collective-permute-done((bf16[384,128]{1,0:T(8,128)(2,1)S(1)}, bf16[384,128]{1,0:T(8,128)(2,1)S(1)}, u32[]{:S(2)}, u32[]{:S(2)}) %collective-permute-start.19) | collective-permute-done | bytes 98336 | tf_op jit(solution)/shard_map/ppermute | solution.py:491
  (59 shorter events, 11.0 us)
Async XLA Ops:
  11.7 38.6 %all-to-all-start = ((bf16[16,96,768]{2,1,0:T(8,128)(2,1)}), bf16[16,96,768]{2,1,0:T(8,128)(2,1)S(1)}, u32[]{:S(2)}, u32[]{:S(2)}) async-start(bf16[16,96,768]{2,1,0:T(8,128)(2,1)} %bitcast.117), calls=%async_computation | async-start | bytes 4718592 | tf_op jit(solution)/shard_map/all_to_all | solution.py:414
  17.9 126.1 %reduce-scatter.2.cloned.1.call-start = ((), (), s32[]{:S(2)}) async-start(), calls=%async_computation.3 | async-start | bytes 5308416 | tf_op jit(solution)/shard_map/reduce_scatter | solution.py:417
  50.3 0.7 copy-start.3
  60.5 3.8 %copy-start.4 = (s32[62]{0:T(128)S(1)}, s32[62]{0:T(128)}, u32[]{:S(2)}) copy-start(s32[62]{0:T(128)} %get-tuple-element.57.lists) | copy-start | bytes 748
  60.5 23.6 %all-to-all-start.1 = ((bf16[16,48,768]{2,1,0:T(8,128)(2,1)}), bf16[16,48,768]{2,1,0:T(8,128)(2,1)S(1)}, u32[]{:S(2)}, u32[]{:S(2)}) async-start(bf16[16,48,768]{2,1,0:T(8,128)(2,1)} %bitcast.118), calls=%async_computation.2 | async-start | bytes 2359296 | tf_op jit(solution)/shard_map/all_to_all | solution.py:414
  71.6 0.9 copy-start.1
  72.5 39.6 %collective-permute-start.2 = (bf16[8,1,384,128]{3,2,1,0:T(8,128)(2,1)}, bf16[8,1,384,128]{3,2,1,0:T(8,128)(2,1)}, u32[]{:S(2)}, u32[]{:S(2)}) collective-permute-start(bf16[8,1,384,128]{3,2,1,0:T(8,128)(2,1)} %get-tuple-element.72), channel_id=1, source_target_pairs={{0,1},{1,0},{2,3},{3,2},{4,5},{5,4},{6,7},{7,6},{8,9},{9,8},{10,11... | collective-permute-start | bytes 2359304 | tf_op jit(solution)/shard_map/ppermute | solution.py:470
  84.1 9.2 %copy-start.2 = (bf16[8,1,384,128]{3,2,1,0:T(8,128)(2,1)S(1)}, bf16[8,1,384,128]{3,2,1,0:T(8,128)(2,1)}, u32[]{:S(2)}) copy-start(bf16[8,1,384,128]{3,2,1,0:T(8,128)(2,1)} %copy-done.1) | copy-start | bytes 2359300
  91.9 21.7 %collective-permute-start.3 = (bf16[8,1,384,128]{3,2,1,0:T(8,128)(2,1)S(1)}, bf16[8,1,384,128]{3,2,1,0:T(8,128)(2,1)S(1)}, u32[]{:S(2)}, u32[]{:S(2)}) collective-permute-start(bf16[8,1,384,128]{3,2,1,0:T(8,128)(2,1)S(1)} %get-tuple-element.73), channel_id=1, source_target_pairs={{0,1},{1,0},{2,3},{3,2},{4,5},{5,4},{6,7},{7,6},{8,9},{9,8},{10,11... | collective-permute-start | bytes 2359304 | tf_op jit(solution)/shard_map/ppermute | solution.py:473
  101.8 10.4 %collective-permute-start = (bf16[1,384,128]{2,1,0:T(8,128)(2,1)S(1)}, bf16[1,384,128]{2,1,0:T(8,128)(2,1)S(1)}, u32[]{:S(2)}, u32[]{:S(2)}) collective-permute-start(bf16[1,384,128]{2,1,0:T(8,128)(2,1)S(1)} %get-tuple-element.68), channel_id=1, source_target_pairs={{0,2},{2,4},{4,6},{6,8},{8,10},{10,12},{12,14},{14,0},{1,3},{3,5},... | collective-permute-start | bytes 294920 | tf_op jit(solution)/shard_map/ppermute | solution.py:428
  102.6 9.6 %collective-permute-start.1 = (bf16[1,384,128]{2,1,0:T(8,128)(2,1)S(1)}, bf16[1,384,128]{2,1,0:T(8,128)(2,1)S(1)}, u32[]{:S(2)}, u32[]{:S(2)}) collective-permute-start(bf16[1,384,128]{2,1,0:T(8,128)(2,1)S(1)} %get-tuple-element.69), channel_id=1, source_target_pairs={{2,0},{4,2},{6,4},{8,6},{10,8},{12,10},{14,12},{0,14},{3,1},{5,3},... | collective-permute-start | bytes 294920 | tf_op jit(solution)/shard_map/ppermute | solution.py:428
  114.6 10.1 %collective-permute-start.11 = (bf16[1,384,128]{2,1,0:T(8,128)(2,1)S(1)}, bf16[1,384,128]{2,1,0:T(8,128)(2,1)S(1)}, u32[]{:S(2)}, u32[]{:S(2)}) collective-permute-start(bf16[1,384,128]{2,1,0:T(8,128)(2,1)S(1)} %get-tuple-element.91), channel_id=1, source_target_pairs={{0,2},{2,4},{4,6},{6,8},{8,10},{10,12},{12,14},{14,0},{1,3},{3,5},... | collective-permute-start | bytes 294920 | tf_op jit(solution)/shard_map/ppermute | solution.py:428
  116.5 8.2 %collective-permute-start.12 = (bf16[1,384,128]{2,1,0:T(8,128)(2,1)S(1)}, bf16[1,384,128]{2,1,0:T(8,128)(2,1)S(1)}, u32[]{:S(2)}, u32[]{:S(2)}) collective-permute-start(bf16[1,384,128]{2,1,0:T(8,128)(2,1)S(1)} %get-tuple-element.92), channel_id=1, source_target_pairs={{2,0},{4,2},{6,4},{8,6},{10,8},{12,10},{14,12},{0,14},{3,1},{5,3},... | collective-permute-start | bytes 294920 | tf_op jit(solution)/shard_map/ppermute | solution.py:428
  121.4 9.0 %collective-permute-start.4 = (bf16[2,384,128]{2,1,0:T(8,128)(2,1)S(1)}, bf16[2,384,128]{2,1,0:T(8,128)(2,1)S(1)}, u32[]{:S(2)}, u32[]{:S(2)}) collective-permute-start(bf16[2,384,128]{2,1,0:T(8,128)(2,1)S(1)} %get-tuple-element.76), channel_id=1, source_target_pairs={{0,2},{2,4},{4,6},{6,8},{8,10},{10,12},{12,14},{14,0},{1,3},{3,5},... | collective-permute-start | bytes 589832 | tf_op jit(solution)/shard_map/ppermute | solution.py:428
  121.5 8.9 %collective-permute-start.5 = (bf16[2,384,128]{2,1,0:T(8,128)(2,1)S(1)}, bf16[2,384,128]{2,1,0:T(8,128)(2,1)S(1)}, u32[]{:S(2)}, u32[]{:S(2)}) collective-permute-start(bf16[2,384,128]{2,1,0:T(8,128)(2,1)S(1)} %get-tuple-element.77), channel_id=1, source_target_pairs={{2,0},{4,2},{6,4},{8,6},{10,8},{12,10},{14,12},{0,14},{3,1},{5,3},... | collective-permute-start | bytes 589832 | tf_op jit(solution)/shard_map/ppermute | solution.py:428
  124.9 9.7 %collective-permute-start.13 = (bf16[2,384,128]{2,1,0:T(8,128)(2,1)S(1)}, bf16[2,384,128]{2,1,0:T(8,128)(2,1)S(1)}, u32[]{:S(2)}, u32[]{:S(2)}) collective-permute-start(bf16[2,384,128]{2,1,0:T(8,128)(2,1)S(1)} %add_convert_fusion.5), channel_id=1, source_target_pairs={{0,2},{2,4},{4,6},{6,8},{8,10},{10,12},{12,14},{14,0},{1,3},{3,5},... | collective-permute-start | bytes 589832 | tf_op jit(solution)/shard_map/ppermute | solution.py:428
  125.0 9.6 %collective-permute-start.14 = (bf16[2,384,128]{2,1,0:T(8,128)(2,1)S(1)}, bf16[2,384,128]{2,1,0:T(8,128)(2,1)S(1)}, u32[]{:S(2)}, u32[]{:S(2)}) collective-permute-start(bf16[2,384,128]{2,1,0:T(8,128)(2,1)S(1)} %add_convert_fusion.4), channel_id=1, source_target_pairs={{2,0},{4,2},{6,4},{8,6},{10,8},{12,10},{14,12},{0,14},{3,1},{5,3},... | collective-permute-start | bytes 589832 | tf_op jit(solution)/shard_map/ppermute | solution.py:428
  130.5 8.3 %collective-permute-start.6 = (bf16[2,384,128]{2,1,0:T(8,128)(2,1)S(1)}, bf16[2,384,128]{2,1,0:T(8,128)(2,1)S(1)}, u32[]{:S(2)}, u32[]{:S(2)}) collective-permute-start(bf16[2,384,128]{2,1,0:T(8,128)(2,1)S(1)} %get-tuple-element.80), channel_id=1, source_target_pairs={{0,2},{2,4},{4,6},{6,8},{8,10},{10,12},{12,14},{14,0},{1,3},{3,5},... | collective-permute-start | bytes 589832 | tf_op jit(solution)/shard_map/ppermute | solution.py:428
  130.6 8.2 %collective-permute-start.7 = (bf16[2,384,128]{2,1,0:T(8,128)(2,1)S(1)}, bf16[2,384,128]{2,1,0:T(8,128)(2,1)S(1)}, u32[]{:S(2)}, u32[]{:S(2)}) collective-permute-start(bf16[2,384,128]{2,1,0:T(8,128)(2,1)S(1)} %get-tuple-element.81), channel_id=1, source_target_pairs={{2,0},{4,2},{6,4},{8,6},{10,8},{12,10},{14,12},{0,14},{3,1},{5,3},... | collective-permute-start | bytes 589832 | tf_op jit(solution)/shard_map/ppermute | solution.py:428
  134.7 11.3 %copy-start.6 = (bf16[1,384,128]{2,1,0:T(8,128)(2,1)S(1)}, bf16[1,384,128]{2,1,0:T(8,128)(2,1)}, u32[]{:S(2)}) copy-start(bf16[1,384,128]{2,1,0:T(8,128)(2,1)} %get-tuple-element.132) | copy-start | bytes 294916
  134.8 14.6 %copy-start.5 = (bf16[1,384,128]{2,1,0:T(8,128)(2,1)S(1)}, bf16[1,384,128]{2,1,0:T(8,128)(2,1)}, u32[]{:S(2)}) copy-start(bf16[1,384,128]{2,1,0:T(8,128)(2,1)} %get-tuple-element.137) | copy-start | bytes 294916
  134.8 9.1 %collective-permute-start.15 = (bf16[2,384,128]{2,1,0:T(8,128)(2,1)S(1)}, bf16[2,384,128]{2,1,0:T(8,128)(2,1)S(1)}, u32[]{:S(2)}, u32[]{:S(2)}) collective-permute-start(bf16[2,384,128]{2,1,0:T(8,128)(2,1)S(1)} %add_convert_fusion.3), channel_id=1, source_target_pairs={{0,2},{2,4},{4,6},{6,8},{8,10},{10,12},{12,14},{14,0},{1,3},{3,5},... | collective-permute-start | bytes 589832 | tf_op jit(solution)/shard_map/ppermute | solution.py:428
  134.9 9.0 %collective-permute-start.16 = (bf16[2,384,128]{2,1,0:T(8,128)(2,1)S(1)}, bf16[2,384,128]{2,1,0:T(8,128)(2,1)S(1)}, u32[]{:S(2)}, u32[]{:S(2)}) collective-permute-start(bf16[2,384,128]{2,1,0:T(8,128)(2,1)S(1)} %add_convert_fusion.2), channel_id=1, source_target_pairs={{2,0},{4,2},{6,4},{8,6},{10,8},{12,10},{14,12},{0,14},{3,1},{5,3},... | collective-permute-start | bytes 589832 | tf_op jit(solution)/shard_map/ppermute | solution.py:428
  138.9 10.5 %collective-permute-start.8 = (bf16[2,384,128]{2,1,0:T(8,128)(2,1)S(1)}, bf16[2,384,128]{2,1,0:T(8,128)(2,1)S(1)}, u32[]{:S(2)}, u32[]{:S(2)}) collective-permute-start(bf16[2,384,128]{2,1,0:T(8,128)(2,1)S(1)} %get-tuple-element.84), channel_id=1, source_target_pairs={{0,2},{2,4},{4,6},{6,8},{8,10},{10,12},{12,14},{14,0},{1,3},{3,5},... | collective-permute-start | bytes 589832 | tf_op jit(solution)/shard_map/ppermute | solution.py:428
  141.5 8.0 %collective-permute-start.9 = (bf16[2,384,128]{2,1,0:T(8,128)(2,1)S(1)}, bf16[2,384,128]{2,1,0:T(8,128)(2,1)S(1)}, u32[]{:S(2)}, u32[]{:S(2)}) collective-permute-start(bf16[2,384,128]{2,1,0:T(8,128)(2,1)S(1)} %get-tuple-element.85), channel_id=1, source_target_pairs={{2,0},{4,2},{6,4},{8,6},{10,8},{12,10},{14,12},{0,14},{3,1},{5,3},... | collective-permute-start | bytes 589832 | tf_op jit(solution)/shard_map/ppermute | solution.py:428
  145.0 8.5 %collective-permute-start.10 = (bf16[1152,128]{1,0:T(8,128)(2,1)S(1)}, bf16[1152,128]{1,0:T(8,128)(2,1)S(1)}, u32[]{:S(2)}, u32[]{:S(2)}) collective-permute-start(bf16[1152,128]{1,0:T(8,128)(2,1)S(1)} %slice_bitcast_fusion), channel_id=1, source_target_pairs={{0,1},{1,0},{2,3},{3,2},{4,5},{5,4},{6,7},{7,6},{8,9},{9,8},{10,11... | collective-permute-start | bytes 884744 | tf_op jit(solution)/shard_map/ppermute | solution.py:489
  146.0 9.6 %copy-start = (bf16[1,2,1152,128]{3,2,1,0:T(8,128)(2,1)S(1)}, bf16[1,2,1152,128]{3,2,1,0:T(8,128)(2,1)}, u32[]{:S(2)}) copy-start(bf16[1,2,1152,128]{3,2,1,0:T(8,128)(2,1)} %reduce-scatter.2.cloned.1.call-done.near) | copy-start | bytes 1769476
  146.1 7.0 %collective-permute-start.17 = (bf16[2,384,128]{2,1,0:T(8,128)(2,1)S(1)}, bf16[2,384,128]{2,1,0:T(8,128)(2,1)S(1)}, u32[]{:S(2)}, u32[]{:S(2)}) collective-permute-start(bf16[2,384,128]{2,1,0:T(8,128)(2,1)S(1)} %add_convert_fusion.1), channel_id=1, source_target_pairs={{0,2},{2,4},{4,6},{6,8},{8,10},{10,12},{12,14},{14,0},{1,3},{3,5},... | collective-permute-start | bytes 589832 | tf_op jit(solution)/shard_map/ppermute | solution.py:428
  147.8 5.7 %collective-permute-start.18 = (bf16[2,384,128]{2,1,0:T(8,128)(2,1)S(1)}, bf16[2,384,128]{2,1,0:T(8,128)(2,1)S(1)}, u32[]{:S(2)}, u32[]{:S(2)}) collective-permute-start(bf16[2,384,128]{2,1,0:T(8,128)(2,1)S(1)} %add_convert_fusion), channel_id=1, source_target_pairs={{2,0},{4,2},{6,4},{8,6},{10,8},{12,10},{14,12},{0,14},{3,1},{5,3},... | collective-permute-start | bytes 589832 | tf_op jit(solution)/shard_map/ppermute | solution.py:428
  153.6 4.7 %collective-permute-start.19 = (bf16[384,128]{1,0:T(8,128)(2,1)S(1)}, bf16[384,128]{1,0:T(8,128)(2,1)S(1)}, u32[]{:S(2)}, u32[]{:S(2)}) collective-permute-start(bf16[384,128]{1,0:T(8,128)(2,1)S(1)} %fusion.9), channel_id=1, source_target_pairs={{0,1},{1,0},{2,3},{3,2},{4,5},{5,4},{6,7},{7,6},{8,9},{9,8},{10,11... | collective-permute-start | bytes 294920 | tf_op jit(solution)/shard_map/ppermute | solution.py:491
Sparse Core Ops, SparseCore 0:
  60.6 61.9 reduce-scatter.1
